TPU v7x, 256 devices: a whole 4x4x8 slice. The times are simulated.
256 devices in a mesh: seq: 16 (over z, core), wt: 16 (over x, y).
Axes of the slice: x: 4, y: 4, z: 8, core: 2. Of those that a mesh axis runs over, the one named last changes fastest.
Arguments:
- queries: bfloat16 [8192, 8192], P('seq', 'wt'), may hold values from -6 to 6
- keys_in: bfloat16 [8192, 8192], P('seq', 'wt'), may hold values from -6 to 6
- values_in: bfloat16 [8192, 8192], P('seq', 'wt'), may hold values from -6 to 6
- stream: bfloat16 [8192, 8192], P('seq', 'wt')
- attn_gain: float32 [8192], P('wt'), may hold values from 0.1 to 1.9
- mlp_gain: float32 [8192], replicated, may hold values from 0.1 to 1.9
- up_index: int32 [128, 16], P('wt'), may hold values from 0 to 63, all different within a row
- up_blocks: bfloat16 [128, 16, 128, 128], P('wt'), may hold values from -0.125 to 0.125
- down_index: int32 [128, 16], P('wt'), may hold values from 0 to 63, all different within a row
- down_blocks: bfloat16 [128, 16, 128, 128], P('wt'), may hold values from -0.09375 to 0.09375
Outputs:
- result: bfloat16 [8192, 8192], P('seq', 'wt')
Inputs may be any that keep to these rules, and one draw needn't show every extreme that they name: `up_index`: each row names 16 different feature blocks, and every feature block is named by some row. `down_index`: each row names 16 different output blocks, and every output block is named by some row.
All inputs are finite; a program needn't handle non-finite values.
Results may differ from a plain program's by a relative error of at most 0.013.
Values may be sent and summed in bfloat16 or wider, within the bound.
No kernel may reach another device: no remote copies, remote signals or barrier semaphores. Data moves between devices by JAX's collectives and lax.ppermute only.
A program may use at most 128 MiB of HBM per device.

v0:
```python
import jax
import jax.numpy as jnp
from jax import lax
from jax.experimental import pallas as pl
from jax.experimental.pallas import tpu as pltpu
from jax.sharding import PartitionSpec as P

HEAD = 128
BLK = 128
SIDE = 4
SEQ = 16
F32 = jnp.float32
BF16 = jnp.bfloat16
VMEM = pl.BlockSpec(memory_space=pltpu.VMEM)
SMEM = pl.BlockSpec(memory_space=pltpu.SMEM)
ANY = pl.BlockSpec(memory_space=pl.ANY)


def feature(a):
    a = a.astype(F32)
    return jnp.where(a > 0, a + 1.0, jnp.exp(jnp.minimum(a, 0.0))).astype(BF16)


def dot(a, b):
    return jnp.dot(a, b, preferred_element_type=F32)


def dot_nt(a, b):
    return lax.dot_general(a, b, (((1,), (1,)), ((), ())), preferred_element_type=F32)


def dot_tn(a, b):
    return lax.dot_general(a, b, (((0,), (0,)), ((), ())), preferred_element_type=F32)


def state_kernel(k_ref, v_ref, out_ref):
    for h in range(4):
        cols = slice(h * HEAD, (h + 1) * HEAD)
        out_ref[h] = dot_tn(feature(k_ref[:, cols]), v_ref[:, cols]).astype(BF16)


def intra_kernel(q_ref, k_ref, v_ref, out_ref):
    half = 256
    row = lax.broadcasted_iota(jnp.int32, (half, half), 0)
    col = lax.broadcasted_iota(jnp.int32, (half, half), 1)
    keep = col <= row
    for h in range(4):
        cols = slice(h * HEAD, (h + 1) * HEAD)
        fq = feature(q_ref[:, cols])
        fk = feature(k_ref[:, cols])
        v = v_ref[:, cols]
        top = jnp.where(keep, dot_nt(fq[:half], fk[:half]), 0.0).astype(BF16)
        out_ref[h, :half] = dot(top, v[:half])
        left = dot_nt(fq[half:], fk[:half]).astype(BF16)
        right = jnp.where(keep, dot_nt(fq[half:], fk[half:]), 0.0).astype(BF16)
        out_ref[h, half:] = dot(left, v[:half]) + dot(right, v[half:])


def mid_kernel(core_ref, q_ref, state_ref, intra_ref, stream_ref, gain_ref, keep_ref, give_ref):
    first = core_ref[0] == 0
    for h in range(4):
        cols = slice(h * HEAD, (h + 1) * HEAD)
        fq = feature(q_ref[:, cols])
        state = state_ref[h]
        high = state.astype(BF16)
        low = (state - high.astype(F32)).astype(BF16)
        raw = intra_ref[h] + dot(fq, high) + dot(fq, low)
        scale = lax.rsqrt(jnp.mean(raw * raw, axis=-1, keepdims=True) + 1e-06)
        attn = raw * scale * gain_ref[:, cols]
        mid = (stream_ref[:, cols].astype(F32) + attn).astype(BF16)
        keep_ref[h] = jnp.where(first, mid[:256], mid[256:])
        give_ref[h] = jnp.where(first, mid[256:], mid[:256])


def ffn_kernel(places_in, places_out, up_index, down_index, gain_ref, *refs):
    pieces, (up_hbm, down_hbm), outs = refs[:8], refs[8:10], refs[10:18]
    x_0, x_1, up_w, down_w, acc_0, acc_1, stage, squares, in_sem, up_sem, down_sem, out_sem = refs[18:]
    xs, accs = (x_0, x_1), (acc_0, acc_1)
    n_hidden, kept = up_w.shape[:2]
    each = 16 // n_hidden

    def piece_copy(i, t):
        source = pieces[i // 2].at[i % 2, t]
        return pltpu.make_async_copy(source, xs[t].at[pl.ds(places_in[i] * 4, 4)], in_sem.at[i, t])

    def up_copy(c):
        return pltpu.make_async_copy(up_hbm.at[c], up_w.at[c], up_sem.at[c])

    def down_copy(c):
        return pltpu.make_async_copy(down_hbm.at[c], down_w.at[c], down_sem.at[c])

    def out_copy(i, t):
        target = outs[i // 2].at[i % 2, t]
        return pltpu.make_async_copy(stage.at[t, pl.ds(i * 4, 4)], target, out_sem.at[i, t])

    def make_ready(i, t):
        total = squares[t]
        for b in range(4):
            block = places_in[i] * 4 + b
            value = xs[t][block].astype(F32)
            total = total + value * value
            xs[t][block] = (value * gain_ref[pl.ds(block, 1), :]).astype(BF16)
        squares[t] = total

    def clear(j, t):
        accs[t][j] = jnp.zeros((256, 128), F32)

    def leave(i, t):
        for b in range(4):
            stage[t, i * 4 + b] = accs[t][places_out[i] * 4 + b].astype(BF16)

    def products(c, t, scale):
        picked = jnp.concatenate([xs[t][up_index[c, k]] for k in range(kept)], axis=1)
        upper = dot(picked, up_w[c].reshape(kept * BLK, BLK)) * scale
        act = (upper / (1.0 + jnp.exp(-upper))).astype(BF16)
        for k in range(0, kept, 2):
            part = dot(act, jnp.concatenate([down_w[c, k], down_w[c, k + 1]], axis=1))
            accs[t][down_index[c, k]] += part[:, :BLK]
            accs[t][down_index[c, k + 1]] += part[:, BLK:]

    def scale_of(t):
        mean = jnp.sum(squares[t], axis=-1, keepdims=True) * (1.0 / (64 * 128))
        return lax.rsqrt(mean + 1e-06)

    for i in range(16):
        piece_copy(i, 0).start()
    for c in range(n_hidden):
        up_copy(c).start()
        down_copy(c).start()
    for i in range(16):
        piece_copy(i, 1).start()
    squares[...] = jnp.zeros(squares.shape, F32)

    @pl.loop(0, 64)
    def _(j):
        clear(j, 0)

    for i in range(16):
        piece_copy(i, 0).wait()
        make_ready(i, 0)
    scale = scale_of(0)

    @pl.loop(0, n_hidden)
    def _(c):
        up_copy(c).wait()
        down_copy(c).wait()
        for e in range(each):
            i = c * each + e
            pltpu.make_async_copy(pieces[0].at[0, 1], x_1.at[pl.ds(0, 4)], in_sem.at[i, 1]).wait()
        for e in range(each):
            i = c * each + e
            make_ready(i, 1)
            for b in range(4):
                clear(i * 4 + b, 1)
        products(c, 0, scale)

    scale_1 = scale_of(1)

    @pl.loop(0, n_hidden)
    def _(c):
        for e in range(each):
            leave(c * each + e, 0)
        products(c, 1, scale_1)
        for i in range(16):

            @pl.when(c == i // each)
            def _():
                out_copy(i, 0).start()

    for i in range(16):
        leave(i, 1)
        out_copy(i, 1).start()
    for i in range(16):
        for t in range(2):
            out_copy(i, t).wait()


PIECE = jax.ShapeDtypeStruct((2, 2, 4, 256, 128), BF16)


def ffn(pieces, places_in, places_out, up_index, down_index, gain, up_blocks, down_blocks):
    n_hidden, kept = up_index.shape
    return pl.pallas_call(
        ffn_kernel,
        out_shape=[PIECE] * 8,
        in_specs=[SMEM] * 4 + [VMEM] + [ANY] * 10,
        out_specs=[ANY] * 8,
        scratch_shapes=[
            pltpu.VMEM((64, 256, 128), BF16),
            pltpu.VMEM((64, 256, 128), BF16),
            pltpu.VMEM((n_hidden, kept, BLK, BLK), BF16),
            pltpu.VMEM((n_hidden, kept, BLK, BLK), BF16),
            pltpu.VMEM((64, 256, 128), F32),
            pltpu.VMEM((64, 256, 128), F32),
            pltpu.VMEM((2, 64, 256, 128), BF16),
            pltpu.VMEM((2, 256, 128), F32),
            pltpu.SemaphoreType.DMA((16, 2)),
            pltpu.SemaphoreType.DMA((n_hidden,)),
            pltpu.SemaphoreType.DMA((n_hidden,)),
            pltpu.SemaphoreType.DMA((16, 2)),
        ],
        name="feed_forward",
        compiler_params=pltpu.CompilerParams(vmem_limit_bytes=52 * 2**20),
        cost_estimate=pl.CostEstimate(
            flops=4 * 512 * n_hidden * kept * BLK * BLK, bytes_accessed=25 * 2**20, transcendentals=512 * 1024
        ),
    )(places_in, places_out, up_index, down_index, gain, *pieces, up_blocks, down_blocks)


def result_kernel(core_ref, mine_ref, traded_ref, out_ref):
    mine = pl.multiple_of(core_ref[0] * 256, 256)
    for b in range(4):
        cols = slice(b * BLK, (b + 1) * BLK)
        out_ref[pl.ds(mine, 256), cols] = mine_ref[b]
        out_ref[pl.ds(256 - mine, 256), cols] = traded_ref[b]


def torus_shift(x, level, step):
    pairs = []
    for s in range(SEQ):
        for a in range(SIDE):
            for b in range(SIDE):
                to = ((a + step) % SIDE, b) if level == s % 2 else (a, (b + step) % SIDE)
                pairs.append(((s * SIDE + a) * SIDE + b, (s * SIDE + to[0]) * SIDE + to[1]))
    return lax.ppermute(x, ("seq", "wt"), pairs)


def swap_cores(x):
    return lax.ppermute(x, "seq", [(s, s ^ 1) for s in range(SEQ)])


def added(*terms):
    total = terms[0].astype(F32)
    for t in terms[1:]:
        total = total + t.astype(F32)
    return total.astype(BF16)


def finished(mid, terms):
    down = terms[0].astype(F32)
    for t in terms[1:]:
        down = down + t.astype(F32)
    return (mid.astype(F32) + down).astype(BF16)


def states_before(own):
    core = lax.axis_index("seq") % 2
    other = swap_cores(own)

    def later(x, places):
        return lax.ppermute(x, "seq", [(s, s + 2 * places) for s in range(SEQ) if s + 2 * places < SEQ])

    both = own.astype(F32) + other.astype(F32)
    pair = jnp.where(core == 0, both[:2], both[2:]).astype(BF16)
    near = later(pair, 1).astype(F32) + later(pair, 2).astype(F32)
    window = (near + pair.astype(F32)).astype(BF16)
    before = near + later(window, 3).astype(F32) + later(window, 6).astype(F32)
    rest = swap_cores(before.astype(BF16)).astype(F32)
    whole = jnp.where(core == 0, jnp.concatenate([before, rest]), jnp.concatenate([rest, before]))
    return whole + jnp.where(core == 0, 0.0, other.astype(F32))


def per_device(queries, keys_in, values_in, stream, attn_gain, mlp_gain, up_index, up_blocks, down_index, down_blocks):
    own = pl.pallas_call(
        state_kernel,
        out_shape=jax.ShapeDtypeStruct((4, HEAD, HEAD), BF16),
        in_specs=[VMEM] * 2,
        out_specs=VMEM,
        name="states",
    )(keys_in, values_in)
    intra = pl.pallas_call(
        intra_kernel,
        out_shape=jax.ShapeDtypeStruct((4, 512, HEAD), F32),
        in_specs=[VMEM] * 3,
        out_specs=VMEM,
        cost_estimate=pl.CostEstimate(flops=2**30, bytes_accessed=3 * 2**20, transcendentals=2**19),
        name="within_block",
    )(queries, keys_in, values_in)
    before = states_before(own)
    half = jax.ShapeDtypeStruct((4, 256, 128), BF16)
    core = lax.axis_index("seq") % 2
    core_arg = core.reshape(1)
    keep, give = pl.pallas_call(
        mid_kernel,
        out_shape=[half, half],
        in_specs=[SMEM] + [VMEM] * 5,
        out_specs=[VMEM] * 2,
        name="mid",
    )(core_arg, queries, before, intra, stream, attn_gain.reshape(1, -1))

    place = lax.axis_index("wt")
    at_x, at_y = place // SIDE, place % SIDE
    number = jnp.arange(16, dtype=jnp.int32)
    outer, inner = jnp.array([0, 1, 3, 2], jnp.int32)[number // 4], number % 4
    step_x, step_y = jnp.where(core == 0, inner, outer), jnp.where(core == 0, outer, inner)

    def where(sign):
        return ((at_x + sign * step_x + SIDE) % SIDE) * SIDE + (at_y + sign * step_y + SIDE) % SIDE

    both = jnp.stack([keep, swap_cores(give)])
    near_1, near_3, near_2 = torus_shift(both, 0, 1), torus_shift(both, 0, -1), torus_shift(both, 0, 2)
    own_a, own_b = jnp.stack([both, near_1]), jnp.stack([near_2, near_3])
    ahead_a = torus_shift(own_a, 1, 1)
    back_b = torus_shift(own_b, 1, -1)
    ahead_b = torus_shift(own_b, 1, 1)
    back_a = torus_shift(own_a, 1, -1)
    far_a = torus_shift(ahead_a, 1, 1)
    far_b = torus_shift(back_b, 1, -1)

    pieces = (own_a, own_b, ahead_a, ahead_b, back_a, back_b, far_a, far_b)
    gain = mlp_gain.reshape(64, BLK)
    own_a, own_b, ahead_a, ahead_b, back_a, back_b, far_a, far_b = ffn(
        pieces, where(-1), where(1), up_index, down_index, gain, up_blocks, down_blocks
    )
    via_a = torus_shift(far_a, 1, 1)
    via_b = torus_shift(far_b, 1, -1)
    from_back_b = torus_shift(ahead_b, 1, 1)
    from_ahead_a = torus_shift(back_a, 1, -1)
    from_back_a = torus_shift(added(via_a, ahead_a), 1, 1)
    from_ahead_b = torus_shift(added(via_b, back_b), 1, -1)
    rows = [added(own_a[r], from_ahead_a[r], from_back_a[r]) for r in range(2)]
    rows += [added(own_b[r], from_ahead_b[r], from_back_b[r]) for r in range(2)]
    terms = [rows[0], torus_shift(rows[1], 0, 1), torus_shift(rows[3], 0, -1), torus_shift(rows[2], 0, 2)]
    done = finished(both, terms)
    return pl.pallas_call(
        result_kernel,
        out_shape=jax.ShapeDtypeStruct((512, 512), BF16),
        in_specs=[SMEM] + [VMEM] * 2,
        out_specs=VMEM,
        name="result",
    )(core_arg, done[0], swap_cores(done[1]))


def solution(mesh):
    placed = (
        P("seq", "wt"),
        P("seq", "wt"),
        P("seq", "wt"),
        P("seq", "wt"),
        P("wt"),
        P(),
        P("wt", None),
        P("wt", None, None, None),
        P("wt", None),
        P("wt", None, None, None),
    )
    return jax.shard_map(
        per_device,
        mesh=mesh,
        in_specs=placed,
        out_specs=P("seq", "wt"),
        check_vma=False,
    )
```

profile of v0, /device:TPU:184, one launch (start us, length us, event | category | flops | bytes accessed | tf_op | source)
XLA Modules:
  0.0 177.5 jit_solution(4651562807953149195)
XLA Ops:
  0.0 2.4 %states.1 = bf16[4,128,128]{2,1,0:T(8,128)(2,1)} custom-call(bf16[512,512]{1,0:T(8,128)(2,1)} %k_ref.3, bf16[512,512]{1,0:T(8,128)(2,1)} %v_ref.3), custom_call_target="tpu_custom_call" | custom-call | tf_op jit(solution)/shard_map/states/pallas_call | solution.py:264
  2.4 0.0 collective-permute-start
  2.4 1.6 collective-permute-done
  3.9 0.9 convert_add_fusion.1
  4.9 3.4 %collective-permute-start.2 = (bf16[2,128,128]{2,1,0:T(8,128)(2,1)S(1)}, bf16[2,128,128]{2,1,0:T(8,128)(2,1)S(1)}, u32[]{:S(2)}, u32[]{:S(2)}) collective-permute-start(bf16[2,128,128]{2,1,0:T(8,128)(2,1)S(1)} %fusion.9), channel_id=1, source_target_pairs={{0,64},{16,80},{32,96},{48,112},{64,128},{80,144},{96,160},{112,17... | collective-permute-start | bytes 196616 | tf_op jit(solution)/shard_map/ppermute | solution.py:251
  8.3 1.9 %collective-permute-start.1 = (bf16[2,128,128]{2,1,0:T(8,128)(2,1)S(1)}, bf16[2,128,128]{2,1,0:T(8,128)(2,1)S(1)}, u32[]{:S(2)}, u32[]{:S(2)}) collective-permute-start(bf16[2,128,128]{2,1,0:T(8,128)(2,1)S(1)} %fusion.9), channel_id=1, source_target_pairs={{0,32},{16,48},{32,64},{48,80},{64,96},{80,112},{96,128},{112,144}... | collective-permute-start | bytes 196616 | tf_op jit(solution)/shard_map/ppermute | solution.py:251
  10.2 4.5 %collective-permute-done.2 = bf16[2,128,128]{2,1,0:T(8,128)(2,1)S(1)} collective-permute-done((bf16[2,128,128]{2,1,0:T(8,128)(2,1)S(1)}, bf16[2,128,128]{2,1,0:T(8,128)(2,1)S(1)}, u32[]{:S(2)}, u32[]{:S(2)}) %collective-permute-start.2) | collective-permute-done | bytes 65568 | tf_op jit(solution)/shard_map/ppermute | solution.py:251
  14.7 0.0 collective-permute-done.1
  14.8 0.7 collective-permute-start.4
  15.4 1.3 collective-permute-start.3
  16.7 0.0 collective-permute-done.4
  16.7 9.9 %collective-permute-done.3 = bf16[2,128,128]{2,1,0:T(8,128)(2,1)S(1)} collective-permute-done((bf16[2,128,128]{2,1,0:T(8,128)(2,1)S(1)}, bf16[2,128,128]{2,1,0:T(8,128)(2,1)S(1)}, u32[]{:S(2)}, u32[]{:S(2)}) %collective-permute-start.3) | collective-permute-done | bytes 65568 | tf_op jit(solution)/shard_map/ppermute | solution.py:251
  26.6 0.1 collective-permute-start.5
  26.7 4.0 %within_block.1.intra_ref = f32[4,512,128]{2,1,0:T(8,128)} custom-call(bf16[512,512]{1,0:T(8,128)(2,1)} %q_ref.3, bf16[512,512]{1,0:T(8,128)(2,1)} %k_ref.3, bf16[512,512]{1,0:T(8,128)(2,1)} %v_ref.3), custom_call_target="tpu_custom_call" | custom-call | flops 1073741824 | bytes 3145728 | tf_op jit(solution)/shard_map/within_block/pallas_call | solution.py:271
  30.8 0.7 fusion.8.state_ref
  31.6 3.2 %mid.1 = (bf16[4,256,128]{2,1,0:T(8,128)(2,1)}, bf16[4,256,128]{2,1,0:T(8,128)(2,1)}) custom-call(s32[1]{0:T(128)} %bitcast.core_ref, bf16[512,512]{1,0:T(8,128)(2,1)} %q_ref.3, f32[4,128,128]{2,1,0:T(8,128)} %fusion.8.state_ref, f32[4,512,128]{2,1,0:T(8,128)} %within_block.1.intra_ref, bf16[512,512]{1,0:T(8,128)(2,1)} %stream_ref.1, f32[1,512]{1,0:T(1,128)} %bitcast.35), custom_call_target="tpu_custom_call" | custom-call | tf_op jit(solution)/shard_map/mid/pallas_call | solution.py:283
  34.7 0.5 collective-permute-start.6
  35.2 1.4 collective-permute-done.6
  36.6 1.0 fusion.19
  37.6 2.8 %collective-permute-start.9 = (bf16[2,4,256,128]{3,2,1,0:T(8,128)(2,1)S(1)}, bf16[2,4,256,128]{3,2,1,0:T(8,128)(2,1)S(1)}, u32[]{:S(2)}, u32[]{:S(2)}) collective-permute-start(bf16[2,4,256,128]{3,2,1,0:T(8,128)(2,1)S(1)} %get-tuple-element.32), channel_id=1, source_target_pairs={{0,12},{1,13},{2,14},{3,15},{4,0},{5,1},{6,2},{7,3},{8,4},{9,5},{1... | collective-permute-start | bytes 1572872 | tf_op jit(solution)/shard_map/ppermute | solution.py:225
  40.5 0.8 collective-permute-start.8
  41.2 0.9 collective-permute-start.7
  42.1 10.7 %collective-permute-done.9 = bf16[2,4,256,128]{3,2,1,0:T(8,128)(2,1)S(1)} collective-permute-done((bf16[2,4,256,128]{3,2,1,0:T(8,128)(2,1)S(1)}, bf16[2,4,256,128]{3,2,1,0:T(8,128)(2,1)S(1)}, u32[]{:S(2)}, u32[]{:S(2)}) %collective-permute-start.9) | collective-permute-done | bytes 524320 | tf_op jit(solution)/shard_map/ppermute | solution.py:225
  52.8 0.0 copy-start.2
  52.8 0.1 pad_maximum_fusion.1.refs_1_
  52.9 1.1 collective-permute-start.13
  54.0 2.7 %collective-permute-done.7 = bf16[2,4,256,128]{3,2,1,0:T(8,128)(2,1)S(1)} collective-permute-done((bf16[2,4,256,128]{3,2,1,0:T(8,128)(2,1)S(1)}, bf16[2,4,256,128]{3,2,1,0:T(8,128)(2,1)S(1)}, u32[]{:S(2)}, u32[]{:S(2)}) %collective-permute-start.7) | collective-permute-done | bytes 524320 | tf_op jit(solution)/shard_map/ppermute | solution.py:225
  56.8 0.1 pad_maximum_fusion.refs_0_
  56.9 0.3 collective-permute-start.10
  57.2 1.6 collective-permute-start.11
  58.7 0.4 collective-permute-start.12
  59.2 9.8 %collective-permute-done.13.refs_5_ = bf16[2,2,4,256,128]{4,3,2,1,0:T(8,128)(2,1)S(1)} collective-permute-done((bf16[2,2,4,256,128]{4,3,2,1,0:T(8,128)(2,1)S(1)}, bf16[2,2,4,256,128]{4,3,2,1,0:T(8,128)(2,1)S(1)}, u32[]{:S(2)}, u32[]{:S(2)}) %collective-permute-start.13) | collective-permute-done | bytes 1048608 | tf_op jit(solution)/shard_map/ppermute | solution.py:225
  69.0 2.8 %collective-permute-done.10.refs_2_ = bf16[2,2,4,256,128]{4,3,2,1,0:T(8,128)(2,1)} collective-permute-done((bf16[2,2,4,256,128]{4,3,2,1,0:T(8,128)(2,1)S(1)}, bf16[2,2,4,256,128]{4,3,2,1,0:T(8,128)(2,1)}, u32[]{:S(2)}, u32[]{:S(2)}) %collective-permute-start.10) | collective-permute-done | bytes 1048608 | tf_op jit(solution)/shard_map/ppermute | solution.py:225
  71.9 1.4 collective-permute-start.14
  73.3 0.7 gather_fusion
  74.0 9.1 %collective-permute-done.11.refs_3_ = bf16[2,2,4,256,128]{4,3,2,1,0:T(8,128)(2,1)} collective-permute-done((bf16[2,2,4,256,128]{4,3,2,1,0:T(8,128)(2,1)S(1)}, bf16[2,2,4,256,128]{4,3,2,1,0:T(8,128)(2,1)}, u32[]{:S(2)}, u32[]{:S(2)}) %collective-permute-start.11) | collective-permute-done | bytes 1048608 | tf_op jit(solution)/shard_map/ppermute | solution.py:225
  83.1 0.0 collective-permute-done.12.refs_4_
  83.1 8.5 %collective-permute-done.15.refs_7_ = bf16[2,2,4,256,128]{4,3,2,1,0:T(8,128)(2,1)} collective-permute-done((bf16[2,2,4,256,128]{4,3,2,1,0:T(8,128)(2,1)S(1)}, bf16[2,2,4,256,128]{4,3,2,1,0:T(8,128)(2,1)}, u32[]{:S(2)}, u32[]{:S(2)}) %collective-permute-start.15) | collective-permute-done | bytes 1048608 | tf_op jit(solution)/shard_map/ppermute | solution.py:225
  91.6 2.7 %collective-permute-done.14.refs_6_ = bf16[2,2,4,256,128]{4,3,2,1,0:T(8,128)(2,1)} collective-permute-done((bf16[2,2,4,256,128]{4,3,2,1,0:T(8,128)(2,1)}, bf16[2,2,4,256,128]{4,3,2,1,0:T(8,128)(2,1)}, u32[]{:S(2)}, u32[]{:S(2)}) %collective-permute-start.14) | collective-permute-done | bytes 1048608 | tf_op jit(solution)/shard_map/ppermute | solution.py:225
  94.4 21.7 %feed_forward.1 = (bf16[2,2,4,256,128]{4,3,2,1,0:T(8,128)(2,1)S(1)}, bf16[2,2,4,256,128]{4,3,2,1,0:T(8,128)(2,1)}, bf16[2,2,4,256,128]{4,3,2,1,0:T(8,128)(2,1)},...) custom-call(s32[16]{0:T(128)S(1)} %get-tuple-element.34.places_in, ...), custom_call_target="tpu_custom_call" | custom-call | flops 4294967296 | bytes 26214400 | tf_op jit(solution)/shard_map/feed_forward/pallas_call | solution.py:183
  116.1 1.6 collective-permute-start.17
  117.6 0.6 collective-permute-start.20
  118.2 0.8 collective-permute-start.16
  119.0 2.4 %collective-permute-start.22 = (bf16[2,2,4,256,128]{4,3,2,1,0:T(8,128)(2,1)}, bf16[2,2,4,256,128]{4,3,2,1,0:T(8,128)(2,1)S(1)}, u32[]{:S(2)}, u32[]{:S(2)}) collective-permute-start(bf16[2,2,4,256,128]{4,3,2,1,0:T(8,128)(2,1)} %get-tuple-element.24), channel_id=1, source_target_pairs={{0,1},{1,2},{2,3},{3,0},{4,5},{5,6},{6,7},{7,4},{8,9},{9,10},{10,1... | collective-permute-start | bytes 3145736 | tf_op jit(solution)/shard_map/ppermute | solution.py:225
  121.4 9.7 %collective-permute-done.17 = bf16[2,2,4,256,128]{4,3,2,1,0:T(8,128)(2,1)S(1)} collective-permute-done((bf16[2,2,4,256,128]{4,3,2,1,0:T(8,128)(2,1)}, bf16[2,2,4,256,128]{4,3,2,1,0:T(8,128)(2,1)S(1)}, u32[]{:S(2)}, u32[]{:S(2)}) %collective-permute-start.17) | collective-permute-done | bytes 1048608 | tf_op jit(solution)/shard_map/ppermute | solution.py:225
  131.2 1.5 add_convert_fusion.1
  132.7 2.8 %collective-permute-start.18 = (bf16[2,2,4,256,128]{4,3,2,1,0:T(8,128)(2,1)S(1)}, bf16[2,2,4,256,128]{4,3,2,1,0:T(8,128)(2,1)S(1)}, u32[]{:S(2)}, u32[]{:S(2)}) collective-permute-start(bf16[2,2,4,256,128]{4,3,2,1,0:T(8,128)(2,1)S(1)} %add_convert_fusion.1), channel_id=1, source_target_pairs={{0,1},{1,2},{2,3},{3,0},{4,5},{5,6},{6,7},{7,4},{8,9},{9,10},{10,1... | collective-permute-start | bytes 3145736 | tf_op jit(solution)/shard_map/ppermute | solution.py:225
  135.4 0.3 add_convert_fusion
  135.7 0.1 collective-permute-start.21
  135.8 9.3 %collective-permute-done.16 = bf16[2,2,4,256,128]{4,3,2,1,0:T(8,128)(2,1)S(1)} collective-permute-done((bf16[2,2,4,256,128]{4,3,2,1,0:T(8,128)(2,1)}, bf16[2,2,4,256,128]{4,3,2,1,0:T(8,128)(2,1)S(1)}, u32[]{:S(2)}, u32[]{:S(2)}) %collective-permute-start.16) | collective-permute-done | bytes 1048608 | tf_op jit(solution)/shard_map/ppermute | solution.py:225
  145.1 8.5 %collective-permute-done.18 = bf16[2,2,4,256,128]{4,3,2,1,0:T(8,128)(2,1)S(1)} collective-permute-done((bf16[2,2,4,256,128]{4,3,2,1,0:T(8,128)(2,1)S(1)}, bf16[2,2,4,256,128]{4,3,2,1,0:T(8,128)(2,1)S(1)}, u32[]{:S(2)}, u32[]{:S(2)}) %collective-permute-start.18) | collective-permute-done | bytes 1048608 | tf_op jit(solution)/shard_map/ppermute | solution.py:225
  153.6 0.2 fusion.5
  153.8 0.8 collective-permute-start.19
  154.6 1.7 collective-permute-done.21
  156.3 0.5 fusion.6
  156.8 3.0 %collective-permute-start.23 = (bf16[2,4,256,128]{3,2,1,0:T(8,128)(2,1)S(1)}, bf16[2,4,256,128]{3,2,1,0:T(8,128)(2,1)S(1)}, u32[]{:S(2)}, u32[]{:S(2)}) collective-permute-start(bf16[2,4,256,128]{3,2,1,0:T(8,128)(2,1)S(1)} %get-tuple-element.27), channel_id=1, source_target_pairs={{0,12},{1,13},{2,14},{3,15},{4,0},{5,1},{6,2},{7,3},{8,4},{9,5},{1... | collective-permute-start | bytes 1572872 | tf_op jit(solution)/shard_map/ppermute | solution.py:225
  159.8 0.6 collective-permute-start.24
  160.3 4.0 %collective-permute-done.19 = bf16[2,4,256,128]{3,2,1,0:T(8,128)(2,1)S(1)} collective-permute-done((bf16[2,4,256,128]{3,2,1,0:T(8,128)(2,1)S(1)}, bf16[2,4,256,128]{3,2,1,0:T(8,128)(2,1)S(1)}, u32[]{:S(2)}, u32[]{:S(2)}) %collective-permute-start.19) | collective-permute-done | bytes 524320 | tf_op jit(solution)/shard_map/ppermute | solution.py:225
  164.3 7.8 %collective-permute-done.23 = bf16[2,4,256,128]{3,2,1,0:T(8,128)(2,1)S(1)} collective-permute-done((bf16[2,4,256,128]{3,2,1,0:T(8,128)(2,1)S(1)}, bf16[2,4,256,128]{3,2,1,0:T(8,128)(2,1)S(1)}, u32[]{:S(2)}, u32[]{:S(2)}) %collective-permute-start.23) | collective-permute-done | bytes 524320 | tf_op jit(solution)/shard_map/ppermute | solution.py:225
  172.1 0.5 fusion.3
  172.6 0.7 slice_bitcast_fusion
  173.4 1.5 collective-permute-done.25.traded_ref
  174.9 0.7 copy-done.10
  175.6 1.9 %result.1 = bf16[512,512]{1,0:T(8,128)(2,1)} custom-call(s32[1]{0:T(128)} %bitcast.core_ref, bf16[4,256,128]{2,1,0:T(8,128)(2,1)} %get-tuple-element.30.mine_ref, bf16[4,256,128]{2,1,0:T(8,128)(2,1)} %copy-done.10), custom_call_target="tpu_custom_call" | custom-call | tf_op jit(solution)/shard_map/result/pallas_call | solution.py:325
  (34 shorter events, 0.2 us)
Async XLA Ops:
  2.4 1.6 collective-permute-start
  4.9 9.8 %collective-permute-start.2 = (bf16[2,128,128]{2,1,0:T(8,128)(2,1)S(1)}, bf16[2,128,128]{2,1,0:T(8,128)(2,1)S(1)}, u32[]{:S(2)}, u32[]{:S(2)}) collective-permute-start(bf16[2,128,128]{2,1,0:T(8,128)(2,1)S(1)} %fusion.9), channel_id=1, source_target_pairs={{0,64},{16,80},{32,96},{48,112},{64,128},{80,144},{96,160},{112,17... | collective-permute-start | bytes 196616 | tf_op jit(solution)/shard_map/ppermute | solution.py:251
  8.3 6.4 %collective-permute-start.1 = (bf16[2,128,128]{2,1,0:T(8,128)(2,1)S(1)}, bf16[2,128,128]{2,1,0:T(8,128)(2,1)S(1)}, u32[]{:S(2)}, u32[]{:S(2)}) collective-permute-start(bf16[2,128,128]{2,1,0:T(8,128)(2,1)S(1)} %fusion.9), channel_id=1, source_target_pairs={{0,32},{16,48},{32,64},{48,80},{64,96},{80,112},{96,128},{112,144}... | collective-permute-start | bytes 196616 | tf_op jit(solution)/shard_map/ppermute | solution.py:251
  14.8 2.0 %collective-permute-start.4 = (bf16[2,128,128]{2,1,0:T(8,128)(2,1)S(1)}, bf16[2,128,128]{2,1,0:T(8,128)(2,1)S(1)}, u32[]{:S(2)}, u32[]{:S(2)}) collective-permute-start(bf16[2,128,128]{2,1,0:T(8,128)(2,1)S(1)} %add_convert_fusion.6), channel_id=1, source_target_pairs={{0,192},{16,208},{32,224},{48,240},{1,193},{17,209},{33,225},{49,2... | collective-permute-start | bytes 196616 | tf_op jit(solution)/shard_map/ppermute | solution.py:251
  15.4 11.2 %collective-permute-start.3 = (bf16[2,128,128]{2,1,0:T(8,128)(2,1)S(1)}, bf16[2,128,128]{2,1,0:T(8,128)(2,1)S(1)}, u32[]{:S(2)}, u32[]{:S(2)}) collective-permute-start(bf16[2,128,128]{2,1,0:T(8,128)(2,1)S(1)} %add_convert_fusion.6), channel_id=1, source_target_pairs={{0,96},{16,112},{32,128},{48,144},{64,160},{80,176},{96,192},{112,... | collective-permute-start | bytes 196616 | tf_op jit(solution)/shard_map/ppermute | solution.py:251
  26.6 4.2 %collective-permute-start.5 = (bf16[2,128,128]{2,1,0:T(8,128)(2,1)S(1)}, bf16[2,128,128]{2,1,0:T(8,128)(2,1)S(1)}, u32[]{:S(2)}, u32[]{:S(2)}) collective-permute-start(bf16[2,128,128]{2,1,0:T(8,128)(2,1)S(1)} %get-tuple-element.25), channel_id=1, source_target_pairs={{0,16},{16,0},{32,48},{48,32},{64,80},{80,64},{96,112},{112,96},{1... | collective-permute-start | bytes 196616 | tf_op jit(solution)/shard_map/ppermute | solution.py:229
  34.7 1.9 %collective-permute-start.6 = (bf16[4,256,128]{2,1,0:T(8,128)(2,1)}, bf16[4,256,128]{2,1,0:T(8,128)(2,1)S(1)}, u32[]{:S(2)}, u32[]{:S(2)}) collective-permute-start(bf16[4,256,128]{2,1,0:T(8,128)(2,1)} %get-tuple-element.16), channel_id=1, source_target_pairs={{0,16},{16,0},{32,48},{48,32},{64,80},{80,64},{96,112},{112,96},{1... | collective-permute-start | bytes 786440 | tf_op jit(solution)/shard_map/ppermute | solution.py:229
  37.6 15.2 %collective-permute-start.9 = (bf16[2,4,256,128]{3,2,1,0:T(8,128)(2,1)S(1)}, bf16[2,4,256,128]{3,2,1,0:T(8,128)(2,1)S(1)}, u32[]{:S(2)}, u32[]{:S(2)}) collective-permute-start(bf16[2,4,256,128]{3,2,1,0:T(8,128)(2,1)S(1)} %get-tuple-element.32), channel_id=1, source_target_pairs={{0,12},{1,13},{2,14},{3,15},{4,0},{5,1},{6,2},{7,3},{8,4},{9,5},{1... | collective-permute-start | bytes 1572872 | tf_op jit(solution)/shard_map/ppermute | solution.py:225
  40.5 12.4 %collective-permute-start.8 = (bf16[2,4,256,128]{3,2,1,0:T(8,128)(2,1)S(1)}, bf16[2,4,256,128]{3,2,1,0:T(8,128)(2,1)S(1)}, u32[]{:S(2)}, u32[]{:S(2)}) collective-permute-start(bf16[2,4,256,128]{3,2,1,0:T(8,128)(2,1)S(1)} %get-tuple-element.32), channel_id=1, source_target_pairs={{0,8},{1,9},{2,10},{3,11},{4,12},{5,13},{6,14},{7,15},{8,0},{9,1},... | collective-permute-start | bytes 1572872 | tf_op jit(solution)/shard_map/ppermute | solution.py:225
  41.2 15.5 %collective-permute-start.7 = (bf16[2,4,256,128]{3,2,1,0:T(8,128)(2,1)S(1)}, bf16[2,4,256,128]{3,2,1,0:T(8,128)(2,1)S(1)}, u32[]{:S(2)}, u32[]{:S(2)}) collective-permute-start(bf16[2,4,256,128]{3,2,1,0:T(8,128)(2,1)S(1)} %get-tuple-element.32), channel_id=1, source_target_pairs={{0,4},{1,5},{2,6},{3,7},{4,8},{5,9},{6,10},{7,11},{8,12},{9,13},{1... | collective-permute-start | bytes 1572872 | tf_op jit(solution)/shard_map/ppermute | solution.py:225
  52.8 20.5 %copy-start.3 = (s32[4]{0:T(128)S(1)}, s32[4]{0:T(128)}, u32[]{:S(2)}) copy-start(s32[4]{0:T(128)} %constant.91.clone) | copy-start | bytes 52
  52.8 41.5 %copy-start = (f32[8192]{0:T(1024)S(1)}, f32[8192]{0:T(1024)}, u32[]{:S(2)}) copy-start(f32[8192]{0:T(1024)} %param.16) | copy-start | bytes 98308
  52.8 41.5 %copy-start.1 = (s32[8,16]{1,0:T(8,128)S(1)}, s32[8,16]{1,0:T(8,128)}, u32[]{:S(2)}) copy-start(s32[8,16]{1,0:T(8,128)} %up_index.1) | copy-start | bytes 1540
  52.8 41.5 %copy-start.2 = (s32[8,16]{1,0:T(8,128)S(1)}, s32[8,16]{1,0:T(8,128)}, u32[]{:S(2)}) copy-start(s32[8,16]{1,0:T(8,128)} %down_index.1) | copy-start | bytes 1540
  52.9 41.4 %copy-start.4 = (bf16[2,2,4,256,128]{4,3,2,1,0:T(8,128)(2,1)}, bf16[2,2,4,256,128]{4,3,2,1,0:T(8,128)(2,1)S(1)}, u32[]{:S(2)}) copy-start(bf16[2,2,4,256,128]{4,3,2,1,0:T(8,128)(2,1)S(1)} %pad_maximum_fusion.1.refs_1_) | copy-start | bytes 3145732
  52.9 16.1 %collective-permute-start.13 = (bf16[2,2,4,256,128]{4,3,2,1,0:T(8,128)(2,1)S(1)}, bf16[2,2,4,256,128]{4,3,2,1,0:T(8,128)(2,1)S(1)}, u32[]{:S(2)}, u32[]{:S(2)}) collective-permute-start(bf16[2,2,4,256,128]{4,3,2,1,0:T(8,128)(2,1)S(1)} %pad_maximum_fusion.1.refs_1_), channel_id=1, source_target_pairs={{0,3},{1,0},{2,1},{3,2},{4,7},{5,4},{6,5},{7,6},{8,11},{9,8},{10,9... | collective-permute-start | bytes 3145736 | tf_op jit(solution)/shard_map/ppermute | solution.py:225
  56.9 37.5 %copy-start.5 = (bf16[2,2,4,256,128]{4,3,2,1,0:T(8,128)(2,1)}, bf16[2,2,4,256,128]{4,3,2,1,0:T(8,128)(2,1)S(1)}, u32[]{:S(2)}) copy-start(bf16[2,2,4,256,128]{4,3,2,1,0:T(8,128)(2,1)S(1)} %pad_maximum_fusion.refs_0_) | copy-start | bytes 3145732
  56.9 15.0 %collective-permute-start.10 = (bf16[2,2,4,256,128]{4,3,2,1,0:T(8,128)(2,1)S(1)}, bf16[2,2,4,256,128]{4,3,2,1,0:T(8,128)(2,1)}, u32[]{:S(2)}, u32[]{:S(2)}) collective-permute-start(bf16[2,2,4,256,128]{4,3,2,1,0:T(8,128)(2,1)S(1)} %pad_maximum_fusion.refs_0_), channel_id=1, source_target_pairs={{0,1},{1,2},{2,3},{3,0},{4,5},{5,6},{6,7},{7,4},{8,9},{9,10},{10,1... | collective-permute-start | bytes 3145736 | tf_op jit(solution)/shard_map/ppermute | solution.py:225
  57.2 25.9 %collective-permute-start.11 = (bf16[2,2,4,256,128]{4,3,2,1,0:T(8,128)(2,1)S(1)}, bf16[2,2,4,256,128]{4,3,2,1,0:T(8,128)(2,1)}, u32[]{:S(2)}, u32[]{:S(2)}) collective-permute-start(bf16[2,2,4,256,128]{4,3,2,1,0:T(8,128)(2,1)S(1)} %pad_maximum_fusion.1.refs_1_), channel_id=1, source_target_pairs={{0,1},{1,2},{2,3},{3,0},{4,5},{5,6},{6,7},{7,4},{8,9},{9,10},{10,1... | collective-permute-start | bytes 3145736 | tf_op jit(solution)/shard_map/ppermute | solution.py:225
  58.7 24.3 %collective-permute-start.12 = (bf16[2,2,4,256,128]{4,3,2,1,0:T(8,128)(2,1)S(1)}, bf16[2,2,4,256,128]{4,3,2,1,0:T(8,128)(2,1)}, u32[]{:S(2)}, u32[]{:S(2)}) collective-permute-start(bf16[2,2,4,256,128]{4,3,2,1,0:T(8,128)(2,1)S(1)} %pad_maximum_fusion.refs_0_), channel_id=1, source_target_pairs={{0,3},{1,0},{2,1},{3,2},{4,7},{5,4},{6,5},{7,6},{8,11},{9,8},{10,9... | collective-permute-start | bytes 3145736 | tf_op jit(solution)/shard_map/ppermute | solution.py:225
  69.0 25.3 %copy-start.9 = (bf16[2,2,4,256,128]{4,3,2,1,0:T(8,128)(2,1)}, bf16[2,2,4,256,128]{4,3,2,1,0:T(8,128)(2,1)S(1)}, u32[]{:S(2)}) copy-start(bf16[2,2,4,256,128]{4,3,2,1,0:T(8,128)(2,1)S(1)} %collective-permute-done.13.refs_5_) | copy-start | bytes 3145732
  69.0 22.6 %collective-permute-start.15 = (bf16[2,2,4,256,128]{4,3,2,1,0:T(8,128)(2,1)S(1)}, bf16[2,2,4,256,128]{4,3,2,1,0:T(8,128)(2,1)}, u32[]{:S(2)}, u32[]{:S(2)}) collective-permute-start(bf16[2,2,4,256,128]{4,3,2,1,0:T(8,128)(2,1)S(1)} %collective-permute-done.13.refs_5_), channel_id=1, source_target_pairs={{0,3},{1,0},{2,1},{3,2},{4,7},{5,4},{6,5},{7,6},{8,11},{9,8},{10,9... | collective-permute-start | bytes 3145736 | tf_op jit(solution)/shard_map/ppermute | solution.py:225
  71.9 22.5 %collective-permute-start.14 = (bf16[2,2,4,256,128]{4,3,2,1,0:T(8,128)(2,1)}, bf16[2,2,4,256,128]{4,3,2,1,0:T(8,128)(2,1)}, u32[]{:S(2)}, u32[]{:S(2)}) collective-permute-start(bf16[2,2,4,256,128]{4,3,2,1,0:T(8,128)(2,1)} %collective-permute-done.10.refs_2_), channel_id=1, source_target_pairs={{0,1},{1,2},{2,3},{3,0},{4,5},{5,6},{6,7},{7,4},{8,9},{9,10},{10,1... | collective-permute-start | bytes 3145736 | tf_op jit(solution)/shard_map/ppermute | solution.py:225
  116.1 19.4 %copy-start.6 = (bf16[2,2,4,256,128]{4,3,2,1,0:T(8,128)(2,1)S(1)}, bf16[2,2,4,256,128]{4,3,2,1,0:T(8,128)(2,1)}, u32[]{:S(2)}) copy-start(bf16[2,2,4,256,128]{4,3,2,1,0:T(8,128)(2,1)} %get-tuple-element.23) | copy-start | bytes 3145732
  116.1 15.1 %collective-permute-start.17 = (bf16[2,2,4,256,128]{4,3,2,1,0:T(8,128)(2,1)}, bf16[2,2,4,256,128]{4,3,2,1,0:T(8,128)(2,1)S(1)}, u32[]{:S(2)}, u32[]{:S(2)}) collective-permute-start(bf16[2,2,4,256,128]{4,3,2,1,0:T(8,128)(2,1)} %get-tuple-element.19), channel_id=1, source_target_pairs={{0,1},{1,2},{2,3},{3,0},{4,5},{5,6},{6,7},{7,4},{8,9},{9,10},{10,1... | collective-permute-start | bytes 3145736 | tf_op jit(solution)/shard_map/ppermute | solution.py:225
  117.6 17.8 %collective-permute-start.20 = (bf16[2,2,4,256,128]{4,3,2,1,0:T(8,128)(2,1)}, bf16[2,2,4,256,128]{4,3,2,1,0:T(8,128)(2,1)S(1)}, u32[]{:S(2)}, u32[]{:S(2)}) collective-permute-start(bf16[2,2,4,256,128]{4,3,2,1,0:T(8,128)(2,1)} %get-tuple-element.22), channel_id=1, source_target_pairs={{0,3},{1,0},{2,1},{3,2},{4,7},{5,4},{6,5},{7,6},{8,11},{9,8},{10,9... | collective-permute-start | bytes 3145736 | tf_op jit(solution)/shard_map/ppermute | solution.py:225
  118.2 26.9 %collective-permute-start.16 = (bf16[2,2,4,256,128]{4,3,2,1,0:T(8,128)(2,1)}, bf16[2,2,4,256,128]{4,3,2,1,0:T(8,128)(2,1)S(1)}, u32[]{:S(2)}, u32[]{:S(2)}) collective-permute-start(bf16[2,2,4,256,128]{4,3,2,1,0:T(8,128)(2,1)} %get-tuple-element.18), channel_id=1, source_target_pairs={{0,3},{1,0},{2,1},{3,2},{4,7},{5,4},{6,5},{7,6},{8,11},{9,8},{10,9... | collective-permute-start | bytes 3145736 | tf_op jit(solution)/shard_map/ppermute | solution.py:225
  119.0 35.6 %collective-permute-start.22 = (bf16[2,2,4,256,128]{4,3,2,1,0:T(8,128)(2,1)}, bf16[2,2,4,256,128]{4,3,2,1,0:T(8,128)(2,1)S(1)}, u32[]{:S(2)}, u32[]{:S(2)}) collective-permute-start(bf16[2,2,4,256,128]{4,3,2,1,0:T(8,128)(2,1)} %get-tuple-element.24), channel_id=1, source_target_pairs={{0,1},{1,2},{2,3},{3,0},{4,5},{5,6},{6,7},{7,4},{8,9},{9,10},{10,1... | collective-permute-start | bytes 3145736 | tf_op jit(solution)/shard_map/ppermute | solution.py:225
  132.7 21.0 %collective-permute-start.18 = (bf16[2,2,4,256,128]{4,3,2,1,0:T(8,128)(2,1)S(1)}, bf16[2,2,4,256,128]{4,3,2,1,0:T(8,128)(2,1)S(1)}, u32[]{:S(2)}, u32[]{:S(2)}) collective-permute-start(bf16[2,2,4,256,128]{4,3,2,1,0:T(8,128)(2,1)S(1)} %add_convert_fusion.1), channel_id=1, source_target_pairs={{0,1},{1,2},{2,3},{3,0},{4,5},{5,6},{6,7},{7,4},{8,9},{9,10},{10,1... | collective-permute-start | bytes 3145736 | tf_op jit(solution)/shard_map/ppermute | solution.py:225
  135.4 20.9 %copy-start.8 = (bf16[2,2,4,256,128]{4,3,2,1,0:T(8,128)(2,1)S(1)}, bf16[2,2,4,256,128]{4,3,2,1,0:T(8,128)(2,1)}, u32[]{:S(2)}) copy-start(bf16[2,2,4,256,128]{4,3,2,1,0:T(8,128)(2,1)} %get-tuple-element.21) | copy-start | bytes 3145732
  135.7 20.6 %collective-permute-start.21 = (bf16[2,2,4,256,128]{4,3,2,1,0:T(8,128)(2,1)S(1)}, bf16[2,2,4,256,128]{4,3,2,1,0:T(8,128)(2,1)S(1)}, u32[]{:S(2)}, u32[]{:S(2)}) collective-permute-start(bf16[2,2,4,256,128]{4,3,2,1,0:T(8,128)(2,1)S(1)} %add_convert_fusion), channel_id=1, source_target_pairs={{0,3},{1,0},{2,1},{3,2},{4,7},{5,4},{6,5},{7,6},{8,11},{9,8},{10,9... | collective-permute-start | bytes 3145736 | tf_op jit(solution)/shard_map/ppermute | solution.py:225
  153.8 10.5 %collective-permute-start.19 = (bf16[2,4,256,128]{3,2,1,0:T(8,128)(2,1)S(1)}, bf16[2,4,256,128]{3,2,1,0:T(8,128)(2,1)S(1)}, u32[]{:S(2)}, u32[]{:S(2)}) collective-permute-start(bf16[2,4,256,128]{3,2,1,0:T(8,128)(2,1)S(1)} %fusion.5), channel_id=1, source_target_pairs={{0,4},{1,5},{2,6},{3,7},{4,8},{5,9},{6,10},{7,11},{8,12},{9,13},{1... | collective-permute-start | bytes 1572872 | tf_op jit(solution)/shard_map/ppermute | solution.py:225
  156.3 15.8 %copy-start.7 = (bf16[4,256,128]{2,1,0:T(8,128)(2,1)S(1)}, bf16[4,256,128]{2,1,0:T(8,128)(2,1)}, u32[]{:S(2)}) copy-start(bf16[4,256,128]{2,1,0:T(8,128)(2,1)} %get-tuple-element.15) | copy-start | bytes 786436
  156.8 15.3 %collective-permute-start.23 = (bf16[2,4,256,128]{3,2,1,0:T(8,128)(2,1)S(1)}, bf16[2,4,256,128]{3,2,1,0:T(8,128)(2,1)S(1)}, u32[]{:S(2)}, u32[]{:S(2)}) collective-permute-start(bf16[2,4,256,128]{3,2,1,0:T(8,128)(2,1)S(1)} %get-tuple-element.27), channel_id=1, source_target_pairs={{0,12},{1,13},{2,14},{3,15},{4,0},{5,1},{6,2},{7,3},{8,4},{9,5},{1... | collective-permute-start | bytes 1572872 | tf_op jit(solution)/shard_map/ppermute | solution.py:225
  159.8 12.3 %collective-permute-start.24 = (bf16[2,4,256,128]{3,2,1,0:T(8,128)(2,1)S(1)}, bf16[2,4,256,128]{3,2,1,0:T(8,128)(2,1)S(1)}, u32[]{:S(2)}, u32[]{:S(2)}) collective-permute-start(bf16[2,4,256,128]{3,2,1,0:T(8,128)(2,1)S(1)} %get-tuple-element.28), channel_id=1, source_target_pairs={{0,8},{1,9},{2,10},{3,11},{4,12},{5,13},{6,14},{7,15},{8,0},{9,1},... | collective-permute-start | bytes 1572872 | tf_op jit(solution)/shard_map/ppermute | solution.py:225
  173.4 1.5 collective-permute-start.25
  174.9 0.7 copy-start.10
where the time goes:
time: 181 us; the launch traced here: 178 us
  waiting for transfers between devices  106 us (59%)
  Pallas kernels  33.2 us (18%)
  starting transfers between devices  29.7 us (16%)
  other arithmetic  6.02 us (3%)
  local copies, waits for them, and re-layouts  2.14 us (1%)
    ppermute x18, waiting for transfers between devices, torus_shift(): return lax.ppermute(x, ('seq', 'wt'), pairs)  87.4 us
    ppermute x18, starting transfers between devices, torus_shift(): return lax.ppermute(x, ('seq', 'wt'), pairs)  21.9 us
    pallas_call x1, Pallas kernels, ffn(): pl.pallas_call(ffn_kernel, out_shape=[PIECE] * 8, in_specs=[SMEM] * 4 + [...  21.7 us
    ppermute x4, waiting for transfers between devices, later(): lax.ppermute(x, 'seq', [(s, s + 2 * places) for s in range(SEQ) if s + 2...  14.4 us
    ppermute x4, starting transfers between devices, later(): lax.ppermute(x, 'seq', [(s, s + 2 * places) for s in range(SEQ) if s + 2...  7.26 us
    ppermute x4, waiting for transfers between devices, swap_cores(): return lax.ppermute(x, 'seq', [(s, s ^ 1) for s in range(SEQ)])  4.46 us
    pallas_call x1, Pallas kernels, per_device(): pl.pallas_call(intra_kernel, out_shape=jax.ShapeDtypeStruct((4, 512, HEAD...  4.05 us
  transfers between devices with their start and end apart: 26, of which 18 were waited for; matrix products, arithmetic and copies ran while one was open for 2% of the time, Pallas kernels for 2%

commit v1 on v0

--- a/solution.py
+++ b/solution.py
@@ -1,3 +1,5 @@
+import functools
+
 import jax
 import jax.numpy as jnp
 from jax import lax
@@ -72,16 +74,14 @@
         give_ref[h] = jnp.where(first, mid[256:], mid[:256])
 
 
-def ffn_kernel(places_in, places_out, up_index, down_index, gain_ref, *refs):
-    pieces, (up_hbm, down_hbm), outs = refs[:8], refs[8:10], refs[10:18]
-    x_0, x_1, up_w, down_w, acc_0, acc_1, stage, squares, in_sem, up_sem, down_sem, out_sem = refs[18:]
-    xs, accs = (x_0, x_1), (acc_0, acc_1)
+def ffn_kernel(t, places_in, places_out, up_index, down_index, gain_ref, *refs):
+    pieces, (up_hbm, down_hbm), outs = refs[:8], refs[8:10], refs[10:14]
+    x, up_w, down_w, acc, stage, squares, in_sem, up_sem, down_sem, out_sem = refs[14:]
     n_hidden, kept = up_w.shape[:2]
-    each = 16 // n_hidden
-
-    def piece_copy(i, t):
-        source = pieces[i // 2].at[i % 2, t]
-        return pltpu.make_async_copy(source, xs[t].at[pl.ds(places_in[i] * 4, 4)], in_sem.at[i, t])
+
+    def piece_copy(i):
+        source = pieces[i // 2].at[i % 2 if i >= 12 else 2 * t + i % 2]
+        return pltpu.make_async_copy(source, x.at[pl.ds(places_in[i] * 4, 4)], in_sem.at[i])
 
     def up_copy(c):
         return pltpu.make_async_copy(up_hbm.at[c], up_w.at[c], up_sem.at[c])
@@ -89,120 +89,75 @@
     def down_copy(c):
         return pltpu.make_async_copy(down_hbm.at[c], down_w.at[c], down_sem.at[c])
 
-    def out_copy(i, t):
-        target = outs[i // 2].at[i % 2, t]
-        return pltpu.make_async_copy(stage.at[t, pl.ds(i * 4, 4)], target, out_sem.at[i, t])
-
-    def make_ready(i, t):
-        total = squares[t]
+    def out_copy(i):
+        return pltpu.make_async_copy(stage.at[pl.ds(i * 4, 4)], outs[i // 4].at[i % 4], out_sem.at[i])
+
+    for i in range(16):
+        piece_copy(i).start()
+    for c in range(n_hidden):
+        up_copy(c).start()
+        down_copy(c).start()
+    squares[...] = jnp.zeros(squares.shape, F32)
+
+    @pl.loop(0, 64)
+    def _(j):
+        acc[j] = jnp.zeros((256, 128), F32)
+
+    for i in range(16):
+        piece_copy(i).wait()
+        total = squares[...]
         for b in range(4):
             block = places_in[i] * 4 + b
-            value = xs[t][block].astype(F32)
+            value = x[block].astype(F32)
             total = total + value * value
-            xs[t][block] = (value * gain_ref[pl.ds(block, 1), :]).astype(BF16)
-        squares[t] = total
-
-    def clear(j, t):
-        accs[t][j] = jnp.zeros((256, 128), F32)
-
-    def leave(i, t):
-        for b in range(4):
-            stage[t, i * 4 + b] = accs[t][places_out[i] * 4 + b].astype(BF16)
-
-    def products(c, t, scale):
-        picked = jnp.concatenate([xs[t][up_index[c, k]] for k in range(kept)], axis=1)
+            x[block] = (value * gain_ref[pl.ds(block, 1), :]).astype(BF16)
+        squares[...] = total
+    mean = jnp.sum(squares[...], axis=-1, keepdims=True) * (1.0 / (64 * 128))
+    scale = lax.rsqrt(mean + 1e-06)
+
+    @pl.loop(0, n_hidden)
+    def _(c):
+        up_copy(c).wait()
+        down_copy(c).wait()
+        picked = jnp.concatenate([x[up_index[c, k]] for k in range(kept)], axis=1)
         upper = dot(picked, up_w[c].reshape(kept * BLK, BLK)) * scale
         act = (upper / (1.0 + jnp.exp(-upper))).astype(BF16)
         for k in range(0, kept, 2):
             part = dot(act, jnp.concatenate([down_w[c, k], down_w[c, k + 1]], axis=1))
-            accs[t][down_index[c, k]] += part[:, :BLK]
-            accs[t][down_index[c, k + 1]] += part[:, BLK:]
-
-    def scale_of(t):
-        mean = jnp.sum(squares[t], axis=-1, keepdims=True) * (1.0 / (64 * 128))
-        return lax.rsqrt(mean + 1e-06)
+            acc[down_index[c, k]] += part[:, :BLK]
+            acc[down_index[c, k + 1]] += part[:, BLK:]
 
     for i in range(16):
-        piece_copy(i, 0).start()
-    for c in range(n_hidden):
-        up_copy(c).start()
-        down_copy(c).start()
+        for b in range(4):
+            stage[i * 4 + b] = acc[places_out[i] * 4 + b].astype(BF16)
+        out_copy(i).start()
     for i in range(16):
-        piece_copy(i, 1).start()
-    squares[...] = jnp.zeros(squares.shape, F32)
-
-    @pl.loop(0, 64)
-    def _(j):
-        clear(j, 0)
-
-    for i in range(16):
-        piece_copy(i, 0).wait()
-        make_ready(i, 0)
-    scale = scale_of(0)
-
-    @pl.loop(0, n_hidden)
-    def _(c):
-        up_copy(c).wait()
-        down_copy(c).wait()
-        for e in range(each):
-            i = c * each + e
-            pltpu.make_async_copy(pieces[0].at[0, 1], x_1.at[pl.ds(0, 4)], in_sem.at[i, 1]).wait()
-        for e in range(each):
-            i = c * each + e
-            make_ready(i, 1)
-            for b in range(4):
-                clear(i * 4 + b, 1)
-        products(c, 0, scale)
-
-    scale_1 = scale_of(1)
-
-    @pl.loop(0, n_hidden)
-    def _(c):
-        for e in range(each):
-            leave(c * each + e, 0)
-        products(c, 1, scale_1)
-        for i in range(16):
-
-            @pl.when(c == i // each)
-            def _():
-                out_copy(i, 0).start()
-
-    for i in range(16):
-        leave(i, 1)
-        out_copy(i, 1).start()
-    for i in range(16):
-        for t in range(2):
-            out_copy(i, t).wait()
-
-
-PIECE = jax.ShapeDtypeStruct((2, 2, 4, 256, 128), BF16)
-
-
-def ffn(pieces, places_in, places_out, up_index, down_index, gain, up_blocks, down_blocks):
+        out_copy(i).wait()
+
+
+def ffn(t, pieces, places_in, places_out, up_index, down_index, gain, up_blocks, down_blocks):
     n_hidden, kept = up_index.shape
     return pl.pallas_call(
-        ffn_kernel,
-        out_shape=[PIECE] * 8,
+        functools.partial(ffn_kernel, t),
+        out_shape=[jax.ShapeDtypeStruct((4, 4, 256, 128), BF16)] * 4,
         in_specs=[SMEM] * 4 + [VMEM] + [ANY] * 10,
-        out_specs=[ANY] * 8,
+        out_specs=[ANY] * 4,
         scratch_shapes=[
-            pltpu.VMEM((64, 256, 128), BF16),
             pltpu.VMEM((64, 256, 128), BF16),
             pltpu.VMEM((n_hidden, kept, BLK, BLK), BF16),
             pltpu.VMEM((n_hidden, kept, BLK, BLK), BF16),
             pltpu.VMEM((64, 256, 128), F32),
-            pltpu.VMEM((64, 256, 128), F32),
-            pltpu.VMEM((2, 64, 256, 128), BF16),
-            pltpu.VMEM((2, 256, 128), F32),
-            pltpu.SemaphoreType.DMA((16, 2)),
+            pltpu.VMEM((64, 256, 128), BF16),
+            pltpu.VMEM((256, 128), F32),
+            pltpu.SemaphoreType.DMA((16,)),
             pltpu.SemaphoreType.DMA((n_hidden,)),
             pltpu.SemaphoreType.DMA((n_hidden,)),
-            pltpu.SemaphoreType.DMA((16, 2)),
+            pltpu.SemaphoreType.DMA((16,)),
         ],
         name="feed_forward",
-        compiler_params=pltpu.CompilerParams(vmem_limit_bytes=52 * 2**20),
+        compiler_params=pltpu.CompilerParams(vmem_limit_bytes=40 * 2**20),
         cost_estimate=pl.CostEstimate(
-            flops=4 * 512 * n_hidden * kept * BLK * BLK, bytes_accessed=25 * 2**20, transcendentals=512 * 1024
+            flops=4 * 256 * n_hidden * kept * BLK * BLK, bytes_accessed=17 * 2**20, transcendentals=256 * 1024
         ),
     )(places_in, places_out, up_index, down_index, gain, *pieces, up_blocks, down_blocks)
 
@@ -229,11 +184,20 @@
     return lax.ppermute(x, "seq", [(s, s ^ 1) for s in range(SEQ)])
 
 
+def by_set(one, two):
+    return jnp.stack([one[0], two[0], one[1], two[1]])
+
+
 def added(*terms):
     total = terms[0].astype(F32)
     for t in terms[1:]:
         total = total + t.astype(F32)
     return total.astype(BF16)
+
+
+def near_sum(own, ahead, back):
+    rows = [added(own[r], ahead[r], back[r]) for r in range(4)]
+    return [rows[0], torus_shift(rows[1], 0, 1), torus_shift(rows[3], 0, -1), torus_shift(rows[2], 0, 2)]
 
 
 def finished(mid, terms):
@@ -297,38 +261,39 @@
     def where(sign):
         return ((at_x + sign * step_x + SIDE) % SIDE) * SIDE + (at_y + sign * step_y + SIDE) % SIDE
 
-    both = jnp.stack([keep, swap_cores(give)])
+    both = jnp.stack([swap_cores(give), keep])
     near_1, near_3, near_2 = torus_shift(both, 0, 1), torus_shift(both, 0, -1), torus_shift(both, 0, 2)
-    own_a, own_b = jnp.stack([both, near_1]), jnp.stack([near_2, near_3])
+    own_a, own_b = by_set(both, near_1), by_set(near_2, near_3)
     ahead_a = torus_shift(own_a, 1, 1)
     back_b = torus_shift(own_b, 1, -1)
     ahead_b = torus_shift(own_b, 1, 1)
     back_a = torus_shift(own_a, 1, -1)
-    far_a = torus_shift(ahead_a, 1, 1)
-    far_b = torus_shift(back_b, 1, -1)
-
-    pieces = (own_a, own_b, ahead_a, ahead_b, back_a, back_b, far_a, far_b)
+    far_0 = torus_shift(ahead_a[:2], 1, 1), torus_shift(back_b[:2], 1, -1)
+    far_1 = torus_shift(ahead_a[2:], 1, 1), torus_shift(back_b[2:], 1, -1)
+
+    pieces = (own_a, own_b, ahead_a, ahead_b, back_a, back_b)
     gain = mlp_gain.reshape(64, BLK)
-    own_a, own_b, ahead_a, ahead_b, back_a, back_b, far_a, far_b = ffn(
-        pieces, where(-1), where(1), up_index, down_index, gain, up_blocks, down_blocks
-    )
-    via_a = torus_shift(far_a, 1, 1)
-    via_b = torus_shift(far_b, 1, -1)
-    from_back_b = torus_shift(ahead_b, 1, 1)
-    from_ahead_a = torus_shift(back_a, 1, -1)
-    from_back_a = torus_shift(added(via_a, ahead_a), 1, 1)
-    from_ahead_b = torus_shift(added(via_b, back_b), 1, -1)
-    rows = [added(own_a[r], from_ahead_a[r], from_back_a[r]) for r in range(2)]
-    rows += [added(own_b[r], from_ahead_b[r], from_back_b[r]) for r in range(2)]
-    terms = [rows[0], torus_shift(rows[1], 0, 1), torus_shift(rows[3], 0, -1), torus_shift(rows[2], 0, 2)]
-    done = finished(both, terms)
+    local = (where(-1), where(1), up_index, down_index, gain, up_blocks, down_blocks)
+
+    own_0, ahead_0, back_0, away_0 = ffn(0, (*pieces, *far_0), *local)
+    via_0 = torus_shift(away_0, 1, 1)
+    from_ahead_0 = torus_shift(back_0, 1, -1)
+    far_1, own_0 = lax.optimization_barrier((far_1, own_0))
+    own_1, ahead_1, back_1, away_1 = ffn(1, (*pieces, *far_1), *local)
+    via_1 = torus_shift(away_1, 1, -1)
+    via_0, from_ahead_0, own_1 = lax.optimization_barrier((via_0, from_ahead_0, own_1))
+    from_back_0 = torus_shift(added(ahead_0, via_0), 1, 1)
+    from_back_1 = torus_shift(ahead_1, 1, 1)
+    from_ahead_1 = torus_shift(added(back_1, via_1), 1, -1)
+    traded = swap_cores(finished(both[0], near_sum(own_0, from_ahead_0, from_back_0)))
+    kept = finished(both[1], near_sum(own_1, from_ahead_1, from_back_1))
     return pl.pallas_call(
         result_kernel,
         out_shape=jax.ShapeDtypeStruct((512, 512), BF16),
         in_specs=[SMEM] + [VMEM] * 2,
         out_specs=VMEM,
         name="result",
-    )(core_arg, done[0], swap_cores(done[1]))
+    )(core_arg, kept, traded)
 
 
 def solution(mesh):

time: 181 us -> 176 us (0.972); the launches traced: 178 us -> 175 us
  waiting for transfers between devices: 106 us -> 87.7 us
  starting transfers between devices: 29.7 us -> 40.4 us
  local copies, waits for them, and re-layouts: 2.14 us -> 5.78 us
  Pallas kernels: 33.2 us -> 35.5 us
    ppermute x18 -> x23, waiting for transfers between devices: 87.4 us -> 70.4 us  [torus_shift(): return lax.ppermute(x, ('seq', 'wt'), pairs)]
    ppermute x18 -> x23, starting transfers between devices: 21.9 us -> 32.4 us  [torus_shift(): return lax.ppermute(x, ('seq', 'wt'), pairs)]
    pallas_call x1 -> x2, Pallas kernels: 21.7 us -> 23.9 us  [ffn(): pl.pallas_call(functools.partial(ffn_kernel, t), out_shape=[jax.ShapeDtyp...]
    slice x0 -> x5, local copies, waits for them, and re-layouts: none -> 2.2 us  [the longest x2 2.09 us: per_device(): far_0 = (torus_shift(ahead_a[:2], 1, 1), torus_shift(back_b[:2], 1, -1))]
    unnamed x22 -> x20, local copies, waits for them, and re-layouts: 0.74 us -> 2.92 us
  transfers between devices with their start and end apart: 26 -> 31, of which waited for: 18 -> 16; matrix products, arithmetic and copies ran while one was open for 2% -> 3% of each run, Pallas kernels for 2% -> 16%
where the time goes in v1:
time: 176 us; the launch traced here: 175 us
  waiting for transfers between devices  87.7 us (50%)
  starting transfers between devices  40.4 us (23%)
  Pallas kernels  35.5 us (20%)
  local copies, waits for them, and re-layouts  5.78 us (3%)
  other arithmetic  5.56 us (3%)
    ppermute x23, waiting for transfers between devices, torus_shift(): return lax.ppermute(x, ('seq', 'wt'), pairs)  70.4 us
    ppermute x23, starting transfers between devices, torus_shift(): return lax.ppermute(x, ('seq', 'wt'), pairs)  32.4 us
    pallas_call x2, Pallas kernels, ffn(): pl.pallas_call(functools.partial(ffn_kernel, t), out_shape=[jax.ShapeDtyp...  23.9 us
    ppermute x4, waiting for transfers between devices, later(): lax.ppermute(x, 'seq', [(s, s + 2 * places) for s in range(SEQ) if s + 2...  14.4 us
    ppermute x4, starting transfers between devices, later(): lax.ppermute(x, 'seq', [(s, s + 2 * places) for s in range(SEQ) if s + 2...  7.26 us
    pallas_call x1, Pallas kernels, per_device(): pl.pallas_call(intra_kernel, out_shape=jax.ShapeDtypeStruct((4, 512, HEAD...  4.06 us
  transfers between devices with their start and end apart: 31, of which 16 were waited for; matrix products, arithmetic and copies ran while one was open for 3% of the time, Pallas kernels for 16%

profile of v1, /device:TPU:184, one launch (start us, length us, event | category | flops | bytes accessed | tf_op | source)
XLA Modules:
  0.0 175.2 jit_solution(7464637510342022940)
XLA Ops:
  0.0 2.4 %states.1 = bf16[4,128,128]{2,1,0:T(8,128)(2,1)} custom-call(bf16[512,512]{1,0:T(8,128)(2,1)} %k_ref.3, bf16[512,512]{1,0:T(8,128)(2,1)} %v_ref.3), custom_call_target="tpu_custom_call" | custom-call | tf_op jit(solution)/shard_map/states/pallas_call | solution.py:228
  2.4 1.6 collective-permute-done
  3.9 0.9 convert_add_fusion.2
  4.9 3.4 %collective-permute-start.2 = (bf16[2,128,128]{2,1,0:T(8,128)(2,1)S(1)}, bf16[2,128,128]{2,1,0:T(8,128)(2,1)S(1)}, u32[]{:S(2)}, u32[]{:S(2)}) collective-permute-start(bf16[2,128,128]{2,1,0:T(8,128)(2,1)S(1)} %fusion.17), channel_id=1, source_target_pairs={{0,64},{16,80},{32,96},{48,112},{64,128},{80,144},{96,160},{112,17... | collective-permute-start | bytes 196616 | tf_op jit(solution)/shard_map/ppermute | solution.py:215
  8.3 1.9 %collective-permute-start.1 = (bf16[2,128,128]{2,1,0:T(8,128)(2,1)S(1)}, bf16[2,128,128]{2,1,0:T(8,128)(2,1)S(1)}, u32[]{:S(2)}, u32[]{:S(2)}) collective-permute-start(bf16[2,128,128]{2,1,0:T(8,128)(2,1)S(1)} %fusion.17), channel_id=1, source_target_pairs={{0,32},{16,48},{32,64},{48,80},{64,96},{80,112},{96,128},{112,144}... | collective-permute-start | bytes 196616 | tf_op jit(solution)/shard_map/ppermute | solution.py:215
  10.2 4.5 %collective-permute-done.2 = bf16[2,128,128]{2,1,0:T(8,128)(2,1)S(1)} collective-permute-done((bf16[2,128,128]{2,1,0:T(8,128)(2,1)S(1)}, bf16[2,128,128]{2,1,0:T(8,128)(2,1)S(1)}, u32[]{:S(2)}, u32[]{:S(2)}) %collective-permute-start.2) | collective-permute-done | bytes 65568 | tf_op jit(solution)/shard_map/ppermute | solution.py:215
  14.8 0.7 collective-permute-start.4
  15.4 1.3 collective-permute-start.3
  16.7 9.9 %collective-permute-done.3 = bf16[2,128,128]{2,1,0:T(8,128)(2,1)S(1)} collective-permute-done((bf16[2,128,128]{2,1,0:T(8,128)(2,1)S(1)}, bf16[2,128,128]{2,1,0:T(8,128)(2,1)S(1)}, u32[]{:S(2)}, u32[]{:S(2)}) %collective-permute-start.3) | collective-permute-done | bytes 65568 | tf_op jit(solution)/shard_map/ppermute | solution.py:215
  26.6 0.1 collective-permute-start.5
  26.7 4.1 %within_block.1.intra_ref = f32[4,512,128]{2,1,0:T(8,128)} custom-call(bf16[512,512]{1,0:T(8,128)(2,1)} %q_ref.3, bf16[512,512]{1,0:T(8,128)(2,1)} %k_ref.3, bf16[512,512]{1,0:T(8,128)(2,1)} %v_ref.3), custom_call_target="tpu_custom_call" | custom-call | flops 1073741824 | bytes 3145728 | tf_op jit(solution)/shard_map/within_block/pallas_call | solution.py:235
  30.8 0.7 fusion.8.state_ref
  31.6 3.2 %mid.1 = (bf16[4,256,128]{2,1,0:T(8,128)(2,1)}, bf16[4,256,128]{2,1,0:T(8,128)(2,1)}) custom-call(s32[1]{0:T(128)} %bitcast.core_ref, bf16[512,512]{1,0:T(8,128)(2,1)} %q_ref.3, f32[4,128,128]{2,1,0:T(8,128)} %fusion.8.state_ref, f32[4,512,128]{2,1,0:T(8,128)} %within_block.1.intra_ref, bf16[512,512]{1,0:T(8,128)(2,1)} %stream_ref.1, f32[1,512]{1,0:T(1,128)} %bitcast.35), custom_call_target="tpu_custom_call" | custom-call | tf_op jit(solution)/shard_map/mid/pallas_call | solution.py:247
  34.8 0.5 collective-permute-start.6
  35.3 1.4 collective-permute-done.6
  36.6 1.1 pad_maximum_fusion.2
  37.7 1.6 collective-permute-start.7
  39.3 1.8 collective-permute-start.9
  41.0 1.8 %collective-permute-start.8 = (bf16[2,4,256,128]{3,2,1,0:T(8,128)(2,1)S(1)}, bf16[2,4,256,128]{3,2,1,0:T(8,128)(2,1)S(1)}, u32[]{:S(2)}, u32[]{:S(2)}) collective-permute-start(bf16[2,4,256,128]{3,2,1,0:T(8,128)(2,1)S(1)} %pad_maximum_fusion.2), channel_id=1, source_target_pairs={{0,8},{1,9},{2,10},{3,11},{4,12},{5,13},{6,14},{7,15},{8,0},{9,1},... | collective-permute-start | bytes 1572872 | tf_op jit(solution)/shard_map/ppermute | solution.py:180
  42.9 5.3 %collective-permute-done.7 = bf16[2,4,256,128]{3,2,1,0:T(8,128)(2,1)S(1)} collective-permute-done((bf16[2,4,256,128]{3,2,1,0:T(8,128)(2,1)S(1)}, bf16[2,4,256,128]{3,2,1,0:T(8,128)(2,1)S(1)}, u32[]{:S(2)}, u32[]{:S(2)}) %collective-permute-start.7) | collective-permute-done | bytes 524320 | tf_op jit(solution)/shard_map/ppermute | solution.py:180
  48.3 0.1 pad_maximum_fusion.refs_0_
  48.4 0.3 collective-permute-start.10
  48.7 4.7 %collective-permute-done.9 = bf16[2,4,256,128]{3,2,1,0:T(8,128)(2,1)S(1)} collective-permute-done((bf16[2,4,256,128]{3,2,1,0:T(8,128)(2,1)S(1)}, bf16[2,4,256,128]{3,2,1,0:T(8,128)(2,1)S(1)}, u32[]{:S(2)}, u32[]{:S(2)}) %collective-permute-start.9) | collective-permute-done | bytes 524320 | tf_op jit(solution)/shard_map/ppermute | solution.py:180
  53.4 4.5 %collective-permute-done.8 = bf16[2,4,256,128]{3,2,1,0:T(8,128)(2,1)S(1)} collective-permute-done((bf16[2,4,256,128]{3,2,1,0:T(8,128)(2,1)S(1)}, bf16[2,4,256,128]{3,2,1,0:T(8,128)(2,1)S(1)}, u32[]{:S(2)}, u32[]{:S(2)}) %collective-permute-start.8) | collective-permute-done | bytes 524320 | tf_op jit(solution)/shard_map/ppermute | solution.py:180
  58.0 0.1 pad_maximum_fusion.1.refs_1_
  58.3 1.2 collective-permute-start.12
  59.5 2.1 %collective-permute-start.11 = (bf16[4,4,256,128]{3,2,1,0:T(8,128)(2,1)S(1)}, bf16[4,4,256,128]{3,2,1,0:T(8,128)(2,1)}, u32[]{:S(2)}, u32[]{:S(2)}) collective-permute-start(bf16[4,4,256,128]{3,2,1,0:T(8,128)(2,1)S(1)} %pad_maximum_fusion.1.refs_1_), channel_id=1, source_target_pairs={{0,1},{1,2},{2,3},{3,0},{4,5},{5,6},{6,7},{7,4},{8,9},{9,10},{10,1... | collective-permute-start | bytes 3145736 | tf_op jit(solution)/shard_map/ppermute | solution.py:180
  61.6 1.7 collective-permute-done.10.refs_2_
  63.3 1.0 fusion.29
  64.3 2.6 %collective-permute-start.14 = (bf16[2,4,256,128]{3,2,1,0:T(8,128)(2,1)}, bf16[2,4,256,128]{3,2,1,0:T(8,128)(2,1)}, u32[]{:S(2)}, u32[]{:S(2)}) collective-permute-start(bf16[2,4,256,128]{3,2,1,0:T(8,128)(2,1)} %get-tuple-element.47), channel_id=1, source_target_pairs={{0,1},{1,2},{2,3},{3,0},{4,5},{5,6},{6,7},{7,4},{8,9},{9,10},{10,1... | collective-permute-start | bytes 1572872 | tf_op jit(solution)/shard_map/ppermute | solution.py:180
  67.0 7.3 %collective-permute-done.13.refs_5_ = bf16[4,4,256,128]{3,2,1,0:T(8,128)(2,1)S(1)} collective-permute-done((bf16[4,4,256,128]{3,2,1,0:T(8,128)(2,1)S(1)}, bf16[4,4,256,128]{3,2,1,0:T(8,128)(2,1)S(1)}, u32[]{:S(2)}, u32[]{:S(2)}) %collective-permute-start.13) | collective-permute-done | bytes 1048608 | tf_op jit(solution)/shard_map/ppermute | solution.py:180
  74.3 1.1 fusion.28
  75.3 1.0 copy-done
  76.3 0.7 gather_fusion
  77.0 3.3 %collective-permute-start.18 = (bf16[2,4,256,128]{3,2,1,0:T(8,128)(2,1)}, bf16[2,4,256,128]{3,2,1,0:T(8,128)(2,1)S(1)}, u32[]{:S(2)}, u32[]{:S(2)}) collective-permute-start(bf16[2,4,256,128]{3,2,1,0:T(8,128)(2,1)} %get-tuple-element.48), channel_id=1, source_target_pairs={{0,1},{1,2},{2,3},{3,0},{4,5},{5,6},{6,7},{7,4},{8,9},{9,10},{10,1... | collective-permute-start | bytes 1572872 | tf_op jit(solution)/shard_map/ppermute | solution.py:180
  80.3 5.3 %collective-permute-done.12.refs_4_ = bf16[4,4,256,128]{3,2,1,0:T(8,128)(2,1)} collective-permute-done((bf16[4,4,256,128]{3,2,1,0:T(8,128)(2,1)S(1)}, bf16[4,4,256,128]{3,2,1,0:T(8,128)(2,1)}, u32[]{:S(2)}, u32[]{:S(2)}) %collective-permute-start.12) | collective-permute-done | bytes 1048608 | tf_op jit(solution)/shard_map/ppermute | solution.py:180
  85.7 5.6 %collective-permute-done.15.refs_7_ = bf16[2,4,256,128]{3,2,1,0:T(8,128)(2,1)} collective-permute-done((bf16[2,4,256,128]{3,2,1,0:T(8,128)(2,1)}, bf16[2,4,256,128]{3,2,1,0:T(8,128)(2,1)}, u32[]{:S(2)}, u32[]{:S(2)}) %collective-permute-start.15) | collective-permute-done | bytes 524320 | tf_op jit(solution)/shard_map/ppermute | solution.py:180
  91.3 1.2 copy-done.1
  92.5 12.7 %feed_forward.2 = (bf16[4,4,256,128]{3,2,1,0:T(8,128)(2,1)S(1)}, bf16[4,4,256,128]{3,2,1,0:T(8,128)(2,1)S(1)}, bf16[4,4,256,128]{3,2,1,0:T(8,128)(2,1)S(1)}, bf16[4,4,256,128]{3,2,1,0:T(8,128)(2,1)S(1)}) custom-call(s32[16]{0:T(128)S(1)} %get-tuple-element.56.places_in, s32[16]{0:T(128)S(1)} %get-tuple-element.55.places_out, s32[8,16]{1,0:T(8,128)S(1)} %copy-done.3, ...), custom_call_target="tpu_custom_call" | custom-call | flops 2147483648 | bytes 17825792 | tf_op jit(solution)/shard_map/feed_forward/pallas_call | solution.py:140
  105.1 0.1 collective-permute-start.16
  105.2 2.0 %collective-permute-start.17 = (bf16[4,4,256,128]{3,2,1,0:T(8,128)(2,1)S(1)}, bf16[4,4,256,128]{3,2,1,0:T(8,128)(2,1)S(1)}, u32[]{:S(2)}, u32[]{:S(2)}) collective-permute-start(bf16[4,4,256,128]{3,2,1,0:T(8,128)(2,1)S(1)} %get-tuple-element.24), channel_id=1, source_target_pairs={{0,3},{1,0},{2,1},{3,2},{4,7},{5,4},{6,5},{7,6},{8,11},{9,8},{10,9... | collective-permute-start | bytes 3145736 | tf_op jit(solution)/shard_map/ppermute | solution.py:180
  107.3 11.3 %feed_forward.3 = (bf16[4,4,256,128]{3,2,1,0:T(8,128)(2,1)S(1)}, bf16[4,4,256,128]{3,2,1,0:T(8,128)(2,1)S(1)}, bf16[4,4,256,128]{3,2,1,0:T(8,128)(2,1)S(1)}, bf16[4,4,256,128]{3,2,1,0:T(8,128)(2,1)S(1)}) custom-call(s32[16]{0:T(128)S(1)} %get-tuple-element.56.places_in, s32[16]{0:T(128)S(1)} %get-tuple-element.55.places_out, s32[8,16]{1,0:T(8,128)S(1)} %copy-done.3, ...), custom_call_target="tpu_custom_call" | custom-call | flops 2147483648 | bytes 17825792 | tf_op jit(solution)/shard_map/feed_forward/pallas_call | solution.py:140
  118.5 0.1 collective-permute-start.20
  118.6 3.2 %collective-permute-start.22 = (bf16[4,4,256,128]{3,2,1,0:T(8,128)(2,1)S(1)}, bf16[4,4,256,128]{3,2,1,0:T(8,128)(2,1)S(1)}, u32[]{:S(2)}, u32[]{:S(2)}) collective-permute-start(bf16[4,4,256,128]{3,2,1,0:T(8,128)(2,1)S(1)} %get-tuple-element.32), channel_id=1, source_target_pairs={{0,1},{1,2},{2,3},{3,0},{4,5},{5,6},{6,7},{7,4},{8,9},{9,10},{10,1... | collective-permute-start | bytes 3145736 | tf_op jit(solution)/shard_map/ppermute | solution.py:180
  121.9 0.3 add_convert_fusion
  122.1 0.2 collective-permute-start.26
  122.3 12.3 %collective-permute-done.20 = bf16[4,4,256,128]{3,2,1,0:T(8,128)(2,1)S(1)} collective-permute-done((bf16[4,4,256,128]{3,2,1,0:T(8,128)(2,1)S(1)}, bf16[4,4,256,128]{3,2,1,0:T(8,128)(2,1)S(1)}, u32[]{:S(2)}, u32[]{:S(2)}) %collective-permute-start.20) | collective-permute-done | bytes 1048608 | tf_op jit(solution)/shard_map/ppermute | solution.py:180
  134.6 0.3 add_convert_fusion.1
  134.9 0.1 collective-permute-start.21
  135.0 11.5 %collective-permute-done.26 = bf16[4,4,256,128]{3,2,1,0:T(8,128)(2,1)S(1)} collective-permute-done((bf16[4,4,256,128]{3,2,1,0:T(8,128)(2,1)S(1)}, bf16[4,4,256,128]{3,2,1,0:T(8,128)(2,1)S(1)}, u32[]{:S(2)}, u32[]{:S(2)}) %collective-permute-start.26) | collective-permute-done | bytes 1048608 | tf_op jit(solution)/shard_map/ppermute | solution.py:180
  146.5 0.3 fusion.14
  147.0 4.9 %collective-permute-start.29 = (bf16[4,256,128]{2,1,0:T(8,128)(2,1)S(1)}, bf16[4,256,128]{2,1,0:T(8,128)(2,1)S(1)}, u32[]{:S(2)}, u32[]{:S(2)}) collective-permute-start(bf16[4,256,128]{2,1,0:T(8,128)(2,1)S(1)} %get-tuple-element.40), channel_id=1, source_target_pairs={{0,8},{1,9},{2,10},{3,11},{4,12},{5,13},{6,14},{7,15},{8,0},{9,1},... | collective-permute-start | bytes 786440 | tf_op jit(solution)/shard_map/ppermute | solution.py:180
  151.8 2.5 %collective-permute-start.28 = (bf16[4,256,128]{2,1,0:T(8,128)(2,1)S(1)}, bf16[4,256,128]{2,1,0:T(8,128)(2,1)S(1)}, u32[]{:S(2)}, u32[]{:S(2)}) collective-permute-start(bf16[4,256,128]{2,1,0:T(8,128)(2,1)S(1)} %get-tuple-element.41), channel_id=1, source_target_pairs={{0,12},{1,13},{2,14},{3,15},{4,0},{5,1},{6,2},{7,3},{8,4},{9,5},{1... | collective-permute-start | bytes 786440 | tf_op jit(solution)/shard_map/ppermute | solution.py:180
  154.4 5.6 %collective-permute-done.21 = bf16[4,4,256,128]{3,2,1,0:T(8,128)(2,1)S(1)} collective-permute-done((bf16[4,4,256,128]{3,2,1,0:T(8,128)(2,1)S(1)}, bf16[4,4,256,128]{3,2,1,0:T(8,128)(2,1)S(1)}, u32[]{:S(2)}, u32[]{:S(2)}) %collective-permute-start.21) | collective-permute-done | bytes 1048608 | tf_op jit(solution)/shard_map/ppermute | solution.py:180
  159.9 0.3 fusion.10
  160.3 1.9 %collective-permute-start.25 = (bf16[4,256,128]{2,1,0:T(8,128)(2,1)S(1)}, bf16[4,256,128]{2,1,0:T(8,128)(2,1)S(1)}, u32[]{:S(2)}, u32[]{:S(2)}) collective-permute-start(bf16[4,256,128]{2,1,0:T(8,128)(2,1)S(1)} %get-tuple-element.43), channel_id=1, source_target_pairs={{0,8},{1,9},{2,10},{3,11},{4,12},{5,13},{6,14},{7,15},{8,0},{9,1},... | collective-permute-start | bytes 786440 | tf_op jit(solution)/shard_map/ppermute | solution.py:180
  162.2 2.5 %collective-permute-start.24 = (bf16[4,256,128]{2,1,0:T(8,128)(2,1)S(1)}, bf16[4,256,128]{2,1,0:T(8,128)(2,1)S(1)}, u32[]{:S(2)}, u32[]{:S(2)}) collective-permute-start(bf16[4,256,128]{2,1,0:T(8,128)(2,1)S(1)} %get-tuple-element.44), channel_id=1, source_target_pairs={{0,12},{1,13},{2,14},{3,15},{4,0},{5,1},{6,2},{7,3},{8,4},{9,5},{1... | collective-permute-start | bytes 786440 | tf_op jit(solution)/shard_map/ppermute | solution.py:180
  164.8 0.2 fusion.3
  165.0 0.1 collective-permute-start.30
  165.1 5.6 %collective-permute-done.23 = bf16[4,256,128]{2,1,0:T(8,128)(2,1)S(1)} collective-permute-done((bf16[4,256,128]{2,1,0:T(8,128)(2,1)S(1)}, bf16[4,256,128]{2,1,0:T(8,128)(2,1)S(1)}, u32[]{:S(2)}, u32[]{:S(2)}) %collective-permute-start.23) | collective-permute-done | bytes 262176 | tf_op jit(solution)/shard_map/ppermute | solution.py:180
  170.7 0.9 collective-permute-done.24
  171.6 1.0 fusion.7.mine_ref
  172.6 0.7 copy-done.9
  173.3 1.9 %result.1 = bf16[512,512]{1,0:T(8,128)(2,1)} custom-call(s32[1]{0:T(128)} %bitcast.core_ref, bf16[4,256,128]{2,1,0:T(8,128)(2,1)} %fusion.7.mine_ref, bf16[4,256,128]{2,1,0:T(8,128)(2,1)} %copy-done.9), custom_call_target="tpu_custom_call" | custom-call | tf_op jit(solution)/shard_map/result/pallas_call | solution.py:290
  (48 shorter events, 0.6 us)
Async XLA Ops:
  2.4 1.6 collective-permute-start
  4.9 9.8 %collective-permute-start.2 = (bf16[2,128,128]{2,1,0:T(8,128)(2,1)S(1)}, bf16[2,128,128]{2,1,0:T(8,128)(2,1)S(1)}, u32[]{:S(2)}, u32[]{:S(2)}) collective-permute-start(bf16[2,128,128]{2,1,0:T(8,128)(2,1)S(1)} %fusion.17), channel_id=1, source_target_pairs={{0,64},{16,80},{32,96},{48,112},{64,128},{80,144},{96,160},{112,17... | collective-permute-start | bytes 196616 | tf_op jit(solution)/shard_map/ppermute | solution.py:215
  8.3 6.4 %collective-permute-start.1 = (bf16[2,128,128]{2,1,0:T(8,128)(2,1)S(1)}, bf16[2,128,128]{2,1,0:T(8,128)(2,1)S(1)}, u32[]{:S(2)}, u32[]{:S(2)}) collective-permute-start(bf16[2,128,128]{2,1,0:T(8,128)(2,1)S(1)} %fusion.17), channel_id=1, source_target_pairs={{0,32},{16,48},{32,64},{48,80},{64,96},{80,112},{96,128},{112,144}... | collective-permute-start | bytes 196616 | tf_op jit(solution)/shard_map/ppermute | solution.py:215
  14.8 2.0 %collective-permute-start.4 = (bf16[2,128,128]{2,1,0:T(8,128)(2,1)S(1)}, bf16[2,128,128]{2,1,0:T(8,128)(2,1)S(1)}, u32[]{:S(2)}, u32[]{:S(2)}) collective-permute-start(bf16[2,128,128]{2,1,0:T(8,128)(2,1)S(1)} %add_convert_fusion.10), channel_id=1, source_target_pairs={{0,192},{16,208},{32,224},{48,240},{1,193},{17,209},{33,225},{49,2... | collective-permute-start | bytes 196616 | tf_op jit(solution)/shard_map/ppermute | solution.py:215
  15.4 11.2 %collective-permute-start.3 = (bf16[2,128,128]{2,1,0:T(8,128)(2,1)S(1)}, bf16[2,128,128]{2,1,0:T(8,128)(2,1)S(1)}, u32[]{:S(2)}, u32[]{:S(2)}) collective-permute-start(bf16[2,128,128]{2,1,0:T(8,128)(2,1)S(1)} %add_convert_fusion.10), channel_id=1, source_target_pairs={{0,96},{16,112},{32,128},{48,144},{64,160},{80,176},{96,192},{112,... | collective-permute-start | bytes 196616 | tf_op jit(solution)/shard_map/ppermute | solution.py:215
  26.6 4.2 %collective-permute-start.5 = (bf16[2,128,128]{2,1,0:T(8,128)(2,1)S(1)}, bf16[2,128,128]{2,1,0:T(8,128)(2,1)S(1)}, u32[]{:S(2)}, u32[]{:S(2)}) collective-permute-start(bf16[2,128,128]{2,1,0:T(8,128)(2,1)S(1)} %get-tuple-element.37), channel_id=1, source_target_pairs={{0,16},{16,0},{32,48},{48,32},{64,80},{80,64},{96,112},{112,96},{1... | collective-permute-start | bytes 196616 | tf_op jit(solution)/shard_map/ppermute | solution.py:184
  34.8 13.5 %copy-start.6 = (bf16[4,256,128]{2,1,0:T(8,128)(2,1)S(1)}, bf16[4,256,128]{2,1,0:T(8,128)(2,1)}, u32[]{:S(2)}) copy-start(bf16[4,256,128]{2,1,0:T(8,128)(2,1)} %get-tuple-element.21) | copy-start | bytes 786436
  34.8 1.9 %collective-permute-start.6 = (bf16[4,256,128]{2,1,0:T(8,128)(2,1)}, bf16[4,256,128]{2,1,0:T(8,128)(2,1)S(1)}, u32[]{:S(2)}, u32[]{:S(2)}) collective-permute-start(bf16[4,256,128]{2,1,0:T(8,128)(2,1)} %get-tuple-element.22), channel_id=1, source_target_pairs={{0,16},{16,0},{32,48},{48,32},{64,80},{80,64},{96,112},{112,96},{1... | collective-permute-start | bytes 786440 | tf_op jit(solution)/shard_map/ppermute | solution.py:184
  36.6 11.6 %copy-start.7 = (bf16[4,256,128]{2,1,0:T(8,128)(2,1)}, bf16[4,256,128]{2,1,0:T(8,128)(2,1)S(1)}, u32[]{:S(2)}) copy-start(bf16[4,256,128]{2,1,0:T(8,128)(2,1)S(1)} %collective-permute-done.6) | copy-start | bytes 786436
  37.7 10.5 %collective-permute-start.7 = (bf16[2,4,256,128]{3,2,1,0:T(8,128)(2,1)S(1)}, bf16[2,4,256,128]{3,2,1,0:T(8,128)(2,1)S(1)}, u32[]{:S(2)}, u32[]{:S(2)}) collective-permute-start(bf16[2,4,256,128]{3,2,1,0:T(8,128)(2,1)S(1)} %pad_maximum_fusion.2), channel_id=1, source_target_pairs={{0,4},{1,5},{2,6},{3,7},{4,8},{5,9},{6,10},{7,11},{8,12},{9,13},{1... | collective-permute-start | bytes 1572872 | tf_op jit(solution)/shard_map/ppermute | solution.py:180
  39.3 14.1 %collective-permute-start.9 = (bf16[2,4,256,128]{3,2,1,0:T(8,128)(2,1)S(1)}, bf16[2,4,256,128]{3,2,1,0:T(8,128)(2,1)S(1)}, u32[]{:S(2)}, u32[]{:S(2)}) collective-permute-start(bf16[2,4,256,128]{3,2,1,0:T(8,128)(2,1)S(1)} %pad_maximum_fusion.2), channel_id=1, source_target_pairs={{0,12},{1,13},{2,14},{3,15},{4,0},{5,1},{6,2},{7,3},{8,4},{9,5},{1... | collective-permute-start | bytes 1572872 | tf_op jit(solution)/shard_map/ppermute | solution.py:180
  41.0 16.9 %collective-permute-start.8 = (bf16[2,4,256,128]{3,2,1,0:T(8,128)(2,1)S(1)}, bf16[2,4,256,128]{3,2,1,0:T(8,128)(2,1)S(1)}, u32[]{:S(2)}, u32[]{:S(2)}) collective-permute-start(bf16[2,4,256,128]{3,2,1,0:T(8,128)(2,1)S(1)} %pad_maximum_fusion.2), channel_id=1, source_target_pairs={{0,8},{1,9},{2,10},{3,11},{4,12},{5,13},{6,14},{7,15},{8,0},{9,1},... | collective-permute-start | bytes 1572872 | tf_op jit(solution)/shard_map/ppermute | solution.py:180
  48.4 14.9 %collective-permute-start.10 = (bf16[4,4,256,128]{3,2,1,0:T(8,128)(2,1)S(1)}, bf16[4,4,256,128]{3,2,1,0:T(8,128)(2,1)S(1)}, u32[]{:S(2)}, u32[]{:S(2)}) collective-permute-start(bf16[4,4,256,128]{3,2,1,0:T(8,128)(2,1)S(1)} %pad_maximum_fusion.refs_0_), channel_id=1, source_target_pairs={{0,1},{1,2},{2,3},{3,0},{4,5},{5,6},{6,7},{7,4},{8,9},{9,10},{10,1... | collective-permute-start | bytes 3145736 | tf_op jit(solution)/shard_map/ppermute | solution.py:180
  58.1 18.2 %copy-start.5 = (s32[4]{0:T(128)S(1)}, s32[4]{0:T(128)}, u32[]{:S(2)}) copy-start(s32[4]{0:T(128)} %constant.91.clone) | copy-start | bytes 52
  58.2 33.1 %copy-start.2 = (f32[8192]{0:T(1024)S(1)}, f32[8192]{0:T(1024)}, u32[]{:S(2)}) copy-start(f32[8192]{0:T(1024)} %param.16) | copy-start | bytes 98308
  58.2 33.1 %copy-start.3 = (s32[8,16]{1,0:T(8,128)S(1)}, s32[8,16]{1,0:T(8,128)}, u32[]{:S(2)}) copy-start(s32[8,16]{1,0:T(8,128)} %up_index.3) | copy-start | bytes 1540
  58.2 33.1 %copy-start.4 = (s32[8,16]{1,0:T(8,128)S(1)}, s32[8,16]{1,0:T(8,128)}, u32[]{:S(2)}) copy-start(s32[8,16]{1,0:T(8,128)} %down_index.3) | copy-start | bytes 1540
  58.2 16.1 %collective-permute-start.13 = (bf16[4,4,256,128]{3,2,1,0:T(8,128)(2,1)S(1)}, bf16[4,4,256,128]{3,2,1,0:T(8,128)(2,1)S(1)}, u32[]{:S(2)}, u32[]{:S(2)}) collective-permute-start(bf16[4,4,256,128]{3,2,1,0:T(8,128)(2,1)S(1)} %pad_maximum_fusion.1.refs_1_), channel_id=1, source_target_pairs={{0,3},{1,0},{2,1},{3,2},{4,7},{5,4},{6,5},{7,6},{8,11},{9,8},{10,9... | collective-permute-start | bytes 3145736 | tf_op jit(solution)/shard_map/ppermute | solution.py:180
  58.3 27.3 %collective-permute-start.12 = (bf16[4,4,256,128]{3,2,1,0:T(8,128)(2,1)S(1)}, bf16[4,4,256,128]{3,2,1,0:T(8,128)(2,1)}, u32[]{:S(2)}, u32[]{:S(2)}) collective-permute-start(bf16[4,4,256,128]{3,2,1,0:T(8,128)(2,1)S(1)} %pad_maximum_fusion.refs_0_), channel_id=1, source_target_pairs={{0,3},{1,0},{2,1},{3,2},{4,7},{5,4},{6,5},{7,6},{8,11},{9,8},{10,9... | collective-permute-start | bytes 3145736 | tf_op jit(solution)/shard_map/ppermute | solution.py:180
  59.5 26.2 %collective-permute-start.11 = (bf16[4,4,256,128]{3,2,1,0:T(8,128)(2,1)S(1)}, bf16[4,4,256,128]{3,2,1,0:T(8,128)(2,1)}, u32[]{:S(2)}, u32[]{:S(2)}) collective-permute-start(bf16[4,4,256,128]{3,2,1,0:T(8,128)(2,1)S(1)} %pad_maximum_fusion.1.refs_1_), channel_id=1, source_target_pairs={{0,1},{1,2},{2,3},{3,0},{4,5},{5,6},{6,7},{7,4},{8,9},{9,10},{10,1... | collective-permute-start | bytes 3145736 | tf_op jit(solution)/shard_map/ppermute | solution.py:180
  64.3 21.3 %collective-permute-start.14 = (bf16[2,4,256,128]{3,2,1,0:T(8,128)(2,1)}, bf16[2,4,256,128]{3,2,1,0:T(8,128)(2,1)}, u32[]{:S(2)}, u32[]{:S(2)}) collective-permute-start(bf16[2,4,256,128]{3,2,1,0:T(8,128)(2,1)} %get-tuple-element.47), channel_id=1, source_target_pairs={{0,1},{1,2},{2,3},{3,0},{4,5},{5,6},{6,7},{7,4},{8,9},{9,10},{10,1... | collective-permute-start | bytes 1572872 | tf_op jit(solution)/shard_map/ppermute | solution.py:180
  75.3 1.0 copy-start
  76.3 14.9 %collective-permute-start.15 = (bf16[2,4,256,128]{3,2,1,0:T(8,128)(2,1)}, bf16[2,4,256,128]{3,2,1,0:T(8,128)(2,1)}, u32[]{:S(2)}, u32[]{:S(2)}) collective-permute-start(bf16[2,4,256,128]{3,2,1,0:T(8,128)(2,1)} %get-tuple-element.45), channel_id=1, source_target_pairs={{0,3},{1,0},{2,1},{3,2},{4,7},{5,4},{6,5},{7,6},{8,11},{9,8},{10,9... | collective-permute-start | bytes 1572872 | tf_op jit(solution)/shard_map/ppermute | solution.py:180
  77.0 30.2 %collective-permute-start.18 = (bf16[2,4,256,128]{3,2,1,0:T(8,128)(2,1)}, bf16[2,4,256,128]{3,2,1,0:T(8,128)(2,1)S(1)}, u32[]{:S(2)}, u32[]{:S(2)}) collective-permute-start(bf16[2,4,256,128]{3,2,1,0:T(8,128)(2,1)} %get-tuple-element.48), channel_id=1, source_target_pairs={{0,1},{1,2},{2,3},{3,0},{4,5},{5,6},{6,7},{7,4},{8,9},{9,10},{10,1... | collective-permute-start | bytes 1572872 | tf_op jit(solution)/shard_map/ppermute | solution.py:180
  85.6 21.6 %collective-permute-start.19 = (bf16[2,4,256,128]{3,2,1,0:T(8,128)(2,1)}, bf16[2,4,256,128]{3,2,1,0:T(8,128)(2,1)S(1)}, u32[]{:S(2)}, u32[]{:S(2)}) collective-permute-start(bf16[2,4,256,128]{3,2,1,0:T(8,128)(2,1)} %get-tuple-element.46), channel_id=1, source_target_pairs={{0,3},{1,0},{2,1},{3,2},{4,7},{5,4},{6,5},{7,6},{8,11},{9,8},{10,9... | collective-permute-start | bytes 1572872 | tf_op jit(solution)/shard_map/ppermute | solution.py:180
  91.2 1.2 copy-start.1
  105.1 16.7 %collective-permute-start.16 = (bf16[4,4,256,128]{3,2,1,0:T(8,128)(2,1)S(1)}, bf16[4,4,256,128]{3,2,1,0:T(8,128)(2,1)S(1)}, u32[]{:S(2)}, u32[]{:S(2)}) collective-permute-start(bf16[4,4,256,128]{3,2,1,0:T(8,128)(2,1)S(1)} %get-tuple-element.23), channel_id=1, source_target_pairs={{0,1},{1,2},{2,3},{3,0},{4,5},{5,6},{6,7},{7,4},{8,9},{9,10},{10,1... | collective-permute-start | bytes 3145736 | tf_op jit(solution)/shard_map/ppermute | solution.py:180
  105.2 16.6 %collective-permute-start.17 = (bf16[4,4,256,128]{3,2,1,0:T(8,128)(2,1)S(1)}, bf16[4,4,256,128]{3,2,1,0:T(8,128)(2,1)S(1)}, u32[]{:S(2)}, u32[]{:S(2)}) collective-permute-start(bf16[4,4,256,128]{3,2,1,0:T(8,128)(2,1)S(1)} %get-tuple-element.24), channel_id=1, source_target_pairs={{0,3},{1,0},{2,1},{3,2},{4,7},{5,4},{6,5},{7,6},{8,11},{9,8},{10,9... | collective-permute-start | bytes 3145736 | tf_op jit(solution)/shard_map/ppermute | solution.py:180
  118.5 16.1 %collective-permute-start.20 = (bf16[4,4,256,128]{3,2,1,0:T(8,128)(2,1)S(1)}, bf16[4,4,256,128]{3,2,1,0:T(8,128)(2,1)S(1)}, u32[]{:S(2)}, u32[]{:S(2)}) collective-permute-start(bf16[4,4,256,128]{3,2,1,0:T(8,128)(2,1)S(1)} %get-tuple-element.31), channel_id=1, source_target_pairs={{0,3},{1,0},{2,1},{3,2},{4,7},{5,4},{6,5},{7,6},{8,11},{9,8},{10,9... | collective-permute-start | bytes 3145736 | tf_op jit(solution)/shard_map/ppermute | solution.py:180
  118.6 35.7 %collective-permute-start.22 = (bf16[4,4,256,128]{3,2,1,0:T(8,128)(2,1)S(1)}, bf16[4,4,256,128]{3,2,1,0:T(8,128)(2,1)S(1)}, u32[]{:S(2)}, u32[]{:S(2)}) collective-permute-start(bf16[4,4,256,128]{3,2,1,0:T(8,128)(2,1)S(1)} %get-tuple-element.32), channel_id=1, source_target_pairs={{0,1},{1,2},{2,3},{3,0},{4,5},{5,6},{6,7},{7,4},{8,9},{9,10},{10,1... | collective-permute-start | bytes 3145736 | tf_op jit(solution)/shard_map/ppermute | solution.py:180
  122.1 24.4 %collective-permute-start.26 = (bf16[4,4,256,128]{3,2,1,0:T(8,128)(2,1)S(1)}, bf16[4,4,256,128]{3,2,1,0:T(8,128)(2,1)S(1)}, u32[]{:S(2)}, u32[]{:S(2)}) collective-permute-start(bf16[4,4,256,128]{3,2,1,0:T(8,128)(2,1)S(1)} %add_convert_fusion), channel_id=1, source_target_pairs={{0,1},{1,2},{2,3},{3,0},{4,5},{5,6},{6,7},{7,4},{8,9},{9,10},{10,1... | collective-permute-start | bytes 3145736 | tf_op jit(solution)/shard_map/ppermute | solution.py:180
  134.9 25.0 %collective-permute-start.21 = (bf16[4,4,256,128]{3,2,1,0:T(8,128)(2,1)S(1)}, bf16[4,4,256,128]{3,2,1,0:T(8,128)(2,1)S(1)}, u32[]{:S(2)}, u32[]{:S(2)}) collective-permute-start(bf16[4,4,256,128]{3,2,1,0:T(8,128)(2,1)S(1)} %add_convert_fusion.1), channel_id=1, source_target_pairs={{0,3},{1,0},{2,1},{3,2},{4,7},{5,4},{6,5},{7,6},{8,11},{9,8},{10,9... | collective-permute-start | bytes 3145736 | tf_op jit(solution)/shard_map/ppermute | solution.py:180
  146.9 17.9 %copy-start.8 = (bf16[4,256,128]{2,1,0:T(8,128)(2,1)S(1)}, bf16[4,256,128]{2,1,0:T(8,128)(2,1)}, u32[]{:S(2)}) copy-start(bf16[4,256,128]{2,1,0:T(8,128)(2,1)} %copy-done.7) | copy-start | bytes 786436
  146.9 15.4 %collective-permute-start.27 = (bf16[4,256,128]{2,1,0:T(8,128)(2,1)S(1)}, bf16[4,256,128]{2,1,0:T(8,128)(2,1)S(1)}, u32[]{:S(2)}, u32[]{:S(2)}) collective-permute-start(bf16[4,256,128]{2,1,0:T(8,128)(2,1)S(1)} %get-tuple-element.39), channel_id=1, source_target_pairs={{0,4},{1,5},{2,6},{3,7},{4,8},{5,9},{6,10},{7,11},{8,12},{9,13},{1... | collective-permute-start | bytes 786440 | tf_op jit(solution)/shard_map/ppermute | solution.py:180
  147.0 17.8 %collective-permute-start.29 = (bf16[4,256,128]{2,1,0:T(8,128)(2,1)S(1)}, bf16[4,256,128]{2,1,0:T(8,128)(2,1)S(1)}, u32[]{:S(2)}, u32[]{:S(2)}) collective-permute-start(bf16[4,256,128]{2,1,0:T(8,128)(2,1)S(1)} %get-tuple-element.40), channel_id=1, source_target_pairs={{0,8},{1,9},{2,10},{3,11},{4,12},{5,13},{6,14},{7,15},{8,0},{9,1},... | collective-permute-start | bytes 786440 | tf_op jit(solution)/shard_map/ppermute | solution.py:180
  151.8 12.9 %collective-permute-start.28 = (bf16[4,256,128]{2,1,0:T(8,128)(2,1)S(1)}, bf16[4,256,128]{2,1,0:T(8,128)(2,1)S(1)}, u32[]{:S(2)}, u32[]{:S(2)}) collective-permute-start(bf16[4,256,128]{2,1,0:T(8,128)(2,1)S(1)} %get-tuple-element.41), channel_id=1, source_target_pairs={{0,12},{1,13},{2,14},{3,15},{4,0},{5,1},{6,2},{7,3},{8,4},{9,5},{1... | collective-permute-start | bytes 786440 | tf_op jit(solution)/shard_map/ppermute | solution.py:180
  160.2 10.5 %collective-permute-start.23 = (bf16[4,256,128]{2,1,0:T(8,128)(2,1)S(1)}, bf16[4,256,128]{2,1,0:T(8,128)(2,1)S(1)}, u32[]{:S(2)}, u32[]{:S(2)}) collective-permute-start(bf16[4,256,128]{2,1,0:T(8,128)(2,1)S(1)} %get-tuple-element.42), channel_id=1, source_target_pairs={{0,4},{1,5},{2,6},{3,7},{4,8},{5,9},{6,10},{7,11},{8,12},{9,13},{1... | collective-permute-start | bytes 786440 | tf_op jit(solution)/shard_map/ppermute | solution.py:180
  160.3 10.4 %collective-permute-start.25 = (bf16[4,256,128]{2,1,0:T(8,128)(2,1)S(1)}, bf16[4,256,128]{2,1,0:T(8,128)(2,1)S(1)}, u32[]{:S(2)}, u32[]{:S(2)}) collective-permute-start(bf16[4,256,128]{2,1,0:T(8,128)(2,1)S(1)} %get-tuple-element.43), channel_id=1, source_target_pairs={{0,8},{1,9},{2,10},{3,11},{4,12},{5,13},{6,14},{7,15},{8,0},{9,1},... | collective-permute-start | bytes 786440 | tf_op jit(solution)/shard_map/ppermute | solution.py:180
  162.2 9.4 %collective-permute-start.24 = (bf16[4,256,128]{2,1,0:T(8,128)(2,1)S(1)}, bf16[4,256,128]{2,1,0:T(8,128)(2,1)S(1)}, u32[]{:S(2)}, u32[]{:S(2)}) collective-permute-start(bf16[4,256,128]{2,1,0:T(8,128)(2,1)S(1)} %get-tuple-element.44), channel_id=1, source_target_pairs={{0,12},{1,13},{2,14},{3,15},{4,0},{5,1},{6,2},{7,3},{8,4},{9,5},{1... | collective-permute-start | bytes 786440 | tf_op jit(solution)/shard_map/ppermute | solution.py:180
  165.0 7.5 %collective-permute-start.30 = (bf16[4,256,128]{2,1,0:T(8,128)(2,1)S(1)}, bf16[4,256,128]{2,1,0:T(8,128)(2,1)S(1)}, u32[]{:S(2)}, u32[]{:S(2)}) collective-permute-start(bf16[4,256,128]{2,1,0:T(8,128)(2,1)S(1)} %fusion.3), channel_id=1, source_target_pairs={{0,16},{16,0},{32,48},{48,32},{64,80},{80,64},{96,112},{112,96},{1... | collective-permute-start | bytes 786440 | tf_op jit(solution)/shard_map/ppermute | solution.py:184
  172.6 0.7 copy-start.9

commit v2 on v1

--- a/solution.py
+++ b/solution.py
@@ -94,9 +94,6 @@
 
     for i in range(16):
         piece_copy(i).start()
-    for c in range(n_hidden):
-        up_copy(c).start()
-        down_copy(c).start()
     squares[...] = jnp.zeros(squares.shape, F32)
 
     @pl.loop(0, 64)
@@ -105,6 +102,9 @@
 
     for i in range(16):
         piece_copy(i).wait()
+        for c in range(i * n_hidden // 16, (i + 1) * n_hidden // 16):
+            up_copy(c).start()
+            down_copy(c).start()
         total = squares[...]
         for b in range(4):
             block = places_in[i] * 4 + b
@@ -207,7 +207,7 @@
     return (mid.astype(F32) + down).astype(BF16)
 
 
-def states_before(own):
+def states_before(own, beside):
     core = lax.axis_index("seq") % 2
     other = swap_cores(own)
 
@@ -217,11 +217,12 @@
     both = own.astype(F32) + other.astype(F32)
     pair = jnp.where(core == 0, both[:2], both[2:]).astype(BF16)
     near = later(pair, 1).astype(F32) + later(pair, 2).astype(F32)
+    near, beside = lax.optimization_barrier((near, beside))
     window = (near + pair.astype(F32)).astype(BF16)
     before = near + later(window, 3).astype(F32) + later(window, 6).astype(F32)
     rest = swap_cores(before.astype(BF16)).astype(F32)
     whole = jnp.where(core == 0, jnp.concatenate([before, rest]), jnp.concatenate([rest, before]))
-    return whole + jnp.where(core == 0, 0.0, other.astype(F32))
+    return whole + jnp.where(core == 0, 0.0, other.astype(F32)), beside
 
 
 def per_device(queries, keys_in, values_in, stream, attn_gain, mlp_gain, up_index, up_blocks, down_index, down_blocks):
@@ -240,7 +241,7 @@
         cost_estimate=pl.CostEstimate(flops=2**30, bytes_accessed=3 * 2**20, transcendentals=2**19),
         name="within_block",
     )(queries, keys_in, values_in)
-    before = states_before(own)
+    before, intra = states_before(own, intra)
     half = jax.ShapeDtypeStruct((4, 256, 128), BF16)
     core = lax.axis_index("seq") % 2
     core_arg = core.reshape(1)

time: 176 us -> 172 us (0.977)
  starting transfers between devices: 40.4 us -> 36.3 us
  waiting for transfers between devices: 87.7 us -> 90.1 us
    ppermute x23, waiting for transfers between devices: 70.4 us -> 75 us  [torus_shift(): return lax.ppermute(x, ('seq', 'wt'), pairs)]
    ppermute x23, starting transfers between devices: 32.4 us -> 28.7 us  [torus_shift(): return lax.ppermute(x, ('seq', 'wt'), pairs)]
    ppermute x4, waiting for transfers between devices: 14.4 us -> 10.7 us  [later(): lax.ppermute(x, 'seq', [(s, s + 2 * places) for s in range(SEQ) if s + 2...]
  transfers between devices with their start and end apart: 31 -> 31, of which waited for: 16 -> 17; matrix products, arithmetic and copies ran while one was open for 3% -> 3% of each run, Pallas kernels for 16% -> 15%
where the time goes in v2:
time: 172 us
  waiting for transfers between devices  90.1 us (52%)
  starting transfers between devices  36.3 us (21%)
  Pallas kernels  34 us (20%)
  local copies, waits for them, and re-layouts  5.78 us (3%)
  other arithmetic  5.55 us (3%)
    ppermute x23, waiting for transfers between devices, torus_shift(): return lax.ppermute(x, ('seq', 'wt'), pairs)  75 us
    ppermute x23, starting transfers between devices, torus_shift(): return lax.ppermute(x, ('seq', 'wt'), pairs)  28.7 us
    pallas_call x2, Pallas kernels, ffn(): pl.pallas_call(functools.partial(ffn_kernel, t), out_shape=[jax.ShapeDtyp...  22.5 us
    ppermute x4, waiting for transfers between devices, later(): lax.ppermute(x, 'seq', [(s, s + 2 * places) for s in range(SEQ) if s + 2...  10.7 us
    ppermute x4, starting transfers between devices, later(): lax.ppermute(x, 'seq', [(s, s + 2 * places) for s in range(SEQ) if s + 2...  7.26 us
    ppermute x4, waiting for transfers between devices, swap_cores(): return lax.ppermute(x, 'seq', [(s, s ^ 1) for s in range(SEQ)])  4.39 us
    pallas_call x1, Pallas kernels, per_device(): pl.pallas_call(intra_kernel, out_shape=jax.ShapeDtypeStruct((4, 512, HEAD...  4.06 us
  transfers between devices with their start and end apart: 31, of which 17 were waited for; matrix products, arithmetic and copies ran while one was open for 3% of the time, Pallas kernels for 15%

profile of v2, /device:TPU:184, one launch (start us, length us, event | category | flops | bytes accessed | tf_op | source)
XLA Modules:
  0.0 172.1 jit_solution(2387528521085883555)
XLA Ops:
  0.0 2.4 %states.1 = bf16[4,128,128]{2,1,0:T(8,128)(2,1)} custom-call(bf16[512,512]{1,0:T(8,128)(2,1)} %k_ref.3, bf16[512,512]{1,0:T(8,128)(2,1)} %v_ref.3), custom_call_target="tpu_custom_call" | custom-call | tf_op jit(solution)/shard_map/states/pallas_call | solution.py:229
  2.4 1.6 collective-permute-done
  3.9 0.9 convert_add_fusion.2
  4.9 3.4 %collective-permute-start.2 = (bf16[2,128,128]{2,1,0:T(8,128)(2,1)S(1)}, bf16[2,128,128]{2,1,0:T(8,128)(2,1)S(1)}, u32[]{:S(2)}, u32[]{:S(2)}) collective-permute-start(bf16[2,128,128]{2,1,0:T(8,128)(2,1)S(1)} %fusion.17), channel_id=1, source_target_pairs={{0,64},{16,80},{32,96},{48,112},{64,128},{80,144},{96,160},{112,17... | collective-permute-start | bytes 196616 | tf_op jit(solution)/shard_map/ppermute | solution.py:215
  8.3 1.9 %collective-permute-start.1 = (bf16[2,128,128]{2,1,0:T(8,128)(2,1)S(1)}, bf16[2,128,128]{2,1,0:T(8,128)(2,1)S(1)}, u32[]{:S(2)}, u32[]{:S(2)}) collective-permute-start(bf16[2,128,128]{2,1,0:T(8,128)(2,1)S(1)} %fusion.17), channel_id=1, source_target_pairs={{0,32},{16,48},{32,64},{48,80},{64,96},{80,112},{96,128},{112,144}... | collective-permute-start | bytes 196616 | tf_op jit(solution)/shard_map/ppermute | solution.py:215
  10.2 4.1 %within_block.1.intra_ref = f32[4,512,128]{2,1,0:T(8,128)} custom-call(bf16[512,512]{1,0:T(8,128)(2,1)} %q_ref.3, bf16[512,512]{1,0:T(8,128)(2,1)} %k_ref.3, bf16[512,512]{1,0:T(8,128)(2,1)} %v_ref.3), custom_call_target="tpu_custom_call" | custom-call | flops 1073741824 | bytes 3145728 | tf_op jit(solution)/shard_map/within_block/pallas_call | solution.py:236
  14.3 0.4 collective-permute-done.2
  14.8 0.7 collective-permute-start.4
  15.4 1.3 collective-permute-start.3
  16.8 10.3 %collective-permute-done.3 = bf16[2,128,128]{2,1,0:T(8,128)(2,1)S(1)} collective-permute-done((bf16[2,128,128]{2,1,0:T(8,128)(2,1)S(1)}, bf16[2,128,128]{2,1,0:T(8,128)(2,1)S(1)}, u32[]{:S(2)}, u32[]{:S(2)}) %collective-permute-start.3) | collective-permute-done | bytes 65568 | tf_op jit(solution)/shard_map/ppermute | solution.py:215
  27.1 0.1 collective-permute-start.5
  27.2 1.2 collective-permute-done.5
  28.4 0.7 fusion.8.state_ref
  29.2 3.2 %mid.1 = (bf16[4,256,128]{2,1,0:T(8,128)(2,1)}, bf16[4,256,128]{2,1,0:T(8,128)(2,1)}) custom-call(s32[1]{0:T(128)} %bitcast.core_ref, bf16[512,512]{1,0:T(8,128)(2,1)} %q_ref.3, f32[4,128,128]{2,1,0:T(8,128)} %fusion.8.state_ref, f32[4,512,128]{2,1,0:T(8,128)} %within_block.1.intra_ref, bf16[512,512]{1,0:T(8,128)(2,1)} %stream_ref.1, f32[1,512]{1,0:T(1,128)} %bitcast.35), custom_call_target="tpu_custom_call" | custom-call | tf_op jit(solution)/shard_map/mid/pallas_call | solution.py:248
  32.4 0.2 collective-permute-start.6
  32.5 1.6 collective-permute-done.6
  34.1 1.1 pad_maximum_fusion.2
  35.2 1.6 collective-permute-start.7
  36.8 1.7 %collective-permute-start.9 = (bf16[2,4,256,128]{3,2,1,0:T(8,128)(2,1)S(1)}, bf16[2,4,256,128]{3,2,1,0:T(8,128)(2,1)S(1)}, u32[]{:S(2)}, u32[]{:S(2)}) collective-permute-start(bf16[2,4,256,128]{3,2,1,0:T(8,128)(2,1)S(1)} %pad_maximum_fusion.2), channel_id=1, source_target_pairs={{0,12},{1,13},{2,14},{3,15},{4,0},{5,1},{6,2},{7,3},{8,4},{9,5},{1... | collective-permute-start | bytes 1572872 | tf_op jit(solution)/shard_map/ppermute | solution.py:180
  38.5 1.8 %collective-permute-start.8 = (bf16[2,4,256,128]{3,2,1,0:T(8,128)(2,1)S(1)}, bf16[2,4,256,128]{3,2,1,0:T(8,128)(2,1)S(1)}, u32[]{:S(2)}, u32[]{:S(2)}) collective-permute-start(bf16[2,4,256,128]{3,2,1,0:T(8,128)(2,1)S(1)} %pad_maximum_fusion.2), channel_id=1, source_target_pairs={{0,8},{1,9},{2,10},{3,11},{4,12},{5,13},{6,14},{7,15},{8,0},{9,1},... | collective-permute-start | bytes 1572872 | tf_op jit(solution)/shard_map/ppermute | solution.py:180
  40.4 5.3 %collective-permute-done.7 = bf16[2,4,256,128]{3,2,1,0:T(8,128)(2,1)S(1)} collective-permute-done((bf16[2,4,256,128]{3,2,1,0:T(8,128)(2,1)S(1)}, bf16[2,4,256,128]{3,2,1,0:T(8,128)(2,1)S(1)}, u32[]{:S(2)}, u32[]{:S(2)}) %collective-permute-start.7) | collective-permute-done | bytes 524320 | tf_op jit(solution)/shard_map/ppermute | solution.py:180
  45.8 0.1 pad_maximum_fusion.refs_0_
  45.9 0.3 collective-permute-start.10
  46.2 4.7 %collective-permute-done.9 = bf16[2,4,256,128]{3,2,1,0:T(8,128)(2,1)S(1)} collective-permute-done((bf16[2,4,256,128]{3,2,1,0:T(8,128)(2,1)S(1)}, bf16[2,4,256,128]{3,2,1,0:T(8,128)(2,1)S(1)}, u32[]{:S(2)}, u32[]{:S(2)}) %collective-permute-start.9) | collective-permute-done | bytes 524320 | tf_op jit(solution)/shard_map/ppermute | solution.py:180
  50.9 4.7 %collective-permute-done.8 = bf16[2,4,256,128]{3,2,1,0:T(8,128)(2,1)S(1)} collective-permute-done((bf16[2,4,256,128]{3,2,1,0:T(8,128)(2,1)S(1)}, bf16[2,4,256,128]{3,2,1,0:T(8,128)(2,1)S(1)}, u32[]{:S(2)}, u32[]{:S(2)}) %collective-permute-start.8) | collective-permute-done | bytes 524320 | tf_op jit(solution)/shard_map/ppermute | solution.py:180
  55.7 0.1 pad_maximum_fusion.1.refs_1_
  56.0 1.2 collective-permute-start.12
  57.2 2.1 %collective-permute-start.11 = (bf16[4,4,256,128]{3,2,1,0:T(8,128)(2,1)S(1)}, bf16[4,4,256,128]{3,2,1,0:T(8,128)(2,1)}, u32[]{:S(2)}, u32[]{:S(2)}) collective-permute-start(bf16[4,4,256,128]{3,2,1,0:T(8,128)(2,1)S(1)} %pad_maximum_fusion.1.refs_1_), channel_id=1, source_target_pairs={{0,1},{1,2},{2,3},{3,0},{4,5},{5,6},{6,7},{7,4},{8,9},{9,10},{10,1... | collective-permute-start | bytes 3145736 | tf_op jit(solution)/shard_map/ppermute | solution.py:180
  59.3 1.5 collective-permute-done.10.refs_2_
  60.8 1.0 fusion.29
  61.8 2.4 %collective-permute-start.14 = (bf16[2,4,256,128]{3,2,1,0:T(8,128)(2,1)}, bf16[2,4,256,128]{3,2,1,0:T(8,128)(2,1)}, u32[]{:S(2)}, u32[]{:S(2)}) collective-permute-start(bf16[2,4,256,128]{3,2,1,0:T(8,128)(2,1)} %get-tuple-element.51), channel_id=1, source_target_pairs={{0,1},{1,2},{2,3},{3,0},{4,5},{5,6},{6,7},{7,4},{8,9},{9,10},{10,1... | collective-permute-start | bytes 1572872 | tf_op jit(solution)/shard_map/ppermute | solution.py:180
  64.2 7.8 %collective-permute-done.13.refs_5_ = bf16[4,4,256,128]{3,2,1,0:T(8,128)(2,1)S(1)} collective-permute-done((bf16[4,4,256,128]{3,2,1,0:T(8,128)(2,1)S(1)}, bf16[4,4,256,128]{3,2,1,0:T(8,128)(2,1)S(1)}, u32[]{:S(2)}, u32[]{:S(2)}) %collective-permute-start.13) | collective-permute-done | bytes 1048608 | tf_op jit(solution)/shard_map/ppermute | solution.py:180
  72.0 1.1 fusion.28
  73.0 1.0 copy-done
  74.1 0.7 gather_fusion
  74.7 3.3 %collective-permute-start.18 = (bf16[2,4,256,128]{3,2,1,0:T(8,128)(2,1)}, bf16[2,4,256,128]{3,2,1,0:T(8,128)(2,1)S(1)}, u32[]{:S(2)}, u32[]{:S(2)}) collective-permute-start(bf16[2,4,256,128]{3,2,1,0:T(8,128)(2,1)} %get-tuple-element.52), channel_id=1, source_target_pairs={{0,1},{1,2},{2,3},{3,0},{4,5},{5,6},{6,7},{7,4},{8,9},{9,10},{10,1... | collective-permute-start | bytes 1572872 | tf_op jit(solution)/shard_map/ppermute | solution.py:180
  78.0 5.3 %collective-permute-done.12.refs_4_ = bf16[4,4,256,128]{3,2,1,0:T(8,128)(2,1)} collective-permute-done((bf16[4,4,256,128]{3,2,1,0:T(8,128)(2,1)S(1)}, bf16[4,4,256,128]{3,2,1,0:T(8,128)(2,1)}, u32[]{:S(2)}, u32[]{:S(2)}) %collective-permute-start.12) | collective-permute-done | bytes 1048608 | tf_op jit(solution)/shard_map/ppermute | solution.py:180
  83.4 5.6 %collective-permute-done.15.refs_7_ = bf16[2,4,256,128]{3,2,1,0:T(8,128)(2,1)} collective-permute-done((bf16[2,4,256,128]{3,2,1,0:T(8,128)(2,1)}, bf16[2,4,256,128]{3,2,1,0:T(8,128)(2,1)}, u32[]{:S(2)}, u32[]{:S(2)}) %collective-permute-start.15) | collective-permute-done | bytes 524320 | tf_op jit(solution)/shard_map/ppermute | solution.py:180
  89.0 1.2 copy-done.1
  90.2 11.2 %feed_forward.2 = (bf16[4,4,256,128]{3,2,1,0:T(8,128)(2,1)S(1)}, bf16[4,4,256,128]{3,2,1,0:T(8,128)(2,1)S(1)}, bf16[4,4,256,128]{3,2,1,0:T(8,128)(2,1)S(1)}, bf16[4,4,256,128]{3,2,1,0:T(8,128)(2,1)S(1)}) custom-call(s32[16]{0:T(128)S(1)} %get-tuple-element.60.places_in, s32[16]{0:T(128)S(1)} %get-tuple-element.59.places_out, s32[8,16]{1,0:T(8,128)S(1)} %copy-done.3, ...), custom_call_target="tpu_custom_call" | custom-call | flops 2147483648 | bytes 17825792 | tf_op jit(solution)/shard_map/feed_forward/pallas_call | solution.py:140
  101.4 0.1 collective-permute-start.16
  101.5 2.0 %collective-permute-start.17 = (bf16[4,4,256,128]{3,2,1,0:T(8,128)(2,1)S(1)}, bf16[4,4,256,128]{3,2,1,0:T(8,128)(2,1)S(1)}, u32[]{:S(2)}, u32[]{:S(2)}) collective-permute-start(bf16[4,4,256,128]{3,2,1,0:T(8,128)(2,1)S(1)} %get-tuple-element.28), channel_id=1, source_target_pairs={{0,3},{1,0},{2,1},{3,2},{4,7},{5,4},{6,5},{7,6},{8,11},{9,8},{10,9... | collective-permute-start | bytes 3145736 | tf_op jit(solution)/shard_map/ppermute | solution.py:180
  103.5 11.3 %feed_forward.3 = (bf16[4,4,256,128]{3,2,1,0:T(8,128)(2,1)S(1)}, bf16[4,4,256,128]{3,2,1,0:T(8,128)(2,1)S(1)}, bf16[4,4,256,128]{3,2,1,0:T(8,128)(2,1)S(1)}, bf16[4,4,256,128]{3,2,1,0:T(8,128)(2,1)S(1)}) custom-call(s32[16]{0:T(128)S(1)} %get-tuple-element.60.places_in, s32[16]{0:T(128)S(1)} %get-tuple-element.59.places_out, s32[8,16]{1,0:T(8,128)S(1)} %copy-done.3, ...), custom_call_target="tpu_custom_call" | custom-call | flops 2147483648 | bytes 17825792 | tf_op jit(solution)/shard_map/feed_forward/pallas_call | solution.py:140
  114.8 0.1 collective-permute-start.20
  114.9 3.2 %collective-permute-start.22 = (bf16[4,4,256,128]{3,2,1,0:T(8,128)(2,1)S(1)}, bf16[4,4,256,128]{3,2,1,0:T(8,128)(2,1)S(1)}, u32[]{:S(2)}, u32[]{:S(2)}) collective-permute-start(bf16[4,4,256,128]{3,2,1,0:T(8,128)(2,1)S(1)} %get-tuple-element.36), channel_id=1, source_target_pairs={{0,1},{1,2},{2,3},{3,0},{4,5},{5,6},{6,7},{7,4},{8,9},{9,10},{10,1... | collective-permute-start | bytes 3145736 | tf_op jit(solution)/shard_map/ppermute | solution.py:180
  118.1 0.3 add_convert_fusion
  118.4 0.2 collective-permute-start.26
  118.6 12.3 %collective-permute-done.20 = bf16[4,4,256,128]{3,2,1,0:T(8,128)(2,1)S(1)} collective-permute-done((bf16[4,4,256,128]{3,2,1,0:T(8,128)(2,1)S(1)}, bf16[4,4,256,128]{3,2,1,0:T(8,128)(2,1)S(1)}, u32[]{:S(2)}, u32[]{:S(2)}) %collective-permute-start.20) | collective-permute-done | bytes 1048608 | tf_op jit(solution)/shard_map/ppermute | solution.py:180
  130.9 0.3 add_convert_fusion.1
  131.2 14.9 %collective-permute-done.26 = bf16[4,4,256,128]{3,2,1,0:T(8,128)(2,1)S(1)} collective-permute-done((bf16[4,4,256,128]{3,2,1,0:T(8,128)(2,1)S(1)}, bf16[4,4,256,128]{3,2,1,0:T(8,128)(2,1)S(1)}, u32[]{:S(2)}, u32[]{:S(2)}) %collective-permute-start.26) | collective-permute-done | bytes 1048608 | tf_op jit(solution)/shard_map/ppermute | solution.py:180
  146.2 0.3 fusion.14
  146.6 2.2 %collective-permute-start.29 = (bf16[4,256,128]{2,1,0:T(8,128)(2,1)S(1)}, bf16[4,256,128]{2,1,0:T(8,128)(2,1)S(1)}, u32[]{:S(2)}, u32[]{:S(2)}) collective-permute-start(bf16[4,256,128]{2,1,0:T(8,128)(2,1)S(1)} %get-tuple-element.44), channel_id=1, source_target_pairs={{0,8},{1,9},{2,10},{3,11},{4,12},{5,13},{6,14},{7,15},{8,0},{9,1},... | collective-permute-start | bytes 786440 | tf_op jit(solution)/shard_map/ppermute | solution.py:180
  148.8 2.5 %collective-permute-start.28 = (bf16[4,256,128]{2,1,0:T(8,128)(2,1)S(1)}, bf16[4,256,128]{2,1,0:T(8,128)(2,1)S(1)}, u32[]{:S(2)}, u32[]{:S(2)}) collective-permute-start(bf16[4,256,128]{2,1,0:T(8,128)(2,1)S(1)} %get-tuple-element.45), channel_id=1, source_target_pairs={{0,12},{1,13},{2,14},{3,15},{4,0},{5,1},{6,2},{7,3},{8,4},{9,5},{1... | collective-permute-start | bytes 786440 | tf_op jit(solution)/shard_map/ppermute | solution.py:180
  151.3 5.5 %collective-permute-done.21 = bf16[4,4,256,128]{3,2,1,0:T(8,128)(2,1)S(1)} collective-permute-done((bf16[4,4,256,128]{3,2,1,0:T(8,128)(2,1)S(1)}, bf16[4,4,256,128]{3,2,1,0:T(8,128)(2,1)S(1)}, u32[]{:S(2)}, u32[]{:S(2)}) %collective-permute-start.21) | collective-permute-done | bytes 1048608 | tf_op jit(solution)/shard_map/ppermute | solution.py:180
  156.9 0.3 fusion.10
  157.3 1.1 collective-permute-start.25
  158.3 2.5 %collective-permute-start.24 = (bf16[4,256,128]{2,1,0:T(8,128)(2,1)S(1)}, bf16[4,256,128]{2,1,0:T(8,128)(2,1)S(1)}, u32[]{:S(2)}, u32[]{:S(2)}) collective-permute-start(bf16[4,256,128]{2,1,0:T(8,128)(2,1)S(1)} %get-tuple-element.48), channel_id=1, source_target_pairs={{0,12},{1,13},{2,14},{3,15},{4,0},{5,1},{6,2},{7,3},{8,4},{9,5},{1... | collective-permute-start | bytes 786440 | tf_op jit(solution)/shard_map/ppermute | solution.py:180
  160.9 0.2 fusion.3
  161.1 0.1 collective-permute-start.30
  161.2 6.4 %collective-permute-done.23 = bf16[4,256,128]{2,1,0:T(8,128)(2,1)S(1)} collective-permute-done((bf16[4,256,128]{2,1,0:T(8,128)(2,1)S(1)}, bf16[4,256,128]{2,1,0:T(8,128)(2,1)S(1)}, u32[]{:S(2)}, u32[]{:S(2)}) %collective-permute-start.23) | collective-permute-done | bytes 262176 | tf_op jit(solution)/shard_map/ppermute | solution.py:180
  167.7 0.9 collective-permute-done.24
  168.6 1.0 fusion.7.mine_ref
  169.5 0.7 copy-done.9
  170.2 1.9 %result.1 = bf16[512,512]{1,0:T(8,128)(2,1)} custom-call(s32[1]{0:T(128)} %bitcast.core_ref, bf16[4,256,128]{2,1,0:T(8,128)(2,1)} %fusion.7.mine_ref, bf16[4,256,128]{2,1,0:T(8,128)(2,1)} %copy-done.9), custom_call_target="tpu_custom_call" | custom-call | tf_op jit(solution)/shard_map/result/pallas_call | solution.py:291
  (49 shorter events, 0.7 us)
Async XLA Ops:
  2.4 1.6 collective-permute-start
  4.9 9.8 %collective-permute-start.2 = (bf16[2,128,128]{2,1,0:T(8,128)(2,1)S(1)}, bf16[2,128,128]{2,1,0:T(8,128)(2,1)S(1)}, u32[]{:S(2)}, u32[]{:S(2)}) collective-permute-start(bf16[2,128,128]{2,1,0:T(8,128)(2,1)S(1)} %fusion.17), channel_id=1, source_target_pairs={{0,64},{16,80},{32,96},{48,112},{64,128},{80,144},{96,160},{112,17... | collective-permute-start | bytes 196616 | tf_op jit(solution)/shard_map/ppermute | solution.py:215
  8.3 6.4 %collective-permute-start.1 = (bf16[2,128,128]{2,1,0:T(8,128)(2,1)S(1)}, bf16[2,128,128]{2,1,0:T(8,128)(2,1)S(1)}, u32[]{:S(2)}, u32[]{:S(2)}) collective-permute-start(bf16[2,128,128]{2,1,0:T(8,128)(2,1)S(1)} %fusion.17), channel_id=1, source_target_pairs={{0,32},{16,48},{32,64},{48,80},{64,96},{80,112},{96,128},{112,144}... | collective-permute-start | bytes 196616 | tf_op jit(solution)/shard_map/ppermute | solution.py:215
  14.8 2.0 %collective-permute-start.4 = (bf16[2,128,128]{2,1,0:T(8,128)(2,1)S(1)}, bf16[2,128,128]{2,1,0:T(8,128)(2,1)S(1)}, u32[]{:S(2)}, u32[]{:S(2)}) collective-permute-start(bf16[2,128,128]{2,1,0:T(8,128)(2,1)S(1)} %add_convert_fusion.10), channel_id=1, source_target_pairs={{0,192},{16,208},{32,224},{48,240},{1,193},{17,209},{33,225},{49,2... | collective-permute-start | bytes 196616 | tf_op jit(solution)/shard_map/ppermute | solution.py:215
  15.4 11.6 %collective-permute-start.3 = (bf16[2,128,128]{2,1,0:T(8,128)(2,1)S(1)}, bf16[2,128,128]{2,1,0:T(8,128)(2,1)S(1)}, u32[]{:S(2)}, u32[]{:S(2)}) collective-permute-start(bf16[2,128,128]{2,1,0:T(8,128)(2,1)S(1)} %add_convert_fusion.10), channel_id=1, source_target_pairs={{0,96},{16,112},{32,128},{48,144},{64,160},{80,176},{96,192},{112,... | collective-permute-start | bytes 196616 | tf_op jit(solution)/shard_map/ppermute | solution.py:215
  27.1 1.3 collective-permute-start.5
  32.4 13.4 %copy-start.6 = (bf16[4,256,128]{2,1,0:T(8,128)(2,1)S(1)}, bf16[4,256,128]{2,1,0:T(8,128)(2,1)}, u32[]{:S(2)}) copy-start(bf16[4,256,128]{2,1,0:T(8,128)(2,1)} %get-tuple-element.25) | copy-start | bytes 786436
  32.4 1.7 %collective-permute-start.6 = (bf16[4,256,128]{2,1,0:T(8,128)(2,1)}, bf16[4,256,128]{2,1,0:T(8,128)(2,1)S(1)}, u32[]{:S(2)}, u32[]{:S(2)}) collective-permute-start(bf16[4,256,128]{2,1,0:T(8,128)(2,1)} %get-tuple-element.26), channel_id=1, source_target_pairs={{0,16},{16,0},{32,48},{48,32},{64,80},{80,64},{96,112},{112,96},{1... | collective-permute-start | bytes 786440 | tf_op jit(solution)/shard_map/ppermute | solution.py:184
  34.1 11.6 %copy-start.7 = (bf16[4,256,128]{2,1,0:T(8,128)(2,1)}, bf16[4,256,128]{2,1,0:T(8,128)(2,1)S(1)}, u32[]{:S(2)}) copy-start(bf16[4,256,128]{2,1,0:T(8,128)(2,1)S(1)} %collective-permute-done.6) | copy-start | bytes 786436
  35.2 10.5 %collective-permute-start.7 = (bf16[2,4,256,128]{3,2,1,0:T(8,128)(2,1)S(1)}, bf16[2,4,256,128]{3,2,1,0:T(8,128)(2,1)S(1)}, u32[]{:S(2)}, u32[]{:S(2)}) collective-permute-start(bf16[2,4,256,128]{3,2,1,0:T(8,128)(2,1)S(1)} %pad_maximum_fusion.2), channel_id=1, source_target_pairs={{0,4},{1,5},{2,6},{3,7},{4,8},{5,9},{6,10},{7,11},{8,12},{9,13},{1... | collective-permute-start | bytes 1572872 | tf_op jit(solution)/shard_map/ppermute | solution.py:180
  36.8 14.1 %collective-permute-start.9 = (bf16[2,4,256,128]{3,2,1,0:T(8,128)(2,1)S(1)}, bf16[2,4,256,128]{3,2,1,0:T(8,128)(2,1)S(1)}, u32[]{:S(2)}, u32[]{:S(2)}) collective-permute-start(bf16[2,4,256,128]{3,2,1,0:T(8,128)(2,1)S(1)} %pad_maximum_fusion.2), channel_id=1, source_target_pairs={{0,12},{1,13},{2,14},{3,15},{4,0},{5,1},{6,2},{7,3},{8,4},{9,5},{1... | collective-permute-start | bytes 1572872 | tf_op jit(solution)/shard_map/ppermute | solution.py:180
  38.5 17.1 %collective-permute-start.8 = (bf16[2,4,256,128]{3,2,1,0:T(8,128)(2,1)S(1)}, bf16[2,4,256,128]{3,2,1,0:T(8,128)(2,1)S(1)}, u32[]{:S(2)}, u32[]{:S(2)}) collective-permute-start(bf16[2,4,256,128]{3,2,1,0:T(8,128)(2,1)S(1)} %pad_maximum_fusion.2), channel_id=1, source_target_pairs={{0,8},{1,9},{2,10},{3,11},{4,12},{5,13},{6,14},{7,15},{8,0},{9,1},... | collective-permute-start | bytes 1572872 | tf_op jit(solution)/shard_map/ppermute | solution.py:180
  45.9 14.9 %collective-permute-start.10 = (bf16[4,4,256,128]{3,2,1,0:T(8,128)(2,1)S(1)}, bf16[4,4,256,128]{3,2,1,0:T(8,128)(2,1)S(1)}, u32[]{:S(2)}, u32[]{:S(2)}) collective-permute-start(bf16[4,4,256,128]{3,2,1,0:T(8,128)(2,1)S(1)} %pad_maximum_fusion.refs_0_), channel_id=1, source_target_pairs={{0,1},{1,2},{2,3},{3,0},{4,5},{5,6},{6,7},{7,4},{8,9},{9,10},{10,1... | collective-permute-start | bytes 3145736 | tf_op jit(solution)/shard_map/ppermute | solution.py:180
  55.9 18.2 %copy-start.5 = (s32[4]{0:T(128)S(1)}, s32[4]{0:T(128)}, u32[]{:S(2)}) copy-start(s32[4]{0:T(128)} %constant.91.clone) | copy-start | bytes 52
  55.9 33.1 %copy-start.2 = (f32[8192]{0:T(1024)S(1)}, f32[8192]{0:T(1024)}, u32[]{:S(2)}) copy-start(f32[8192]{0:T(1024)} %param.16) | copy-start | bytes 98308
  55.9 33.1 %copy-start.3 = (s32[8,16]{1,0:T(8,128)S(1)}, s32[8,16]{1,0:T(8,128)}, u32[]{:S(2)}) copy-start(s32[8,16]{1,0:T(8,128)} %up_index.3) | copy-start | bytes 1540
  55.9 33.1 %copy-start.4 = (s32[8,16]{1,0:T(8,128)S(1)}, s32[8,16]{1,0:T(8,128)}, u32[]{:S(2)}) copy-start(s32[8,16]{1,0:T(8,128)} %down_index.3) | copy-start | bytes 1540
  55.9 16.1 %collective-permute-start.13 = (bf16[4,4,256,128]{3,2,1,0:T(8,128)(2,1)S(1)}, bf16[4,4,256,128]{3,2,1,0:T(8,128)(2,1)S(1)}, u32[]{:S(2)}, u32[]{:S(2)}) collective-permute-start(bf16[4,4,256,128]{3,2,1,0:T(8,128)(2,1)S(1)} %pad_maximum_fusion.1.refs_1_), channel_id=1, source_target_pairs={{0,3},{1,0},{2,1},{3,2},{4,7},{5,4},{6,5},{7,6},{8,11},{9,8},{10,9... | collective-permute-start | bytes 3145736 | tf_op jit(solution)/shard_map/ppermute | solution.py:180
  56.0 27.3 %collective-permute-start.12 = (bf16[4,4,256,128]{3,2,1,0:T(8,128)(2,1)S(1)}, bf16[4,4,256,128]{3,2,1,0:T(8,128)(2,1)}, u32[]{:S(2)}, u32[]{:S(2)}) collective-permute-start(bf16[4,4,256,128]{3,2,1,0:T(8,128)(2,1)S(1)} %pad_maximum_fusion.refs_0_), channel_id=1, source_target_pairs={{0,3},{1,0},{2,1},{3,2},{4,7},{5,4},{6,5},{7,6},{8,11},{9,8},{10,9... | collective-permute-start | bytes 3145736 | tf_op jit(solution)/shard_map/ppermute | solution.py:180
  57.2 26.2 %collective-permute-start.11 = (bf16[4,4,256,128]{3,2,1,0:T(8,128)(2,1)S(1)}, bf16[4,4,256,128]{3,2,1,0:T(8,128)(2,1)}, u32[]{:S(2)}, u32[]{:S(2)}) collective-permute-start(bf16[4,4,256,128]{3,2,1,0:T(8,128)(2,1)S(1)} %pad_maximum_fusion.1.refs_1_), channel_id=1, source_target_pairs={{0,1},{1,2},{2,3},{3,0},{4,5},{5,6},{6,7},{7,4},{8,9},{9,10},{10,1... | collective-permute-start | bytes 3145736 | tf_op jit(solution)/shard_map/ppermute | solution.py:180
  61.8 21.6 %collective-permute-start.14 = (bf16[2,4,256,128]{3,2,1,0:T(8,128)(2,1)}, bf16[2,4,256,128]{3,2,1,0:T(8,128)(2,1)}, u32[]{:S(2)}, u32[]{:S(2)}) collective-permute-start(bf16[2,4,256,128]{3,2,1,0:T(8,128)(2,1)} %get-tuple-element.51), channel_id=1, source_target_pairs={{0,1},{1,2},{2,3},{3,0},{4,5},{5,6},{6,7},{7,4},{8,9},{9,10},{10,1... | collective-permute-start | bytes 1572872 | tf_op jit(solution)/shard_map/ppermute | solution.py:180
  73.0 1.0 copy-start
  74.0 14.9 %collective-permute-start.15 = (bf16[2,4,256,128]{3,2,1,0:T(8,128)(2,1)}, bf16[2,4,256,128]{3,2,1,0:T(8,128)(2,1)}, u32[]{:S(2)}, u32[]{:S(2)}) collective-permute-start(bf16[2,4,256,128]{3,2,1,0:T(8,128)(2,1)} %get-tuple-element.49), channel_id=1, source_target_pairs={{0,3},{1,0},{2,1},{3,2},{4,7},{5,4},{6,5},{7,6},{8,11},{9,8},{10,9... | collective-permute-start | bytes 1572872 | tf_op jit(solution)/shard_map/ppermute | solution.py:180
  74.7 28.8 %collective-permute-start.18 = (bf16[2,4,256,128]{3,2,1,0:T(8,128)(2,1)}, bf16[2,4,256,128]{3,2,1,0:T(8,128)(2,1)S(1)}, u32[]{:S(2)}, u32[]{:S(2)}) collective-permute-start(bf16[2,4,256,128]{3,2,1,0:T(8,128)(2,1)} %get-tuple-element.52), channel_id=1, source_target_pairs={{0,1},{1,2},{2,3},{3,0},{4,5},{5,6},{6,7},{7,4},{8,9},{9,10},{10,1... | collective-permute-start | bytes 1572872 | tf_op jit(solution)/shard_map/ppermute | solution.py:180
  83.3 20.2 %collective-permute-start.19 = (bf16[2,4,256,128]{3,2,1,0:T(8,128)(2,1)}, bf16[2,4,256,128]{3,2,1,0:T(8,128)(2,1)S(1)}, u32[]{:S(2)}, u32[]{:S(2)}) collective-permute-start(bf16[2,4,256,128]{3,2,1,0:T(8,128)(2,1)} %get-tuple-element.50), channel_id=1, source_target_pairs={{0,3},{1,0},{2,1},{3,2},{4,7},{5,4},{6,5},{7,6},{8,11},{9,8},{10,9... | collective-permute-start | bytes 1572872 | tf_op jit(solution)/shard_map/ppermute | solution.py:180
  89.0 1.2 copy-start.1
  101.4 16.7 %collective-permute-start.16 = (bf16[4,4,256,128]{3,2,1,0:T(8,128)(2,1)S(1)}, bf16[4,4,256,128]{3,2,1,0:T(8,128)(2,1)S(1)}, u32[]{:S(2)}, u32[]{:S(2)}) collective-permute-start(bf16[4,4,256,128]{3,2,1,0:T(8,128)(2,1)S(1)} %get-tuple-element.27), channel_id=1, source_target_pairs={{0,1},{1,2},{2,3},{3,0},{4,5},{5,6},{6,7},{7,4},{8,9},{9,10},{10,1... | collective-permute-start | bytes 3145736 | tf_op jit(solution)/shard_map/ppermute | solution.py:180
  101.5 16.6 %collective-permute-start.17 = (bf16[4,4,256,128]{3,2,1,0:T(8,128)(2,1)S(1)}, bf16[4,4,256,128]{3,2,1,0:T(8,128)(2,1)S(1)}, u32[]{:S(2)}, u32[]{:S(2)}) collective-permute-start(bf16[4,4,256,128]{3,2,1,0:T(8,128)(2,1)S(1)} %get-tuple-element.28), channel_id=1, source_target_pairs={{0,3},{1,0},{2,1},{3,2},{4,7},{5,4},{6,5},{7,6},{8,11},{9,8},{10,9... | collective-permute-start | bytes 3145736 | tf_op jit(solution)/shard_map/ppermute | solution.py:180
  114.8 16.1 %collective-permute-start.20 = (bf16[4,4,256,128]{3,2,1,0:T(8,128)(2,1)S(1)}, bf16[4,4,256,128]{3,2,1,0:T(8,128)(2,1)S(1)}, u32[]{:S(2)}, u32[]{:S(2)}) collective-permute-start(bf16[4,4,256,128]{3,2,1,0:T(8,128)(2,1)S(1)} %get-tuple-element.35), channel_id=1, source_target_pairs={{0,3},{1,0},{2,1},{3,2},{4,7},{5,4},{6,5},{7,6},{8,11},{9,8},{10,9... | collective-permute-start | bytes 3145736 | tf_op jit(solution)/shard_map/ppermute | solution.py:180
  114.9 36.5 %collective-permute-start.22 = (bf16[4,4,256,128]{3,2,1,0:T(8,128)(2,1)S(1)}, bf16[4,4,256,128]{3,2,1,0:T(8,128)(2,1)S(1)}, u32[]{:S(2)}, u32[]{:S(2)}) collective-permute-start(bf16[4,4,256,128]{3,2,1,0:T(8,128)(2,1)S(1)} %get-tuple-element.36), channel_id=1, source_target_pairs={{0,1},{1,2},{2,3},{3,0},{4,5},{5,6},{6,7},{7,4},{8,9},{9,10},{10,1... | collective-permute-start | bytes 3145736 | tf_op jit(solution)/shard_map/ppermute | solution.py:180
  118.4 27.8 %collective-permute-start.26 = (bf16[4,4,256,128]{3,2,1,0:T(8,128)(2,1)S(1)}, bf16[4,4,256,128]{3,2,1,0:T(8,128)(2,1)S(1)}, u32[]{:S(2)}, u32[]{:S(2)}) collective-permute-start(bf16[4,4,256,128]{3,2,1,0:T(8,128)(2,1)S(1)} %add_convert_fusion), channel_id=1, source_target_pairs={{0,1},{1,2},{2,3},{3,0},{4,5},{5,6},{6,7},{7,4},{8,9},{9,10},{10,1... | collective-permute-start | bytes 3145736 | tf_op jit(solution)/shard_map/ppermute | solution.py:180
  131.2 25.7 %collective-permute-start.21 = (bf16[4,4,256,128]{3,2,1,0:T(8,128)(2,1)S(1)}, bf16[4,4,256,128]{3,2,1,0:T(8,128)(2,1)S(1)}, u32[]{:S(2)}, u32[]{:S(2)}) collective-permute-start(bf16[4,4,256,128]{3,2,1,0:T(8,128)(2,1)S(1)} %add_convert_fusion.1), channel_id=1, source_target_pairs={{0,3},{1,0},{2,1},{3,2},{4,7},{5,4},{6,5},{7,6},{8,11},{9,8},{10,9... | collective-permute-start | bytes 3145736 | tf_op jit(solution)/shard_map/ppermute | solution.py:180
  146.5 14.4 %copy-start.8 = (bf16[4,256,128]{2,1,0:T(8,128)(2,1)S(1)}, bf16[4,256,128]{2,1,0:T(8,128)(2,1)}, u32[]{:S(2)}) copy-start(bf16[4,256,128]{2,1,0:T(8,128)(2,1)} %copy-done.7) | copy-start | bytes 786436
  146.5 11.9 %collective-permute-start.27 = (bf16[4,256,128]{2,1,0:T(8,128)(2,1)S(1)}, bf16[4,256,128]{2,1,0:T(8,128)(2,1)S(1)}, u32[]{:S(2)}, u32[]{:S(2)}) collective-permute-start(bf16[4,256,128]{2,1,0:T(8,128)(2,1)S(1)} %get-tuple-element.43), channel_id=1, source_target_pairs={{0,4},{1,5},{2,6},{3,7},{4,8},{5,9},{6,10},{7,11},{8,12},{9,13},{1... | collective-permute-start | bytes 786440 | tf_op jit(solution)/shard_map/ppermute | solution.py:180
  146.6 14.3 %collective-permute-start.29 = (bf16[4,256,128]{2,1,0:T(8,128)(2,1)S(1)}, bf16[4,256,128]{2,1,0:T(8,128)(2,1)S(1)}, u32[]{:S(2)}, u32[]{:S(2)}) collective-permute-start(bf16[4,256,128]{2,1,0:T(8,128)(2,1)S(1)} %get-tuple-element.44), channel_id=1, source_target_pairs={{0,8},{1,9},{2,10},{3,11},{4,12},{5,13},{6,14},{7,15},{8,0},{9,1},... | collective-permute-start | bytes 786440 | tf_op jit(solution)/shard_map/ppermute | solution.py:180
  148.8 12.1 %collective-permute-start.28 = (bf16[4,256,128]{2,1,0:T(8,128)(2,1)S(1)}, bf16[4,256,128]{2,1,0:T(8,128)(2,1)S(1)}, u32[]{:S(2)}, u32[]{:S(2)}) collective-permute-start(bf16[4,256,128]{2,1,0:T(8,128)(2,1)S(1)} %get-tuple-element.45), channel_id=1, source_target_pairs={{0,12},{1,13},{2,14},{3,15},{4,0},{5,1},{6,2},{7,3},{8,4},{9,5},{1... | collective-permute-start | bytes 786440 | tf_op jit(solution)/shard_map/ppermute | solution.py:180
  157.2 10.5 %collective-permute-start.23 = (bf16[4,256,128]{2,1,0:T(8,128)(2,1)S(1)}, bf16[4,256,128]{2,1,0:T(8,128)(2,1)S(1)}, u32[]{:S(2)}, u32[]{:S(2)}) collective-permute-start(bf16[4,256,128]{2,1,0:T(8,128)(2,1)S(1)} %get-tuple-element.46), channel_id=1, source_target_pairs={{0,4},{1,5},{2,6},{3,7},{4,8},{5,9},{6,10},{7,11},{8,12},{9,13},{1... | collective-permute-start | bytes 786440 | tf_op jit(solution)/shard_map/ppermute | solution.py:180
  157.3 10.4 %collective-permute-start.25 = (bf16[4,256,128]{2,1,0:T(8,128)(2,1)S(1)}, bf16[4,256,128]{2,1,0:T(8,128)(2,1)S(1)}, u32[]{:S(2)}, u32[]{:S(2)}) collective-permute-start(bf16[4,256,128]{2,1,0:T(8,128)(2,1)S(1)} %get-tuple-element.47), channel_id=1, source_target_pairs={{0,8},{1,9},{2,10},{3,11},{4,12},{5,13},{6,14},{7,15},{8,0},{9,1},... | collective-permute-start | bytes 786440 | tf_op jit(solution)/shard_map/ppermute | solution.py:180
  158.3 10.2 %collective-permute-start.24 = (bf16[4,256,128]{2,1,0:T(8,128)(2,1)S(1)}, bf16[4,256,128]{2,1,0:T(8,128)(2,1)S(1)}, u32[]{:S(2)}, u32[]{:S(2)}) collective-permute-start(bf16[4,256,128]{2,1,0:T(8,128)(2,1)S(1)} %get-tuple-element.48), channel_id=1, source_target_pairs={{0,12},{1,13},{2,14},{3,15},{4,0},{5,1},{6,2},{7,3},{8,4},{9,5},{1... | collective-permute-start | bytes 786440 | tf_op jit(solution)/shard_map/ppermute | solution.py:180
  161.1 8.4 %collective-permute-start.30 = (bf16[4,256,128]{2,1,0:T(8,128)(2,1)S(1)}, bf16[4,256,128]{2,1,0:T(8,128)(2,1)S(1)}, u32[]{:S(2)}, u32[]{:S(2)}) collective-permute-start(bf16[4,256,128]{2,1,0:T(8,128)(2,1)S(1)} %fusion.3), channel_id=1, source_target_pairs={{0,16},{16,0},{32,48},{48,32},{64,80},{80,64},{96,112},{112,96},{1... | collective-permute-start | bytes 786440 | tf_op jit(solution)/shard_map/ppermute | solution.py:184
  169.5 0.7 copy-start.9

commit v3 on v2

--- a/solution.py
+++ b/solution.py
@@ -76,7 +76,7 @@
 
 def ffn_kernel(t, places_in, places_out, up_index, down_index, gain_ref, *refs):
     pieces, (up_hbm, down_hbm), outs = refs[:8], refs[8:10], refs[10:14]
-    x, up_w, down_w, acc, stage, squares, in_sem, up_sem, down_sem, out_sem = refs[14:]
+    x, up_w, down_w, acc, stage, squares, act, in_sem, up_sem, down_sem, out_sem = refs[14:]
     n_hidden, kept = up_w.shape[:2]
 
     def piece_copy(i):
@@ -115,17 +115,28 @@
     mean = jnp.sum(squares[...], axis=-1, keepdims=True) * (1.0 / (64 * 128))
     scale = lax.rsqrt(mean + 1e-06)
 
-    @pl.loop(0, n_hidden)
-    def _(c):
-        up_copy(c).wait()
-        down_copy(c).wait()
+    def activated(c):
         picked = jnp.concatenate([x[up_index[c, k]] for k in range(kept)], axis=1)
         upper = dot(picked, up_w[c].reshape(kept * BLK, BLK)) * scale
-        act = (upper / (1.0 + jnp.exp(-upper))).astype(BF16)
-        for k in range(0, kept, 2):
-            part = dot(act, jnp.concatenate([down_w[c, k], down_w[c, k + 1]], axis=1))
-            acc[down_index[c, k]] += part[:, :BLK]
-            acc[down_index[c, k + 1]] += part[:, BLK:]
+        return (upper / (1.0 + jnp.exp(-upper))).astype(BF16)
+
+    def spread(c, units):
+        for k in range(kept):
+            acc[down_index[c, k]] += dot(units, down_w[c, k])
+
+    up_copy(0).wait()
+    act[...] = activated(0)
+
+    @pl.loop(0, n_hidden - 1)
+    def _(c):
+        down_copy(c).wait()
+        up_copy(c + 1).wait()
+        units = act[...]
+        spread(c, units)
+        act[...] = activated(c + 1)
+
+    down_copy(n_hidden - 1).wait()
+    spread(n_hidden - 1, act[...])
 
     for i in range(16):
         for b in range(4):
@@ -149,6 +160,7 @@
             pltpu.VMEM((64, 256, 128), F32),
             pltpu.VMEM((64, 256, 128), BF16),
             pltpu.VMEM((256, 128), F32),
+            pltpu.VMEM((256, 128), BF16),
             pltpu.SemaphoreType.DMA((16,)),
             pltpu.SemaphoreType.DMA((n_hidden,)),
             pltpu.SemaphoreType.DMA((n_hidden,)),

time: 172 us -> 171 us (level)
  transfers between devices with their start and end apart: 31 -> 31, of which waited for: 17 -> 18; matrix products, arithmetic and copies ran while one was open for 3% -> 3% of each run, Pallas kernels for 15% -> 15%
where the time goes in v3:
time: 171 us
  waiting for transfers between devices  89.9 us (53%)
  starting transfers between devices  36.8 us (22%)
  Pallas kernels  32.4 us (19%)
  local copies, waits for them, and re-layouts  5.78 us (3%)
  other arithmetic  5.55 us (3%)
    ppermute x23, waiting for transfers between devices, torus_shift(): return lax.ppermute(x, ('seq', 'wt'), pairs)  74.8 us
    ppermute x23, starting transfers between devices, torus_shift(): return lax.ppermute(x, ('seq', 'wt'), pairs)  29.2 us
    pallas_call x2, Pallas kernels, ffn(): pl.pallas_call(functools.partial(ffn_kernel, t), out_shape=[jax.ShapeDtyp...  20.8 us
    ppermute x4, waiting for transfers between devices, later(): lax.ppermute(x, 'seq', [(s, s + 2 * places) for s in range(SEQ) if s + 2...  10.7 us
    ppermute x4, starting transfers between devices, later(): lax.ppermute(x, 'seq', [(s, s + 2 * places) for s in range(SEQ) if s + 2...  7.26 us
    ppermute x4, waiting for transfers between devices, swap_cores(): return lax.ppermute(x, 'seq', [(s, s ^ 1) for s in range(SEQ)])  4.39 us
    pallas_call x1, Pallas kernels, per_device(): pl.pallas_call(intra_kernel, out_shape=jax.ShapeDtypeStruct((4, 512, HEAD...  4.06 us
  transfers between devices with their start and end apart: 31, of which 18 were waited for; matrix products, arithmetic and copies ran while one was open for 3% of the time, Pallas kernels for 15%

profile of v3, /device:TPU:184, one launch (start us, length us, event | category | flops | bytes accessed | tf_op | source)
XLA Modules:
  0.0 170.7 jit_solution(11173006225352963725)
XLA Ops:
  0.0 2.4 %states.1 = bf16[4,128,128]{2,1,0:T(8,128)(2,1)} custom-call(bf16[512,512]{1,0:T(8,128)(2,1)} %k_ref.3, bf16[512,512]{1,0:T(8,128)(2,1)} %v_ref.3), custom_call_target="tpu_custom_call" | custom-call | tf_op jit(solution)/shard_map/states/pallas_call | solution.py:241
  2.4 1.6 collective-permute-done
  3.9 0.9 convert_add_fusion.2
  4.9 3.4 %collective-permute-start.2 = (bf16[2,128,128]{2,1,0:T(8,128)(2,1)S(1)}, bf16[2,128,128]{2,1,0:T(8,128)(2,1)S(1)}, u32[]{:S(2)}, u32[]{:S(2)}) collective-permute-start(bf16[2,128,128]{2,1,0:T(8,128)(2,1)S(1)} %fusion.17), channel_id=1, source_target_pairs={{0,64},{16,80},{32,96},{48,112},{64,128},{80,144},{96,160},{112,17... | collective-permute-start | bytes 196616 | tf_op jit(solution)/shard_map/ppermute | solution.py:227
  8.3 1.9 %collective-permute-start.1 = (bf16[2,128,128]{2,1,0:T(8,128)(2,1)S(1)}, bf16[2,128,128]{2,1,0:T(8,128)(2,1)S(1)}, u32[]{:S(2)}, u32[]{:S(2)}) collective-permute-start(bf16[2,128,128]{2,1,0:T(8,128)(2,1)S(1)} %fusion.17), channel_id=1, source_target_pairs={{0,32},{16,48},{32,64},{48,80},{64,96},{80,112},{96,128},{112,144}... | collective-permute-start | bytes 196616 | tf_op jit(solution)/shard_map/ppermute | solution.py:227
  10.2 4.1 %within_block.1.intra_ref = f32[4,512,128]{2,1,0:T(8,128)} custom-call(bf16[512,512]{1,0:T(8,128)(2,1)} %q_ref.3, bf16[512,512]{1,0:T(8,128)(2,1)} %k_ref.3, bf16[512,512]{1,0:T(8,128)(2,1)} %v_ref.3), custom_call_target="tpu_custom_call" | custom-call | flops 1073741824 | bytes 3145728 | tf_op jit(solution)/shard_map/within_block/pallas_call | solution.py:248
  14.3 0.4 collective-permute-done.2
  14.8 0.7 collective-permute-start.4
  15.4 1.3 collective-permute-start.3
  16.8 10.3 %collective-permute-done.3 = bf16[2,128,128]{2,1,0:T(8,128)(2,1)S(1)} collective-permute-done((bf16[2,128,128]{2,1,0:T(8,128)(2,1)S(1)}, bf16[2,128,128]{2,1,0:T(8,128)(2,1)S(1)}, u32[]{:S(2)}, u32[]{:S(2)}) %collective-permute-start.3) | collective-permute-done | bytes 65568 | tf_op jit(solution)/shard_map/ppermute | solution.py:227
  27.1 0.1 collective-permute-start.5
  27.2 1.2 collective-permute-done.5
  28.4 0.7 fusion.8.state_ref
  29.2 3.2 %mid.1 = (bf16[4,256,128]{2,1,0:T(8,128)(2,1)}, bf16[4,256,128]{2,1,0:T(8,128)(2,1)}) custom-call(s32[1]{0:T(128)} %bitcast.core_ref, bf16[512,512]{1,0:T(8,128)(2,1)} %q_ref.3, f32[4,128,128]{2,1,0:T(8,128)} %fusion.8.state_ref, f32[4,512,128]{2,1,0:T(8,128)} %within_block.1.intra_ref, bf16[512,512]{1,0:T(8,128)(2,1)} %stream_ref.1, f32[1,512]{1,0:T(1,128)} %bitcast.35), custom_call_target="tpu_custom_call" | custom-call | tf_op jit(solution)/shard_map/mid/pallas_call | solution.py:260
  32.4 0.2 collective-permute-start.6
  32.5 1.6 collective-permute-done.6
  34.1 1.1 pad_maximum_fusion.2
  35.2 1.6 collective-permute-start.7
  36.8 1.7 %collective-permute-start.9 = (bf16[2,4,256,128]{3,2,1,0:T(8,128)(2,1)S(1)}, bf16[2,4,256,128]{3,2,1,0:T(8,128)(2,1)S(1)}, u32[]{:S(2)}, u32[]{:S(2)}) collective-permute-start(bf16[2,4,256,128]{3,2,1,0:T(8,128)(2,1)S(1)} %pad_maximum_fusion.2), channel_id=1, source_target_pairs={{0,12},{1,13},{2,14},{3,15},{4,0},{5,1},{6,2},{7,3},{8,4},{9,5},{1... | collective-permute-start | bytes 1572872 | tf_op jit(solution)/shard_map/ppermute | solution.py:192
  38.5 1.8 %collective-permute-start.8 = (bf16[2,4,256,128]{3,2,1,0:T(8,128)(2,1)S(1)}, bf16[2,4,256,128]{3,2,1,0:T(8,128)(2,1)S(1)}, u32[]{:S(2)}, u32[]{:S(2)}) collective-permute-start(bf16[2,4,256,128]{3,2,1,0:T(8,128)(2,1)S(1)} %pad_maximum_fusion.2), channel_id=1, source_target_pairs={{0,8},{1,9},{2,10},{3,11},{4,12},{5,13},{6,14},{7,15},{8,0},{9,1},... | collective-permute-start | bytes 1572872 | tf_op jit(solution)/shard_map/ppermute | solution.py:192
  40.4 5.3 %collective-permute-done.7 = bf16[2,4,256,128]{3,2,1,0:T(8,128)(2,1)S(1)} collective-permute-done((bf16[2,4,256,128]{3,2,1,0:T(8,128)(2,1)S(1)}, bf16[2,4,256,128]{3,2,1,0:T(8,128)(2,1)S(1)}, u32[]{:S(2)}, u32[]{:S(2)}) %collective-permute-start.7) | collective-permute-done | bytes 524320 | tf_op jit(solution)/shard_map/ppermute | solution.py:192
  45.8 0.1 pad_maximum_fusion.refs_0_
  45.9 0.3 collective-permute-start.10
  46.2 4.7 %collective-permute-done.9 = bf16[2,4,256,128]{3,2,1,0:T(8,128)(2,1)S(1)} collective-permute-done((bf16[2,4,256,128]{3,2,1,0:T(8,128)(2,1)S(1)}, bf16[2,4,256,128]{3,2,1,0:T(8,128)(2,1)S(1)}, u32[]{:S(2)}, u32[]{:S(2)}) %collective-permute-start.9) | collective-permute-done | bytes 524320 | tf_op jit(solution)/shard_map/ppermute | solution.py:192
  50.9 4.7 %collective-permute-done.8 = bf16[2,4,256,128]{3,2,1,0:T(8,128)(2,1)S(1)} collective-permute-done((bf16[2,4,256,128]{3,2,1,0:T(8,128)(2,1)S(1)}, bf16[2,4,256,128]{3,2,1,0:T(8,128)(2,1)S(1)}, u32[]{:S(2)}, u32[]{:S(2)}) %collective-permute-start.8) | collective-permute-done | bytes 524320 | tf_op jit(solution)/shard_map/ppermute | solution.py:192
  55.7 0.1 pad_maximum_fusion.1.refs_1_
  56.0 1.2 collective-permute-start.12
  57.2 2.1 %collective-permute-start.11 = (bf16[4,4,256,128]{3,2,1,0:T(8,128)(2,1)S(1)}, bf16[4,4,256,128]{3,2,1,0:T(8,128)(2,1)}, u32[]{:S(2)}, u32[]{:S(2)}) collective-permute-start(bf16[4,4,256,128]{3,2,1,0:T(8,128)(2,1)S(1)} %pad_maximum_fusion.1.refs_1_), channel_id=1, source_target_pairs={{0,1},{1,2},{2,3},{3,0},{4,5},{5,6},{6,7},{7,4},{8,9},{9,10},{10,1... | collective-permute-start | bytes 3145736 | tf_op jit(solution)/shard_map/ppermute | solution.py:192
  59.3 1.5 collective-permute-done.10.refs_2_
  60.8 1.0 fusion.29
  61.8 2.4 %collective-permute-start.14 = (bf16[2,4,256,128]{3,2,1,0:T(8,128)(2,1)}, bf16[2,4,256,128]{3,2,1,0:T(8,128)(2,1)}, u32[]{:S(2)}, u32[]{:S(2)}) collective-permute-start(bf16[2,4,256,128]{3,2,1,0:T(8,128)(2,1)} %get-tuple-element.51), channel_id=1, source_target_pairs={{0,1},{1,2},{2,3},{3,0},{4,5},{5,6},{6,7},{7,4},{8,9},{9,10},{10,1... | collective-permute-start | bytes 1572872 | tf_op jit(solution)/shard_map/ppermute | solution.py:192
  64.2 7.8 %collective-permute-done.13.refs_5_ = bf16[4,4,256,128]{3,2,1,0:T(8,128)(2,1)S(1)} collective-permute-done((bf16[4,4,256,128]{3,2,1,0:T(8,128)(2,1)S(1)}, bf16[4,4,256,128]{3,2,1,0:T(8,128)(2,1)S(1)}, u32[]{:S(2)}, u32[]{:S(2)}) %collective-permute-start.13) | collective-permute-done | bytes 1048608 | tf_op jit(solution)/shard_map/ppermute | solution.py:192
  72.0 1.1 fusion.28
  73.0 1.0 copy-done
  74.1 0.7 gather_fusion
  74.7 3.3 %collective-permute-start.18 = (bf16[2,4,256,128]{3,2,1,0:T(8,128)(2,1)}, bf16[2,4,256,128]{3,2,1,0:T(8,128)(2,1)S(1)}, u32[]{:S(2)}, u32[]{:S(2)}) collective-permute-start(bf16[2,4,256,128]{3,2,1,0:T(8,128)(2,1)} %get-tuple-element.52), channel_id=1, source_target_pairs={{0,1},{1,2},{2,3},{3,0},{4,5},{5,6},{6,7},{7,4},{8,9},{9,10},{10,1... | collective-permute-start | bytes 1572872 | tf_op jit(solution)/shard_map/ppermute | solution.py:192
  78.0 5.3 %collective-permute-done.12.refs_4_ = bf16[4,4,256,128]{3,2,1,0:T(8,128)(2,1)} collective-permute-done((bf16[4,4,256,128]{3,2,1,0:T(8,128)(2,1)S(1)}, bf16[4,4,256,128]{3,2,1,0:T(8,128)(2,1)}, u32[]{:S(2)}, u32[]{:S(2)}) %collective-permute-start.12) | collective-permute-done | bytes 1048608 | tf_op jit(solution)/shard_map/ppermute | solution.py:192
  83.4 5.6 %collective-permute-done.15.refs_7_ = bf16[2,4,256,128]{3,2,1,0:T(8,128)(2,1)} collective-permute-done((bf16[2,4,256,128]{3,2,1,0:T(8,128)(2,1)}, bf16[2,4,256,128]{3,2,1,0:T(8,128)(2,1)}, u32[]{:S(2)}, u32[]{:S(2)}) %collective-permute-start.15) | collective-permute-done | bytes 524320 | tf_op jit(solution)/shard_map/ppermute | solution.py:192
  89.0 1.2 copy-done.1
  90.2 10.4 %feed_forward.2 = (bf16[4,4,256,128]{3,2,1,0:T(8,128)(2,1)S(1)}, bf16[4,4,256,128]{3,2,1,0:T(8,128)(2,1)S(1)}, bf16[4,4,256,128]{3,2,1,0:T(8,128)(2,1)S(1)}, bf16[4,4,256,128]{3,2,1,0:T(8,128)(2,1)S(1)}) custom-call(s32[16]{0:T(128)S(1)} %get-tuple-element.60.places_in, s32[16]{0:T(128)S(1)} %get-tuple-element.59.places_out, s32[8,16]{1,0:T(8,128)S(1)} %copy-done.3, ...), custom_call_target="tpu_custom_call" | custom-call | flops 2147483648 | bytes 17825792 | tf_op jit(solution)/shard_map/feed_forward/pallas_call | solution.py:151
  100.7 2.0 %collective-permute-start.17 = (bf16[4,4,256,128]{3,2,1,0:T(8,128)(2,1)S(1)}, bf16[4,4,256,128]{3,2,1,0:T(8,128)(2,1)S(1)}, u32[]{:S(2)}, u32[]{:S(2)}) collective-permute-start(bf16[4,4,256,128]{3,2,1,0:T(8,128)(2,1)S(1)} %get-tuple-element.28), channel_id=1, source_target_pairs={{0,3},{1,0},{2,1},{3,2},{4,7},{5,4},{6,5},{7,6},{8,11},{9,8},{10,9... | collective-permute-start | bytes 3145736 | tf_op jit(solution)/shard_map/ppermute | solution.py:192
  102.7 10.5 %feed_forward.3 = (bf16[4,4,256,128]{3,2,1,0:T(8,128)(2,1)S(1)}, bf16[4,4,256,128]{3,2,1,0:T(8,128)(2,1)S(1)}, bf16[4,4,256,128]{3,2,1,0:T(8,128)(2,1)S(1)}, bf16[4,4,256,128]{3,2,1,0:T(8,128)(2,1)S(1)}) custom-call(s32[16]{0:T(128)S(1)} %get-tuple-element.60.places_in, s32[16]{0:T(128)S(1)} %get-tuple-element.59.places_out, s32[8,16]{1,0:T(8,128)S(1)} %copy-done.3, ...), custom_call_target="tpu_custom_call" | custom-call | flops 2147483648 | bytes 17825792 | tf_op jit(solution)/shard_map/feed_forward/pallas_call | solution.py:151
  113.2 0.3 collective-permute-start.20
  113.5 3.2 %collective-permute-start.22 = (bf16[4,4,256,128]{3,2,1,0:T(8,128)(2,1)S(1)}, bf16[4,4,256,128]{3,2,1,0:T(8,128)(2,1)S(1)}, u32[]{:S(2)}, u32[]{:S(2)}) collective-permute-start(bf16[4,4,256,128]{3,2,1,0:T(8,128)(2,1)S(1)} %get-tuple-element.36), channel_id=1, source_target_pairs={{0,1},{1,2},{2,3},{3,0},{4,5},{5,6},{6,7},{7,4},{8,9},{9,10},{10,1... | collective-permute-start | bytes 3145736 | tf_op jit(solution)/shard_map/ppermute | solution.py:192
  116.7 0.3 add_convert_fusion
  117.0 0.1 collective-permute-start.26
  117.2 12.3 %collective-permute-done.20 = bf16[4,4,256,128]{3,2,1,0:T(8,128)(2,1)S(1)} collective-permute-done((bf16[4,4,256,128]{3,2,1,0:T(8,128)(2,1)S(1)}, bf16[4,4,256,128]{3,2,1,0:T(8,128)(2,1)S(1)}, u32[]{:S(2)}, u32[]{:S(2)}) %collective-permute-start.20) | collective-permute-done | bytes 1048608 | tf_op jit(solution)/shard_map/ppermute | solution.py:192
  129.5 0.3 add_convert_fusion.1
  129.7 0.1 collective-permute-start.21
  129.8 14.9 %collective-permute-done.26 = bf16[4,4,256,128]{3,2,1,0:T(8,128)(2,1)S(1)} collective-permute-done((bf16[4,4,256,128]{3,2,1,0:T(8,128)(2,1)S(1)}, bf16[4,4,256,128]{3,2,1,0:T(8,128)(2,1)S(1)}, u32[]{:S(2)}, u32[]{:S(2)}) %collective-permute-start.26) | collective-permute-done | bytes 1048608 | tf_op jit(solution)/shard_map/ppermute | solution.py:192
  144.8 0.3 fusion.14
  145.2 2.3 %collective-permute-start.29 = (bf16[4,256,128]{2,1,0:T(8,128)(2,1)S(1)}, bf16[4,256,128]{2,1,0:T(8,128)(2,1)S(1)}, u32[]{:S(2)}, u32[]{:S(2)}) collective-permute-start(bf16[4,256,128]{2,1,0:T(8,128)(2,1)S(1)} %get-tuple-element.44), channel_id=1, source_target_pairs={{0,8},{1,9},{2,10},{3,11},{4,12},{5,13},{6,14},{7,15},{8,0},{9,1},... | collective-permute-start | bytes 786440 | tf_op jit(solution)/shard_map/ppermute | solution.py:192
  147.5 2.5 %collective-permute-start.28 = (bf16[4,256,128]{2,1,0:T(8,128)(2,1)S(1)}, bf16[4,256,128]{2,1,0:T(8,128)(2,1)S(1)}, u32[]{:S(2)}, u32[]{:S(2)}) collective-permute-start(bf16[4,256,128]{2,1,0:T(8,128)(2,1)S(1)} %get-tuple-element.45), channel_id=1, source_target_pairs={{0,12},{1,13},{2,14},{3,15},{4,0},{5,1},{6,2},{7,3},{8,4},{9,5},{1... | collective-permute-start | bytes 786440 | tf_op jit(solution)/shard_map/ppermute | solution.py:192
  150.1 5.4 %collective-permute-done.21 = bf16[4,4,256,128]{3,2,1,0:T(8,128)(2,1)S(1)} collective-permute-done((bf16[4,4,256,128]{3,2,1,0:T(8,128)(2,1)S(1)}, bf16[4,4,256,128]{3,2,1,0:T(8,128)(2,1)S(1)}, u32[]{:S(2)}, u32[]{:S(2)}) %collective-permute-start.21) | collective-permute-done | bytes 1048608 | tf_op jit(solution)/shard_map/ppermute | solution.py:192
  155.5 0.3 fusion.10
  155.9 1.2 collective-permute-start.25
  157.1 2.5 %collective-permute-start.24 = (bf16[4,256,128]{2,1,0:T(8,128)(2,1)S(1)}, bf16[4,256,128]{2,1,0:T(8,128)(2,1)S(1)}, u32[]{:S(2)}, u32[]{:S(2)}) collective-permute-start(bf16[4,256,128]{2,1,0:T(8,128)(2,1)S(1)} %get-tuple-element.48), channel_id=1, source_target_pairs={{0,12},{1,13},{2,14},{3,15},{4,0},{5,1},{6,2},{7,3},{8,4},{9,5},{1... | collective-permute-start | bytes 786440 | tf_op jit(solution)/shard_map/ppermute | solution.py:192
  159.6 0.2 fusion.3
  159.9 0.1 collective-permute-start.30
  160.0 6.3 %collective-permute-done.23 = bf16[4,256,128]{2,1,0:T(8,128)(2,1)S(1)} collective-permute-done((bf16[4,256,128]{2,1,0:T(8,128)(2,1)S(1)}, bf16[4,256,128]{2,1,0:T(8,128)(2,1)S(1)}, u32[]{:S(2)}, u32[]{:S(2)}) %collective-permute-start.23) | collective-permute-done | bytes 262176 | tf_op jit(solution)/shard_map/ppermute | solution.py:192
  166.3 0.9 collective-permute-done.24
  167.2 1.0 fusion.7.mine_ref
  168.1 0.7 copy-done.9
  168.8 1.9 %result.1 = bf16[512,512]{1,0:T(8,128)(2,1)} custom-call(s32[1]{0:T(128)} %bitcast.core_ref, bf16[4,256,128]{2,1,0:T(8,128)(2,1)} %fusion.7.mine_ref, bf16[4,256,128]{2,1,0:T(8,128)(2,1)} %copy-done.9), custom_call_target="tpu_custom_call" | custom-call | tf_op jit(solution)/shard_map/result/pallas_call | solution.py:303
  (49 shorter events, 0.7 us)
Async XLA Ops:
  2.4 1.6 collective-permute-start
  4.9 9.8 %collective-permute-start.2 = (bf16[2,128,128]{2,1,0:T(8,128)(2,1)S(1)}, bf16[2,128,128]{2,1,0:T(8,128)(2,1)S(1)}, u32[]{:S(2)}, u32[]{:S(2)}) collective-permute-start(bf16[2,128,128]{2,1,0:T(8,128)(2,1)S(1)} %fusion.17), channel_id=1, source_target_pairs={{0,64},{16,80},{32,96},{48,112},{64,128},{80,144},{96,160},{112,17... | collective-permute-start | bytes 196616 | tf_op jit(solution)/shard_map/ppermute | solution.py:227
  8.3 6.4 %collective-permute-start.1 = (bf16[2,128,128]{2,1,0:T(8,128)(2,1)S(1)}, bf16[2,128,128]{2,1,0:T(8,128)(2,1)S(1)}, u32[]{:S(2)}, u32[]{:S(2)}) collective-permute-start(bf16[2,128,128]{2,1,0:T(8,128)(2,1)S(1)} %fusion.17), channel_id=1, source_target_pairs={{0,32},{16,48},{32,64},{48,80},{64,96},{80,112},{96,128},{112,144}... | collective-permute-start | bytes 196616 | tf_op jit(solution)/shard_map/ppermute | solution.py:227
  14.8 2.0 %collective-permute-start.4 = (bf16[2,128,128]{2,1,0:T(8,128)(2,1)S(1)}, bf16[2,128,128]{2,1,0:T(8,128)(2,1)S(1)}, u32[]{:S(2)}, u32[]{:S(2)}) collective-permute-start(bf16[2,128,128]{2,1,0:T(8,128)(2,1)S(1)} %add_convert_fusion.10), channel_id=1, source_target_pairs={{0,192},{16,208},{32,224},{48,240},{1,193},{17,209},{33,225},{49,2... | collective-permute-start | bytes 196616 | tf_op jit(solution)/shard_map/ppermute | solution.py:227
  15.4 11.6 %collective-permute-start.3 = (bf16[2,128,128]{2,1,0:T(8,128)(2,1)S(1)}, bf16[2,128,128]{2,1,0:T(8,128)(2,1)S(1)}, u32[]{:S(2)}, u32[]{:S(2)}) collective-permute-start(bf16[2,128,128]{2,1,0:T(8,128)(2,1)S(1)} %add_convert_fusion.10), channel_id=1, source_target_pairs={{0,96},{16,112},{32,128},{48,144},{64,160},{80,176},{96,192},{112,... | collective-permute-start | bytes 196616 | tf_op jit(solution)/shard_map/ppermute | solution.py:227
  27.1 1.3 collective-permute-start.5
  32.4 13.4 %copy-start.6 = (bf16[4,256,128]{2,1,0:T(8,128)(2,1)S(1)}, bf16[4,256,128]{2,1,0:T(8,128)(2,1)}, u32[]{:S(2)}) copy-start(bf16[4,256,128]{2,1,0:T(8,128)(2,1)} %get-tuple-element.25) | copy-start | bytes 786436
  32.4 1.7 %collective-permute-start.6 = (bf16[4,256,128]{2,1,0:T(8,128)(2,1)}, bf16[4,256,128]{2,1,0:T(8,128)(2,1)S(1)}, u32[]{:S(2)}, u32[]{:S(2)}) collective-permute-start(bf16[4,256,128]{2,1,0:T(8,128)(2,1)} %get-tuple-element.26), channel_id=1, source_target_pairs={{0,16},{16,0},{32,48},{48,32},{64,80},{80,64},{96,112},{112,96},{1... | collective-permute-start | bytes 786440 | tf_op jit(solution)/shard_map/ppermute | solution.py:196
  34.1 11.6 %copy-start.7 = (bf16[4,256,128]{2,1,0:T(8,128)(2,1)}, bf16[4,256,128]{2,1,0:T(8,128)(2,1)S(1)}, u32[]{:S(2)}) copy-start(bf16[4,256,128]{2,1,0:T(8,128)(2,1)S(1)} %collective-permute-done.6) | copy-start | bytes 786436
  35.2 10.5 %collective-permute-start.7 = (bf16[2,4,256,128]{3,2,1,0:T(8,128)(2,1)S(1)}, bf16[2,4,256,128]{3,2,1,0:T(8,128)(2,1)S(1)}, u32[]{:S(2)}, u32[]{:S(2)}) collective-permute-start(bf16[2,4,256,128]{3,2,1,0:T(8,128)(2,1)S(1)} %pad_maximum_fusion.2), channel_id=1, source_target_pairs={{0,4},{1,5},{2,6},{3,7},{4,8},{5,9},{6,10},{7,11},{8,12},{9,13},{1... | collective-permute-start | bytes 1572872 | tf_op jit(solution)/shard_map/ppermute | solution.py:192
  36.8 14.1 %collective-permute-start.9 = (bf16[2,4,256,128]{3,2,1,0:T(8,128)(2,1)S(1)}, bf16[2,4,256,128]{3,2,1,0:T(8,128)(2,1)S(1)}, u32[]{:S(2)}, u32[]{:S(2)}) collective-permute-start(bf16[2,4,256,128]{3,2,1,0:T(8,128)(2,1)S(1)} %pad_maximum_fusion.2), channel_id=1, source_target_pairs={{0,12},{1,13},{2,14},{3,15},{4,0},{5,1},{6,2},{7,3},{8,4},{9,5},{1... | collective-permute-start | bytes 1572872 | tf_op jit(solution)/shard_map/ppermute | solution.py:192
  38.5 17.1 %collective-permute-start.8 = (bf16[2,4,256,128]{3,2,1,0:T(8,128)(2,1)S(1)}, bf16[2,4,256,128]{3,2,1,0:T(8,128)(2,1)S(1)}, u32[]{:S(2)}, u32[]{:S(2)}) collective-permute-start(bf16[2,4,256,128]{3,2,1,0:T(8,128)(2,1)S(1)} %pad_maximum_fusion.2), channel_id=1, source_target_pairs={{0,8},{1,9},{2,10},{3,11},{4,12},{5,13},{6,14},{7,15},{8,0},{9,1},... | collective-permute-start | bytes 1572872 | tf_op jit(solution)/shard_map/ppermute | solution.py:192
  45.9 14.9 %collective-permute-start.10 = (bf16[4,4,256,128]{3,2,1,0:T(8,128)(2,1)S(1)}, bf16[4,4,256,128]{3,2,1,0:T(8,128)(2,1)S(1)}, u32[]{:S(2)}, u32[]{:S(2)}) collective-permute-start(bf16[4,4,256,128]{3,2,1,0:T(8,128)(2,1)S(1)} %pad_maximum_fusion.refs_0_), channel_id=1, source_target_pairs={{0,1},{1,2},{2,3},{3,0},{4,5},{5,6},{6,7},{7,4},{8,9},{9,10},{10,1... | collective-permute-start | bytes 3145736 | tf_op jit(solution)/shard_map/ppermute | solution.py:192
  55.9 18.2 %copy-start.5 = (s32[4]{0:T(128)S(1)}, s32[4]{0:T(128)}, u32[]{:S(2)}) copy-start(s32[4]{0:T(128)} %constant.91.clone) | copy-start | bytes 52
  55.9 33.1 %copy-start.2 = (f32[8192]{0:T(1024)S(1)}, f32[8192]{0:T(1024)}, u32[]{:S(2)}) copy-start(f32[8192]{0:T(1024)} %param.16) | copy-start | bytes 98308
  55.9 33.1 %copy-start.3 = (s32[8,16]{1,0:T(8,128)S(1)}, s32[8,16]{1,0:T(8,128)}, u32[]{:S(2)}) copy-start(s32[8,16]{1,0:T(8,128)} %up_index.3) | copy-start | bytes 1540
  55.9 33.1 %copy-start.4 = (s32[8,16]{1,0:T(8,128)S(1)}, s32[8,16]{1,0:T(8,128)}, u32[]{:S(2)}) copy-start(s32[8,16]{1,0:T(8,128)} %down_index.3) | copy-start | bytes 1540
  55.9 16.1 %collective-permute-start.13 = (bf16[4,4,256,128]{3,2,1,0:T(8,128)(2,1)S(1)}, bf16[4,4,256,128]{3,2,1,0:T(8,128)(2,1)S(1)}, u32[]{:S(2)}, u32[]{:S(2)}) collective-permute-start(bf16[4,4,256,128]{3,2,1,0:T(8,128)(2,1)S(1)} %pad_maximum_fusion.1.refs_1_), channel_id=1, source_target_pairs={{0,3},{1,0},{2,1},{3,2},{4,7},{5,4},{6,5},{7,6},{8,11},{9,8},{10,9... | collective-permute-start | bytes 3145736 | tf_op jit(solution)/shard_map/ppermute | solution.py:192
  56.0 27.3 %collective-permute-start.12 = (bf16[4,4,256,128]{3,2,1,0:T(8,128)(2,1)S(1)}, bf16[4,4,256,128]{3,2,1,0:T(8,128)(2,1)}, u32[]{:S(2)}, u32[]{:S(2)}) collective-permute-start(bf16[4,4,256,128]{3,2,1,0:T(8,128)(2,1)S(1)} %pad_maximum_fusion.refs_0_), channel_id=1, source_target_pairs={{0,3},{1,0},{2,1},{3,2},{4,7},{5,4},{6,5},{7,6},{8,11},{9,8},{10,9... | collective-permute-start | bytes 3145736 | tf_op jit(solution)/shard_map/ppermute | solution.py:192
  57.2 26.2 %collective-permute-start.11 = (bf16[4,4,256,128]{3,2,1,0:T(8,128)(2,1)S(1)}, bf16[4,4,256,128]{3,2,1,0:T(8,128)(2,1)}, u32[]{:S(2)}, u32[]{:S(2)}) collective-permute-start(bf16[4,4,256,128]{3,2,1,0:T(8,128)(2,1)S(1)} %pad_maximum_fusion.1.refs_1_), channel_id=1, source_target_pairs={{0,1},{1,2},{2,3},{3,0},{4,5},{5,6},{6,7},{7,4},{8,9},{9,10},{10,1... | collective-permute-start | bytes 3145736 | tf_op jit(solution)/shard_map/ppermute | solution.py:192
  61.8 21.6 %collective-permute-start.14 = (bf16[2,4,256,128]{3,2,1,0:T(8,128)(2,1)}, bf16[2,4,256,128]{3,2,1,0:T(8,128)(2,1)}, u32[]{:S(2)}, u32[]{:S(2)}) collective-permute-start(bf16[2,4,256,128]{3,2,1,0:T(8,128)(2,1)} %get-tuple-element.51), channel_id=1, source_target_pairs={{0,1},{1,2},{2,3},{3,0},{4,5},{5,6},{6,7},{7,4},{8,9},{9,10},{10,1... | collective-permute-start | bytes 1572872 | tf_op jit(solution)/shard_map/ppermute | solution.py:192
  73.0 1.0 copy-start
  74.0 14.9 %collective-permute-start.15 = (bf16[2,4,256,128]{3,2,1,0:T(8,128)(2,1)}, bf16[2,4,256,128]{3,2,1,0:T(8,128)(2,1)}, u32[]{:S(2)}, u32[]{:S(2)}) collective-permute-start(bf16[2,4,256,128]{3,2,1,0:T(8,128)(2,1)} %get-tuple-element.49), channel_id=1, source_target_pairs={{0,3},{1,0},{2,1},{3,2},{4,7},{5,4},{6,5},{7,6},{8,11},{9,8},{10,9... | collective-permute-start | bytes 1572872 | tf_op jit(solution)/shard_map/ppermute | solution.py:192
  74.7 28.0 %collective-permute-start.18 = (bf16[2,4,256,128]{3,2,1,0:T(8,128)(2,1)}, bf16[2,4,256,128]{3,2,1,0:T(8,128)(2,1)S(1)}, u32[]{:S(2)}, u32[]{:S(2)}) collective-permute-start(bf16[2,4,256,128]{3,2,1,0:T(8,128)(2,1)} %get-tuple-element.52), channel_id=1, source_target_pairs={{0,1},{1,2},{2,3},{3,0},{4,5},{5,6},{6,7},{7,4},{8,9},{9,10},{10,1... | collective-permute-start | bytes 1572872 | tf_op jit(solution)/shard_map/ppermute | solution.py:192
  83.3 19.4 %collective-permute-start.19 = (bf16[2,4,256,128]{3,2,1,0:T(8,128)(2,1)}, bf16[2,4,256,128]{3,2,1,0:T(8,128)(2,1)S(1)}, u32[]{:S(2)}, u32[]{:S(2)}) collective-permute-start(bf16[2,4,256,128]{3,2,1,0:T(8,128)(2,1)} %get-tuple-element.50), channel_id=1, source_target_pairs={{0,3},{1,0},{2,1},{3,2},{4,7},{5,4},{6,5},{7,6},{8,11},{9,8},{10,9... | collective-permute-start | bytes 1572872 | tf_op jit(solution)/shard_map/ppermute | solution.py:192
  89.0 1.2 copy-start.1
  100.6 16.1 %collective-permute-start.16 = (bf16[4,4,256,128]{3,2,1,0:T(8,128)(2,1)S(1)}, bf16[4,4,256,128]{3,2,1,0:T(8,128)(2,1)S(1)}, u32[]{:S(2)}, u32[]{:S(2)}) collective-permute-start(bf16[4,4,256,128]{3,2,1,0:T(8,128)(2,1)S(1)} %get-tuple-element.27), channel_id=1, source_target_pairs={{0,1},{1,2},{2,3},{3,0},{4,5},{5,6},{6,7},{7,4},{8,9},{9,10},{10,1... | collective-permute-start | bytes 3145736 | tf_op jit(solution)/shard_map/ppermute | solution.py:192
  100.7 16.1 %collective-permute-start.17 = (bf16[4,4,256,128]{3,2,1,0:T(8,128)(2,1)S(1)}, bf16[4,4,256,128]{3,2,1,0:T(8,128)(2,1)S(1)}, u32[]{:S(2)}, u32[]{:S(2)}) collective-permute-start(bf16[4,4,256,128]{3,2,1,0:T(8,128)(2,1)S(1)} %get-tuple-element.28), channel_id=1, source_target_pairs={{0,3},{1,0},{2,1},{3,2},{4,7},{5,4},{6,5},{7,6},{8,11},{9,8},{10,9... | collective-permute-start | bytes 3145736 | tf_op jit(solution)/shard_map/ppermute | solution.py:192
  113.2 16.3 %collective-permute-start.20 = (bf16[4,4,256,128]{3,2,1,0:T(8,128)(2,1)S(1)}, bf16[4,4,256,128]{3,2,1,0:T(8,128)(2,1)S(1)}, u32[]{:S(2)}, u32[]{:S(2)}) collective-permute-start(bf16[4,4,256,128]{3,2,1,0:T(8,128)(2,1)S(1)} %get-tuple-element.35), channel_id=1, source_target_pairs={{0,3},{1,0},{2,1},{3,2},{4,7},{5,4},{6,5},{7,6},{8,11},{9,8},{10,9... | collective-permute-start | bytes 3145736 | tf_op jit(solution)/shard_map/ppermute | solution.py:192
  113.5 36.6 %collective-permute-start.22 = (bf16[4,4,256,128]{3,2,1,0:T(8,128)(2,1)S(1)}, bf16[4,4,256,128]{3,2,1,0:T(8,128)(2,1)S(1)}, u32[]{:S(2)}, u32[]{:S(2)}) collective-permute-start(bf16[4,4,256,128]{3,2,1,0:T(8,128)(2,1)S(1)} %get-tuple-element.36), channel_id=1, source_target_pairs={{0,1},{1,2},{2,3},{3,0},{4,5},{5,6},{6,7},{7,4},{8,9},{9,10},{10,1... | collective-permute-start | bytes 3145736 | tf_op jit(solution)/shard_map/ppermute | solution.py:192
  117.0 27.7 %collective-permute-start.26 = (bf16[4,4,256,128]{3,2,1,0:T(8,128)(2,1)S(1)}, bf16[4,4,256,128]{3,2,1,0:T(8,128)(2,1)S(1)}, u32[]{:S(2)}, u32[]{:S(2)}) collective-permute-start(bf16[4,4,256,128]{3,2,1,0:T(8,128)(2,1)S(1)} %add_convert_fusion), channel_id=1, source_target_pairs={{0,1},{1,2},{2,3},{3,0},{4,5},{5,6},{6,7},{7,4},{8,9},{9,10},{10,1... | collective-permute-start | bytes 3145736 | tf_op jit(solution)/shard_map/ppermute | solution.py:192
  129.7 25.7 %collective-permute-start.21 = (bf16[4,4,256,128]{3,2,1,0:T(8,128)(2,1)S(1)}, bf16[4,4,256,128]{3,2,1,0:T(8,128)(2,1)S(1)}, u32[]{:S(2)}, u32[]{:S(2)}) collective-permute-start(bf16[4,4,256,128]{3,2,1,0:T(8,128)(2,1)S(1)} %add_convert_fusion.1), channel_id=1, source_target_pairs={{0,3},{1,0},{2,1},{3,2},{4,7},{5,4},{6,5},{7,6},{8,11},{9,8},{10,9... | collective-permute-start | bytes 3145736 | tf_op jit(solution)/shard_map/ppermute | solution.py:192
  145.1 14.5 %copy-start.8 = (bf16[4,256,128]{2,1,0:T(8,128)(2,1)S(1)}, bf16[4,256,128]{2,1,0:T(8,128)(2,1)}, u32[]{:S(2)}) copy-start(bf16[4,256,128]{2,1,0:T(8,128)(2,1)} %copy-done.7) | copy-start | bytes 786436
  145.1 12.0 %collective-permute-start.27 = (bf16[4,256,128]{2,1,0:T(8,128)(2,1)S(1)}, bf16[4,256,128]{2,1,0:T(8,128)(2,1)S(1)}, u32[]{:S(2)}, u32[]{:S(2)}) collective-permute-start(bf16[4,256,128]{2,1,0:T(8,128)(2,1)S(1)} %get-tuple-element.43), channel_id=1, source_target_pairs={{0,4},{1,5},{2,6},{3,7},{4,8},{5,9},{6,10},{7,11},{8,12},{9,13},{1... | collective-permute-start | bytes 786440 | tf_op jit(solution)/shard_map/ppermute | solution.py:192
  145.2 14.4 %collective-permute-start.29 = (bf16[4,256,128]{2,1,0:T(8,128)(2,1)S(1)}, bf16[4,256,128]{2,1,0:T(8,128)(2,1)S(1)}, u32[]{:S(2)}, u32[]{:S(2)}) collective-permute-start(bf16[4,256,128]{2,1,0:T(8,128)(2,1)S(1)} %get-tuple-element.44), channel_id=1, source_target_pairs={{0,8},{1,9},{2,10},{3,11},{4,12},{5,13},{6,14},{7,15},{8,0},{9,1},... | collective-permute-start | bytes 786440 | tf_op jit(solution)/shard_map/ppermute | solution.py:192
  147.5 12.1 %collective-permute-start.28 = (bf16[4,256,128]{2,1,0:T(8,128)(2,1)S(1)}, bf16[4,256,128]{2,1,0:T(8,128)(2,1)S(1)}, u32[]{:S(2)}, u32[]{:S(2)}) collective-permute-start(bf16[4,256,128]{2,1,0:T(8,128)(2,1)S(1)} %get-tuple-element.45), channel_id=1, source_target_pairs={{0,12},{1,13},{2,14},{3,15},{4,0},{5,1},{6,2},{7,3},{8,4},{9,5},{1... | collective-permute-start | bytes 786440 | tf_op jit(solution)/shard_map/ppermute | solution.py:192
  155.8 10.5 %collective-permute-start.23 = (bf16[4,256,128]{2,1,0:T(8,128)(2,1)S(1)}, bf16[4,256,128]{2,1,0:T(8,128)(2,1)S(1)}, u32[]{:S(2)}, u32[]{:S(2)}) collective-permute-start(bf16[4,256,128]{2,1,0:T(8,128)(2,1)S(1)} %get-tuple-element.46), channel_id=1, source_target_pairs={{0,4},{1,5},{2,6},{3,7},{4,8},{5,9},{6,10},{7,11},{8,12},{9,13},{1... | collective-permute-start | bytes 786440 | tf_op jit(solution)/shard_map/ppermute | solution.py:192
  155.9 10.4 %collective-permute-start.25 = (bf16[4,256,128]{2,1,0:T(8,128)(2,1)S(1)}, bf16[4,256,128]{2,1,0:T(8,128)(2,1)S(1)}, u32[]{:S(2)}, u32[]{:S(2)}) collective-permute-start(bf16[4,256,128]{2,1,0:T(8,128)(2,1)S(1)} %get-tuple-element.47), channel_id=1, source_target_pairs={{0,8},{1,9},{2,10},{3,11},{4,12},{5,13},{6,14},{7,15},{8,0},{9,1},... | collective-permute-start | bytes 786440 | tf_op jit(solution)/shard_map/ppermute | solution.py:192
  157.1 10.1 %collective-permute-start.24 = (bf16[4,256,128]{2,1,0:T(8,128)(2,1)S(1)}, bf16[4,256,128]{2,1,0:T(8,128)(2,1)S(1)}, u32[]{:S(2)}, u32[]{:S(2)}) collective-permute-start(bf16[4,256,128]{2,1,0:T(8,128)(2,1)S(1)} %get-tuple-element.48), channel_id=1, source_target_pairs={{0,12},{1,13},{2,14},{3,15},{4,0},{5,1},{6,2},{7,3},{8,4},{9,5},{1... | collective-permute-start | bytes 786440 | tf_op jit(solution)/shard_map/ppermute | solution.py:192
  159.9 8.2 %collective-permute-start.30 = (bf16[4,256,128]{2,1,0:T(8,128)(2,1)S(1)}, bf16[4,256,128]{2,1,0:T(8,128)(2,1)S(1)}, u32[]{:S(2)}, u32[]{:S(2)}) collective-permute-start(bf16[4,256,128]{2,1,0:T(8,128)(2,1)S(1)} %fusion.3), channel_id=1, source_target_pairs={{0,16},{16,0},{32,48},{48,32},{64,80},{80,64},{96,112},{112,96},{1... | collective-permute-start | bytes 786440 | tf_op jit(solution)/shard_map/ppermute | solution.py:196
  168.1 0.7 copy-start.9
